TPU v7x, 32 devices: a whole 2x2x4 slice. The times are simulated.
32 devices in a mesh: dp: 2 (over x), expert: 16 (over z, y, core).
Axes of the slice: x: 2, y: 2, z: 4, core: 2. Of those that a mesh axis runs over, the one named last changes fastest.
Arguments:
- tokens_in: bfloat16 [4096, 3584], P(('dp', 'expert')), may hold values from -6 to 6
- out_grad: bfloat16 [4096, 3584], P(('dp', 'expert')), may hold values from -0.59765625 to 0.59765625
- router_logits: float32 [4096, 192], P(('dp', 'expert')), may hold values from -12 to 250
- expert_ids: int32 [4096, 8], P(('dp', 'expert')), may hold values from 0 to 191, all different within a row; in each aligned block of 128 rows (0 to 127, 128 to 255, ...) at most 8 rows name the same one
- saved_hidden: bfloat16 [2, 16, 16, 8, 1024], P('dp', 'expert'), may hold values from -6 to 6
- down_weight: bfloat16 [16, 1024, 3584], P('expert', 'dp'), may hold values from -0.1875 to 0.1875
Outputs:
- hidden_grad: bfloat16 [2, 16, 16, 8, 1024], P('dp', 'expert')
- logit_grad: float32 [4096, 192], P(('dp', 'expert'))
- router_grad: float32 [3584, 192], P('expert', 'dp')
Inputs may be any that keep to these rules, and one draw needn't show every extreme that they name: `expert_ids`: among the 128 rows of one device no expert is named by more than 8 rows, a bound that some block reaches.
All inputs are finite; a program needn't handle non-finite values.
Results may differ from a plain program's by a relative error of at most 0.013.
Values may be sent and summed in bfloat16 or wider, within the bound.
No kernel may reach another device: no remote copies, remote signals or barrier semaphores. Data moves between devices by JAX's collectives and lax.ppermute only.
A program may use at most 64 MiB of HBM per device.

v0:
```python
import jax
import jax.numpy as jnp
from jax import lax
from jax.sharding import PartitionSpec as P

RSCALE = 2.827
ZLOSS = 0.25


def entering(shard, axis, combine, identity):
    length, place = (lax.axis_size(axis), lax.axis_index(axis))
    everything = lax.all_gather(shard.astype(jnp.bfloat16), axis)
    start = jnp.broadcast_to(jnp.asarray(identity, shard.dtype), shard.shape)

    def lap(k, before):
        reached = k < place
        new = combine(before, everything[k].astype(shard.dtype))
        return jnp.where(reached, new, before)

    return lax.fori_loop(0, length, lap, start)


def from_root(value, axis, source):
    kept = jnp.where(lax.axis_index(axis) == source, value, 0).astype(value.dtype)
    return lax.psum(kept, axis)


def slot_table(ids_block, flight, cap):
    owners = jnp.arange(flight, dtype=jnp.int32)
    chosen = jnp.any(ids_block[:, :, None] == owners[None, None, :], axis=1)
    as_int = chosen.astype(jnp.int32)
    rank = jnp.cumsum(as_int, axis=0) - as_int
    places = jnp.arange(cap, dtype=jnp.int32)
    table = chosen[None, :, :] & (rank[None, :, :] == places[:, None, None])
    return jnp.transpose(table, (2, 0, 1))


def own_columns(panel):
    count = panel.shape[1] // lax.axis_size("dp")
    return lax.dynamic_slice_in_dim(panel, lax.axis_index("dp") * count, count, 1)


def local(tokens_in, out_grad, router_logits, expert_ids, saved_hidden, down_weight):
    highest = lax.Precision.HIGHEST
    flight = lax.axis_size("expert")
    cap = saved_hidden.shape[3]
    hidden = saved_hidden.shape[4]
    width = out_grad.shape[1]
    experts = router_logits.shape[1]
    top = jnp.max(router_logits, axis=1, keepdims=True)
    shifted = jnp.exp(router_logits - top)
    total = jnp.sum(shifted, axis=1, keepdims=True)
    probs = shifted / total
    lse = top + jnp.log(total)
    columns = jnp.arange(experts, dtype=jnp.int32)
    picks = (expert_ids[:, :, None] == columns[None, None, :]).astype(jnp.float32)
    chosen_logit = jnp.sum(picks * router_logits[:, None, :], axis=2)
    scores = jax.nn.sigmoid(chosen_logit)
    ssum = jnp.sum(scores, axis=1, keepdims=True)
    gates = RSCALE * scores / ssum
    gate_half = gates.astype(jnp.bfloat16)
    in_window = picks[:, :, :flight]
    gate_te = jnp.sum(in_window * gate_half.astype(jnp.float32)[:, :, None], axis=1)
    table = slot_table(expert_ids, flight, cap)
    table_half = table.astype(jnp.bfloat16)
    table_full = table.astype(jnp.float32)
    send_rows = jnp.einsum(
        "ect,td->ecd", table_half, out_grad, preferred_element_type=jnp.float32
    ).astype(jnp.bfloat16)
    send_gates = jnp.einsum("ect,te->ec", table_full, gate_te, precision=highest).astype(
        jnp.bfloat16
    )
    recv_rows, recv_gates = (
        lax.all_to_all(send_rows, "expert", split_axis=0, concat_axis=0, tiled=True),
        lax.all_to_all(send_gates, "expert", split_axis=0, concat_axis=0, tiled=True),
    )
    flat_rows = recv_rows.reshape(flight * cap, width)
    part = lax.dot_general(
        flat_rows,
        lax.all_gather(down_weight, "dp", axis=1, tiled=True)[0],
        (((1,), (1,)), ((), ())),
        preferred_element_type=jnp.float32,
    )
    slot_gates = recv_gates.reshape(flight * cap, 1).astype(jnp.float32)
    hidden_grad = (slot_gates * part).astype(jnp.bfloat16).reshape(1, 1, flight, cap, hidden)
    saved_flat = saved_hidden.reshape(flight * cap, hidden)
    gate_grad = jnp.sum(saved_flat * part, axis=1).reshape(flight, cap)
    returned = lax.all_to_all(gate_grad, "expert", split_axis=0, concat_axis=0, tiled=True)
    grad_te = jnp.einsum("ect,ec->te", table_full, returned, precision=highest)
    grad_choice = jnp.sum(in_window * grad_te[:, None, :], axis=2)
    mixed = jnp.sum(grad_choice * gates, axis=1, keepdims=True) / RSCALE
    dscore = RSCALE / ssum * (grad_choice - mixed)
    dchosen = dscore * scores * (1.0 - scores)
    logit_grad = jnp.sum(picks * dchosen[:, :, None], axis=1) + 2.0 * ZLOSS * lse * probs
    tokens_full = tokens_in.astype(jnp.float32)
    own_rows = lax.psum_scatter(
        lax.dot_general(tokens_full, logit_grad, (((0,), (0,)), ((), ())), precision=highest),
        "expert",
        scatter_dimension=0,
        tiled=True,
    )
    before = entering(
        own_rows, "dp", lambda earlier, later: earlier + later, jnp.zeros_like(own_rows)
    )
    finished = before + own_rows
    spread = from_root(finished.astype(jnp.bfloat16), "dp", lax.axis_size("dp") - 1).astype(
        finished.dtype
    )
    router_grad = own_columns(spread)
    return (hidden_grad, logit_grad, router_grad)


def solution(mesh):
    in_specs = (
        P(("dp", "expert"), None),
        P(("dp", "expert"), None),
        P(("dp", "expert"), None),
        P(("dp", "expert"), None),
        P("dp", "expert", None, None, None),
        P("expert", "dp", None),
    )
    out_specs = (P("dp", "expert", None, None, None), P(("dp", "expert"), None), P("expert", "dp"))
    return jax.shard_map(local, mesh=mesh, in_specs=in_specs, out_specs=out_specs, check_vma=False)
```

profile of v0, /device:TPU:0, one launch (start us, length us, event | category | flops | bytes accessed | tf_op | source)
XLA Modules:
  0.0 231.7 jit_solution(10085355655853971935)
XLA Ops:
  7.2 0.0 copy-start
  7.2 0.0 copy-start.5
  7.2 0.0 copy-start.2
  7.2 0.0 copy-start.1
  7.2 0.0 copy-start.4
  7.2 0.0 all-gather.4.cloned.1.call-start
  7.3 0.7 all-gather.4.cloned.1.call-update
  8.0 0.0 copy-done.5
  8.0 0.1 copy.46
  8.1 0.2 reduce_window_sum.13
  8.3 0.1 copy.47
  8.3 0.1 copy-done.2
  8.5 1.3 convolution_convert_fusion
  9.8 7.4 %all-to-all-start.1 = ((bf16[16,8,3584]{2,1,0:T(8,128)(2,1)}), bf16[16,8,3584]{2,1,0:T(8,128)(2,1)S(1)}, u32[]{:S(2)}, u32[]{:S(2)}) async-start(bf16[16,8,3584]{2,1,0:T(8,128)(2,1)} %convolution_convert_fusion), calls=%async_computation.1 | async-start | bytes 1835008 | tf_op jit(solution)/shard_map/all_to_all | solution.py:74
  17.2 0.0 copy-done.1
  17.2 0.1 select_reduce_fusion.1
  17.3 0.1 fusion.7
  17.4 0.1 iota_compare_fusion
  17.5 20.4 %all-to-all-done.1 = bf16[16,8,3584]{2,1,0:T(8,128)(2,1)S(1)} async-done(((bf16[16,8,3584]{2,1,0:T(8,128)(2,1)}), bf16[16,8,3584]{2,1,0:T(8,128)(2,1)S(1)}, u32[]{:S(2)}, u32[]{:S(2)}) %all-to-all-start.1) | async-done | bytes 917536 | tf_op jit(solution)/shard_map/all_to_all | solution.py:74
  38.0 66.5 %all-gather.4.cloned.1.call-done = bf16[1,1024,3584]{2,1,0:T(8,128)(2,1)} async-done(((bf16[1,512,3584]{2,1,0:T(8,128)(2,1)}), bf16[1,1024,3584]{2,1,0:T(8,128)(2,1)}) %all-gather.4.cloned.1.call-update) | async-done | bytes 7340048 | tf_op jit(solution)/shard_map/all_gather | solution.py:80
  104.5 0.0 copy-done.4
  104.5 5.6 %fusion.4 = (f32[128]{0:T(128)S(1)}, f32[128,1024]{1,0:T(8,128)S(1)}) fusion(bf16[1,1,16,8,1024]{4,3,2,1,0:T(8,128)(2,1)S(1)} %copy-done.4, bf16[1,1024,3584]{2,1,0:T(8,128)(2,1)} %all-gather.4.cloned.1.call-done, bf16[16,8,3584]{2,1,0:T(8,128)(2,1)S(1)} %all-to-all-done.1), kind=kOutput, calls=%fused_computation.12 | convolution fusion | flops 939917184 | bytes 9044480 | tf_op jit(solution)/shard_map/dot_general | solution.py:78
  110.2 0.7 all_to_all.20
  110.9 5.6 %all-to-all-start.2 = ((f32[16,1,8]{2,1,0:T(1,128)}), f32[16,1,8]{2,1,0:T(1,128)S(1)}, u32[]{:S(2)}, u32[]{:S(2)}) async-start(f32[16,1,8]{2,1,0:T(1,128)} %bitcast.11), calls=%async_computation.2 | async-start | bytes 16384 | tf_op jit(solution)/shard_map/all_to_all | solution.py:88
  116.5 0.0 reduce-scatter.4.cloned.1.call-start
  116.5 6.3 %all-to-all-done.2 = f32[16,1,8]{2,1,0:T(1,128)S(1)} async-done(((f32[16,1,8]{2,1,0:T(1,128)}), f32[16,1,8]{2,1,0:T(1,128)S(1)}, u32[]{:S(2)}, u32[]{:S(2)}) %all-to-all-start.2) | async-done | bytes 544 | tf_op jit(solution)/shard_map/all_to_all | solution.py:88
  122.8 0.1 copy.50
  122.9 0.1 copy.55
  122.9 0.2 fusion.10
  123.2 0.1 select_reduce_fusion
  123.4 0.0 copy-done
  123.4 0.0 copy-start.3
  123.4 2.8 %convolution_bitcast_fusion = f32[3584,192]{0,1:T(8,128)} fusion(f32[128,192]{0,1:T(8,128)S(1)} %multiply_add_fusion, bf16[128,3584]{1,0:T(8,128)(2,1)S(1)} %copy-done), kind=kOutput, calls=%fused_computation.4 | convolution fusion | flops 1056964608 | bytes 3768320 | tf_op jit(solution)/shard_map/dot_general | solution.py:97
  126.2 4.7 %copy.57 = f32[3584,192]{1,0:T(8,128)} copy(f32[3584,192]{0,1:T(8,128)} %convolution_bitcast_fusion) | data formatting | bytes 5505024
  130.9 0.0 copy-done.3
  130.9 0.0 reduce-scatter.4.cloned.1.call-update
  130.9 0.2 fusion.13
  131.1 0.1 copy.54
  131.2 0.7 copy.48
  131.9 3.5 %all-to-all-start = ((bf16[16,1,8]{2,1,0:T(2,128)(2,1)}), bf16[16,1,8]{2,1,0:T(2,128)(2,1)S(1)}, u32[]{:S(2)}, u32[]{:S(2)}) async-start(bf16[16,1,8]{2,1,0:T(2,128)(2,1)} %copy.48), calls=%async_computation | async-start | bytes 16384 | tf_op jit(solution)/shard_map/all_to_all | solution.py:75
  135.4 0.0 all-reduce.2.cloned.1.call-start
  135.4 6.2 %all-to-all-done = bf16[16,1,8]{2,1,0:T(2,128)(2,1)S(1)} async-done(((bf16[16,1,8]{2,1,0:T(2,128)(2,1)}), bf16[16,1,8]{2,1,0:T(2,128)(2,1)S(1)}, u32[]{:S(2)}, u32[]{:S(2)}) %all-to-all-start) | async-done | bytes 288 | tf_op jit(solution)/shard_map/all_to_all | solution.py:75
  141.7 0.1 reshape.135
  141.8 54.3 %reduce-scatter.4.cloned.1.call-done = f32[224,192]{1,0:T(8,128)} async-done(((f32[3584,192]{1,0:T(8,128)}), f32[224,192]{1,0:T(8,128)}) %reduce-scatter.4.cloned.1.call-update) | async-done | bytes 172048
  196.1 1.0 copy.58
  197.2 5.3 %all-gather.1 = bf16[2,224,192]{1,2,0:T(8,128)(2,1)S(1)} all-gather(bf16[1,224,192]{1,2,0:T(8,128)(2,1)S(1)} %convert_bitcast_fusion), channel_id=2, replica_groups=mesh['dp'=2,'expert'=16] {'dp'}, dimensions={0}, use_global_device_ids=true | all-gather | bytes 258048 | tf_op jit(solution)/shard_map/all_gather | solution.py:12
  202.4 0.5 while.14
  202.5 0.1 copy.61
  202.6 0.1 add_select_fusion.2
  202.7 0.1 copy.61
  202.8 0.1 add_select_fusion.2
  202.9 0.1 copy.52
  203.1 0.7 fusion.6
  203.7 0.0 all-reduce.2.cloned.1.call-update
  203.8 0.8 fusion.5
  204.6 19.2 %all-reduce.2.cloned.1.call-done = bf16[224,192]{0,1:T(8,128)(2,1)} async-done(((bf16[224,192]{0,1:T(8,128)(2,1)}), bf16[224,192]{0,1:T(8,128)(2,1)}) %all-reduce.2.cloned.1.call-update) | async-done | bytes 86032 | tf_op jit(solution)/shard_map/psum | solution.py:25
  223.7 1.4 dynamic-slice_convert_fusion
  (18 shorter events, 0.3 us)
Async XLA Ops:
  7.2 116.2 %copy-start = (bf16[128,3584]{1,0:T(8,128)(2,1)S(1)}, bf16[128,3584]{1,0:T(8,128)(2,1)}, u32[]{:S(2)}) copy-start(bf16[128,3584]{1,0:T(8,128)(2,1)} %param.8) | copy-start | bytes 2752516
  7.2 0.8 copy-start.5
  7.2 1.3 copy-start.2
  7.2 10.0 %copy-start.1 = (f32[128,192]{0,1:T(8,128)S(1)}, f32[128,192]{0,1:T(8,128)}, u32[]{:S(2)}) copy-start(f32[128,192]{0,1:T(8,128)} %param.10) | copy-start | bytes 294916
  7.2 97.3 %copy-start.4 = (bf16[1,1,16,8,1024]{4,3,2,1,0:T(8,128)(2,1)S(1)}, bf16[1,1,16,8,1024]{4,3,2,1,0:T(8,128)(2,1)}, u32[]{:S(2)}) copy-start(bf16[1,1,16,8,1024]{4,3,2,1,0:T(8,128)(2,1)} %param.12) | copy-start | bytes 786436
  7.2 97.3 %all-gather.4.cloned.1.call-start = ((), (), s32[]{:S(2)}) async-start(), calls=%async_computation.4 | async-start | bytes 11010048 | tf_op jit(solution)/shard_map/all_gather | solution.py:80
  9.8 28.2 %all-to-all-start.1 = ((bf16[16,8,3584]{2,1,0:T(8,128)(2,1)}), bf16[16,8,3584]{2,1,0:T(8,128)(2,1)S(1)}, u32[]{:S(2)}, u32[]{:S(2)}) async-start(bf16[16,8,3584]{2,1,0:T(8,128)(2,1)} %convolution_convert_fusion), calls=%async_computation.1 | async-start | bytes 1835008 | tf_op jit(solution)/shard_map/all_to_all | solution.py:74
  110.9 12.0 %all-to-all-start.2 = ((f32[16,1,8]{2,1,0:T(1,128)}), f32[16,1,8]{2,1,0:T(1,128)S(1)}, u32[]{:S(2)}, u32[]{:S(2)}) async-start(f32[16,1,8]{2,1,0:T(1,128)} %bitcast.11), calls=%async_computation.2 | async-start | bytes 16384 | tf_op jit(solution)/shard_map/all_to_all | solution.py:88
  116.5 79.6 %reduce-scatter.4.cloned.1.call-start = ((), (), s32[]{:S(2)}) async-start(), calls=%async_computation.6 | async-start | bytes 3899392
  123.4 7.5 %copy-start.3 = (f32[128,192]{0,1:T(8,128)}, f32[128,192]{0,1:T(8,128)S(1)}, u32[]{:S(2)}) copy-start(f32[128,192]{0,1:T(8,128)S(1)} %multiply_add_fusion) | copy-start | bytes 294916
  131.9 9.8 %all-to-all-start = ((bf16[16,1,8]{2,1,0:T(2,128)(2,1)}), bf16[16,1,8]{2,1,0:T(2,128)(2,1)S(1)}, u32[]{:S(2)}, u32[]{:S(2)}) async-start(bf16[16,1,8]{2,1,0:T(2,128)(2,1)} %copy.48), calls=%async_computation | async-start | bytes 16384 | tf_op jit(solution)/shard_map/all_to_all | solution.py:75
  135.4 88.4 %all-reduce.2.cloned.1.call-start = ((), (), s32[]{:S(2)}) async-start(), calls=%async_computation.5 | async-start | bytes 196608 | tf_op jit(solution)/shard_map/psum | solution.py:25
Sparse Core Ops, SparseCore 0:
  9.6 94.8 all-gather.3
  131.0 65.0 reduce-scatter.3
  203.9 19.7 all-reduce.1
where the time goes:
time: 232 us
  waiting for transfers between devices  174 us (75%)
  starting transfers between devices  16.6 us (7%)
  between operations  14 us (6%)
  matrix products  10.1 us (4%)
  local copies, waits for them, and re-layouts  8.13 us (4%)
  blocking collectives  5.29 us (2%)
  other arithmetic  3.91 us (2%)
    all_gather x1, waiting for transfers between devices, local(): lax.all_gather(down_weight, 'dp', axis=1, tiled=True)[0]  66.5 us
    unnamed x4, waiting for transfers between devices  55 us
    all_to_all x1, waiting for transfers between devices, local(): lax.all_to_all(send_rows, 'expert', split_axis=0, concat_axis=0, tiled=True)  20.4 us
    psum x1, waiting for transfers between devices, from_root(): return lax.psum(kept, axis)  19.2 us
    all_to_all x1, starting transfers between devices, local(): lax.all_to_all(send_rows, 'expert', split_axis=0, concat_axis=0, tiled=True)  7.38 us
    all_to_all x1, waiting for transfers between devices, local(): lax.all_to_all(gate_grad, 'expert', split_axis=0, concat_axis=0, tiled=True)  6.27 us
    all_to_all x1, waiting for transfers between devices, local(): lax.all_to_all(send_gates, 'expert', split_axis=0, concat_axis=0, tiled=T...  6.24 us
    unnamed x14, local copies, waits for them, and re-layouts  5.92 us
  transfers between devices with their start and end apart: 6, of which 6 were waited for; matrix products, arithmetic and copies ran while one was open for 2% of the time, Pallas kernels for 0%

commit v1 on v0

--- a/solution.py
+++ b/solution.py
@@ -1,6 +1,8 @@
 import jax
 import jax.numpy as jnp
 from jax import lax
+from jax.experimental import pallas as pl
+from jax.experimental.pallas import tpu as pltpu
 from jax.sharding import PartitionSpec as P
 
 RSCALE = 2.827
@@ -40,7 +42,7 @@
     return lax.dynamic_slice_in_dim(panel, lax.axis_index("dp") * count, count, 1)
 
 
-def local(tokens_in, out_grad, router_logits, expert_ids, saved_hidden, down_weight):
+def general_local(tokens_in, out_grad, router_logits, expert_ids, saved_hidden, down_weight):
     highest = lax.Precision.HIGHEST
     flight = lax.axis_size("expert")
     cap = saved_hidden.shape[3]
@@ -110,6 +112,327 @@
     return (hidden_grad, logit_grad, router_grad)
 
 
+NT = (((1,), (1,)), ((), ()))
+NN = (((1,), (0,)), ((), ()))
+VMEM_LIMIT = 48 * 1024 * 1024
+
+
+def kernel_call(body, out_shape, name, flops, touched, *operands, smem=0):
+    specs = [
+        pl.BlockSpec(memory_space=pltpu.SMEM if k < smem else pltpu.VMEM)
+        for k in range(len(operands))
+    ]
+    return pl.pallas_call(
+        body,
+        out_shape=out_shape,
+        in_specs=specs,
+        out_specs=jax.tree.map(lambda _: pl.BlockSpec(memory_space=pltpu.VMEM), out_shape),
+        compiler_params=pltpu.CompilerParams(vmem_limit_bytes=VMEM_LIMIT),
+        cost_estimate=pl.CostEstimate(flops=flops, bytes_accessed=touched, transcendentals=0),
+        name=name,
+    )(*operands)
+
+
+def iota(shape, dim):
+    return lax.broadcasted_iota(jnp.int32, shape, dim)
+
+
+def three_halves(value):
+    high = value.astype(jnp.bfloat16)
+    rest = value - high.astype(jnp.float32)
+    middle = rest.astype(jnp.bfloat16)
+    low = (rest - middle.astype(jnp.float32)).astype(jnp.bfloat16)
+    return high, middle, low
+
+
+def ranks(chosen):
+    tokens = chosen.shape[1]
+    before = (iota((tokens, tokens), 0) < iota((tokens, tokens), 1)).astype(jnp.bfloat16)
+    return lax.dot_general(
+        chosen.astype(jnp.bfloat16), before, NN, preferred_element_type=jnp.float32
+    )
+
+
+def route_body(logits_ref, ids_ref, z_ref, a_ref, bundle_ref, *, flight):
+    logits = logits_ref[...]
+    ids = ids_ref[...]
+    experts, tokens = logits.shape
+    topk = ids.shape[0]
+    top = jnp.max(logits, axis=0, keepdims=True)
+    shifted = jnp.exp(logits - top)
+    total = jnp.sum(shifted, axis=0, keepdims=True)
+    lse = top + jnp.log(total)
+    z = (2.0 * ZLOSS) * lse * (shifted / total)
+    z_ref[...] = z
+    rows = iota((experts, tokens), 0)
+    chosen = [
+        jnp.sum(jnp.where(rows == ids[k : k + 1], logits, 0.0), axis=0, keepdims=True)
+        for k in range(topk)
+    ]
+    scores = jax.nn.sigmoid(jnp.concatenate(chosen, axis=0))
+    ssum = jnp.sum(scores, axis=0, keepdims=True)
+    gates = RSCALE * scores / ssum
+    slope = (RSCALE / ssum) * scores * (1.0 - scores)
+    dense = jnp.zeros((experts, tokens), jnp.float32)
+    window = iota((flight, tokens), 0)
+    gate_te = jnp.zeros((flight, tokens), jnp.float32)
+    picked = jnp.zeros((flight, tokens), jnp.float32)
+    for k in range(topk):
+        dense = jnp.where(rows == ids[k : k + 1], slope[k : k + 1], dense)
+        gate_te = jnp.where(window == ids[k : k + 1], gates[k : k + 1], gate_te)
+        picked = jnp.where(window == ids[k : k + 1], 1.0, picked)
+    a_ref[...] = dense
+    slot = jnp.where(picked > 0.0, ranks(picked), -1.0)
+    high, middle, low = three_halves(gate_te)
+    bundle_ref[0:experts] = z.astype(jnp.bfloat16)
+    bundle_ref[experts : experts + 16] = jnp.concatenate(
+        [ids.astype(jnp.float32), slope], axis=0
+    ).astype(jnp.bfloat16)
+    bundle_ref[experts + 16 : experts + 32] = slot.astype(jnp.bfloat16)
+    bundle_ref[experts + 32 : experts + 48] = high
+    bundle_ref[experts + 48 : experts + 64] = middle
+    bundle_ref[experts + 64 : experts + 80] = low
+
+
+def pack_body(place_ref, ids_ref, ids_peer_ref, out_grad_ref, out_grad_peer_ref, *outs, cap):
+    me = place_ref[1]
+    parts = []
+    for ids_one, grad_one in ((ids_ref, out_grad_ref), (ids_peer_ref, out_grad_peer_ref)):
+        ids = ids_one[...]
+        topk, tokens = ids.shape
+        wanted = (iota((8, tokens), 0) * 2) ^ me
+        picked = jnp.zeros((8, tokens), jnp.float32)
+        for k in range(topk):
+            picked = jnp.where(wanted == ids[k : k + 1], 1.0, picked)
+        slot = jnp.where(picked > 0.0, ranks(picked), -1.0)
+        place = iota((cap, tokens), 0).astype(jnp.float32)
+        select = jnp.concatenate(
+            [jnp.where(slot[q : q + 1] == place, 1.0, 0.0) for q in range(8)], axis=0
+        )
+        parts.append(
+            lax.dot_general(
+                select.astype(jnp.bfloat16), grad_one[...], NN, preferred_element_type=jnp.float32
+            )
+        )
+    for q, out in enumerate(outs):
+        rows = slice(q * cap, (q + 1) * cap)
+        out[...] = jnp.concatenate([parts[0][rows], parts[1][rows]], axis=0).astype(jnp.bfloat16)
+
+
+def turn_body(tokens_ref, out_ref):
+    out_ref[...] = tokens_ref[...].T
+
+
+def swap_matrix(me, size, cap, dtype):
+    return (iota((size, size), 1) == (iota((size, size), 0) ^ (me * cap))).astype(dtype)
+
+
+def grads_body(place_ref, saved_ref, saved_other_ref, weight_ref, *refs, cap):
+    pieces, (own_ref, other_ref, gate_ref) = refs[:16], refs[16:]
+    dp, me = place_ref[0], place_ref[1]
+    weight = weight_ref[...]
+    slots = saved_ref.shape[0]
+    swap = swap_matrix(me, slots, cap, jnp.bfloat16)
+    where_to = swap_matrix(me, slots, cap, jnp.float32)
+    lines = []
+    for half, saved_one in enumerate((saved_ref, saved_other_ref)):
+        rows = jnp.concatenate([p[...] for p in pieces[half * 8 : half * 8 + 8]], axis=0)
+        grads = lax.dot_general(rows, weight, NT, preferred_element_type=jnp.float32)
+        saved = lax.dot_general(swap, saved_one[...], NN, preferred_element_type=jnp.float32)
+        if half == 0:
+            own_ref[...] = grads
+        else:
+            other_ref[...] = grads.astype(jnp.bfloat16)
+        sums = jnp.sum(saved * grads, axis=1, keepdims=True)
+        lines.append(jnp.sum(where_to * sums, axis=0, keepdims=True))
+    count = gate_ref.shape[0] // 2
+    for k in range(2):
+        line = jnp.where(dp == k, lines[0], lines[1])
+        gate_ref[k * count : (k + 1) * count] = jnp.broadcast_to(
+            line[None], (count, 1, line.shape[1])
+        )
+
+
+def hidden_body(place_ref, own_ref, other_ref, *refs, cap, experts):
+    bundles, out_ref = refs[:4], refs[4]
+    dp, me = place_ref[0], place_ref[1]
+    slots, half = own_ref.shape
+    tokens = bundles[0].shape[2]
+    mine = iota((16, tokens), 0) == me
+    place = iota((cap, tokens), 0).astype(jnp.float32)
+    columns = []
+    for r in range(16):
+        bundle = bundles[r % 4]
+        slot = bundle[r // 4, experts + 16 : experts + 32].astype(jnp.float32)
+        gate = bundle[r // 4, experts + 32 : experts + 48].astype(jnp.float32)
+        slot = jnp.sum(jnp.where(mine, slot, 0.0), axis=0, keepdims=True)
+        gate = jnp.sum(jnp.where(mine, gate, 0.0), axis=0, keepdims=True)
+        columns.append(jnp.sum(jnp.where(slot == place, gate, 0.0), axis=1, keepdims=True))
+    gates = jnp.concatenate(columns, axis=0)
+    swap = swap_matrix(me, slots, cap, jnp.bfloat16)
+    for k, part in enumerate((own_ref, other_ref)):
+        value = (gates * part[...].astype(jnp.float32)).astype(jnp.bfloat16)
+        value = lax.dot_general(swap, value, NN, preferred_element_type=jnp.float32)
+        start = pl.multiple_of((dp if k == 0 else 1 - dp) * half, 128)
+        out_ref[:, pl.ds(start, half)] = value.astype(jnp.bfloat16)
+
+
+def panel_body(place_ref, z_ref, a_ref, gate_ref, turned_ref, *refs, cap, experts):
+    bundles, (logit_ref, keep_ref, send_ref) = refs[:4], refs[4:7]
+    dp, me = place_ref[0], place_ref[1]
+    tokens = z_ref.shape[1]
+    both = jnp.concatenate([gate_ref[k] for k in range(gate_ref.shape[0])], axis=0)
+    gate_abs = both[:16] + both[16:]
+    swap = swap_matrix(me, gate_abs.shape[1], cap, jnp.bfloat16)
+    gate_rel = sum(
+        lax.dot_general(part, swap, NN, preferred_element_type=jnp.float32)
+        for part in three_halves(gate_abs)
+    )
+    rows = iota((experts, tokens), 0).astype(jnp.float32)
+    lines, blocks = [], []
+    total = None
+    for r in range(16):
+        bundle = bundles[r % 4]
+        slot = bundle[r // 4, experts + 16 : experts + 32].astype(jnp.float32)
+        gate = sum(
+            bundle[r // 4, experts + 32 + 16 * k : experts + 48 + 16 * k].astype(jnp.float32)
+            for k in (2, 1, 0)
+        )
+        grad = jnp.zeros((16, tokens), jnp.float32)
+        for c in range(cap):
+            grad = jnp.where(slot == float(c), gate_rel[:, r * cap + c : r * cap + c + 1], grad)
+        mixed = jnp.sum(grad * gate, axis=0, keepdims=True) / RSCALE
+        spread = jnp.concatenate(
+            [grad - mixed, jnp.broadcast_to(-mixed, (experts - 16, tokens))], axis=0
+        )
+        if r == 0:
+            line = z_ref[...] + a_ref[...] * spread
+            logit_ref[...] = line
+        else:
+            pairs = bundle[r // 4, experts : experts + 16].astype(jnp.float32)
+            dense = jnp.zeros((experts, tokens), jnp.float32)
+            for k in range(8):
+                dense = jnp.where(rows == pairs[k : k + 1], pairs[8 + k : 9 + k], dense)
+            line = bundle[r // 4, 0:experts].astype(jnp.float32) + dense * spread
+        lines.append(line.astype(jnp.bfloat16))
+        blocks.append(turned_ref[me ^ r])
+        if len(lines) == 2:
+            part = lax.dot_general(
+                jnp.concatenate(lines, axis=1),
+                jnp.concatenate(blocks, axis=1),
+                NT,
+                preferred_element_type=jnp.float32,
+            )
+            total = part if total is None else total + part
+            lines, blocks = [], []
+    count = keep_ref.shape[0]
+    first, second = total[:count], total[count:]
+    keep_ref[...] = jnp.where(dp == 0, first, second)
+    send_ref[...] = jnp.where(dp == 0, second, first).astype(jnp.bfloat16)
+
+
+def over_dp(value):
+    return lax.ppermute(value, "dp", [(0, 1), (1, 0)])
+
+
+def over_expert(value, bits):
+    count = lax.axis_size("expert")
+    return lax.ppermute(value, "expert", [(k, k ^ bits) for k in range(count)])
+
+
+def paired_local(tokens_in, out_grad, router_logits, expert_ids, saved_hidden, down_weight):
+    flight = lax.axis_size("expert")
+    cap, hidden = saved_hidden.shape[3:]
+    tokens, width = out_grad.shape
+    experts = router_logits.shape[1]
+    half = hidden // 2
+    slots = flight * cap
+    f32, bf16 = jnp.float32, jnp.bfloat16
+    dp, me = lax.axis_index("dp"), lax.axis_index("expert")
+    place = jnp.stack([dp, me]).astype(jnp.int32)
+    weight = down_weight[0]
+    logits_t, ids_t = router_logits.T, expert_ids.T
+    saved = saved_hidden.reshape(slots, hidden)
+
+    ids_peer = over_expert(ids_t, 1)
+    grad_peer = over_expert(out_grad, 1)
+    saved_own = lax.dynamic_slice_in_dim(saved, dp * half, half, 1)
+    saved_other = over_dp(lax.dynamic_slice_in_dim(saved, (1 - dp) * half, half, 1))
+
+    bundle_rows = experts + 80
+    z, a, bundle = kernel_call(
+        lambda *refs: route_body(*refs, flight=flight),
+        (
+            jax.ShapeDtypeStruct((experts, tokens), f32),
+            jax.ShapeDtypeStruct((experts, tokens), f32),
+            jax.ShapeDtypeStruct((bundle_rows, tokens), bf16),
+        ),
+        "route", 1 << 22, 1 << 19, logits_t, ids_t,
+    )
+    blocks = kernel_call(
+        lambda *refs: pack_body(*refs, cap=cap),
+        tuple(jax.ShapeDtypeStruct((2 * cap, width), bf16) for _ in range(8)),
+        "pack", 4 * slots * tokens * width, 3 << 20,
+        place, ids_t, ids_peer, out_grad, grad_peer, smem=1,
+    )
+    own = [None] * 8
+    own[0] = blocks[0]
+    turn = [None] * 4
+    for rz in (3, 2, 1):
+        own[2 * rz] = over_expert(blocks[2 * rz], 4 * rz)
+        turn[rz] = over_expert(blocks[2 * rz + 1], 2)
+    own[1] = over_expert(blocks[1], 2)
+    for rz in (3, 2, 1):
+        own[2 * rz + 1] = over_expert(turn[rz], 4 * rz)
+    other = [over_dp(piece) for piece in own]
+
+    turned = kernel_call(
+        turn_body, jax.ShapeDtypeStruct((width, tokens), bf16), "turn", 1 << 20, 2 << 20, tokens_in
+    )
+    turned = lax.all_to_all(
+        turned.reshape(flight, width // flight, tokens), "expert", 0, 0, tiled=True
+    )
+
+    ring = jnp.stack([bundle] + [over_expert(bundle, 4 * rz) for rz in (1, 2, 3)])
+    ring_y = over_expert(ring, 2)
+    bundles = (ring, over_expert(ring, 1), ring_y, over_expert(ring_y, 1))
+
+    grads_own, grads_other, gate_part = kernel_call(
+        lambda *refs: grads_body(*refs, cap=cap),
+        (
+            jax.ShapeDtypeStruct((slots, half), f32),
+            jax.ShapeDtypeStruct((slots, half), bf16),
+            jax.ShapeDtypeStruct((2 * flight, 1, slots), f32),
+        ),
+        "grads", 4 * slots * width * half, 6 << 20,
+        place, saved_own, saved_other, weight, *own, *other, smem=1,
+    )
+    gate_all = lax.all_to_all(gate_part, ("dp", "expert"), 0, 0, tiled=True)
+    grads_back = over_dp(grads_other)
+    hidden_grad = kernel_call(
+        lambda *refs: hidden_body(*refs, cap=cap, experts=experts),
+        jax.ShapeDtypeStruct((slots, hidden), bf16),
+        "hidden", 1 << 24, 1 << 20,
+        place, grads_own, grads_back, *bundles, smem=1,
+    )
+    logit_t, keep, send = kernel_call(
+        lambda *refs: panel_body(*refs, cap=cap, experts=experts),
+        (
+            jax.ShapeDtypeStruct((experts, tokens), f32),
+            jax.ShapeDtypeStruct((experts // 2, width // flight), f32),
+            jax.ShapeDtypeStruct((experts // 2, width // flight), bf16),
+        ),
+        "panel", 1 << 28, 4 << 20,
+        place, z, a, gate_all, turned, *bundles, smem=1,
+    )
+    router_t = keep + over_dp(send).astype(f32)
+    return (
+        hidden_grad.reshape(1, 1, flight, cap, hidden),
+        logit_t.T,
+        router_t.T,
+    )
+
+
 def solution(mesh):
     in_specs = (
         P(("dp", "expert"), None),
@@ -120,4 +443,6 @@
         P("expert", "dp", None),
     )
     out_specs = (P("dp", "expert", None, None, None), P(("dp", "expert"), None), P("expert", "dp"))
+    paired = mesh.shape["dp"] == 2 and mesh.shape["expert"] == 16
+    local = paired_local if paired else general_local
     return jax.shard_map(local, mesh=mesh, in_specs=in_specs, out_specs=out_specs, check_vma=False)

time: 232 us -> 113 us (0.49)
  waiting for transfers between devices: 174 us -> 53.3 us
  starting transfers between devices: 16.6 us -> 42.4 us
  between operations: 14 us -> 0.73 us
  Pallas kernels: 0 us -> 10.7 us
  matrix products: 10.1 us -> 0 us
  blocking collectives: 5.29 us -> 0 us
  local copies, waits for them, and re-layouts: 8.13 us -> 4.9 us
  other arithmetic: 3.91 us -> 0.76 us
    all_gather x1 -> x0, waiting for transfers between devices: 66.5 us -> none  [local(): lax.all_gather(down_weight, 'dp', axis=1, tiled=True)[0]]
    unnamed x4 -> x0, waiting for transfers between devices: 55 us -> none
    ppermute x0 -> x29, waiting for transfers between devices: none -> 47.5 us  [the longest x18 38.7 us: over_expert(): return lax.ppermute(value, 'expert', [(k, k ^ bits) for k in range(count)])]
    ppermute x0 -> x29, starting transfers between devices: none -> 33.7 us  [the longest x18 22.3 us: over_expert(): return lax.ppermute(value, 'expert', [(k, k ^ bits) for k in range(count)])]
    all_to_all x3 -> x2, waiting for transfers between devices: 33 us -> 5.84 us  [the longest x1 5.83 us: paired_local(): gate_all = lax.all_to_all(gate_part, ('dp', 'expert'), 0, 0, tiled=True)]
    psum x1 -> x0, waiting for transfers between devices: 19.2 us -> none  [from_root(): return lax.psum(kept, axis)]
    pallas_call x0 -> x6, Pallas kernels: none -> 10.7 us  [kernel_call(): pl.pallas_call(body, out_shape=out_shape, in_specs=specs, out_specs=jax.t...]
    dot_general x5 -> x0, matrix products: 10.1 us -> none  [the longest x1 5.63 us: local(): lax.dot_general(flat_rows, lax.all_gather(down_weight, 'dp', axis=1, tile...]
  transfers between devices with their start and end apart: 6 -> 31, of which waited for: 6 -> 14; matrix products, arithmetic and copies ran while one was open for 2% -> 1% of each run, Pallas kernels for 0% -> 6%
where the time goes in v1:
time: 113 us
  waiting for transfers between devices  53.3 us (47%)
  starting transfers between devices  42.4 us (38%)
  Pallas kernels  10.7 us (9%)
  local copies, waits for them, and re-layouts  4.9 us (4%)
    ppermute x18, waiting for transfers between devices, over_expert(): return lax.ppermute(value, 'expert', [(k, k ^ bits) for k in range(count)])  38.7 us
    ppermute x18, starting transfers between devices, over_expert(): return lax.ppermute(value, 'expert', [(k, k ^ bits) for k in range(count)])  22.3 us
    ppermute x11, starting transfers between devices, over_dp(): return lax.ppermute(value, 'dp', [(0, 1), (1, 0)])  11.4 us
    pallas_call x6, Pallas kernels, kernel_call(): pl.pallas_call(body, out_shape=out_shape, in_specs=specs, out_specs=jax.t...  10.7 us
    ppermute x11, waiting for transfers between devices, over_dp(): return lax.ppermute(value, 'dp', [(0, 1), (1, 0)])  8.72 us
    all_to_all x1, waiting for transfers between devices, paired_local(): gate_all = lax.all_to_all(gate_part, ('dp', 'expert'), 0, 0, tiled=True)  5.83 us
    all_to_all x1, starting transfers between devices, paired_local(): gate_all = lax.all_to_all(gate_part, ('dp', 'expert'), 0, 0, tiled=True)  5.08 us
    unnamed x12, local copies, waits for them, and re-layouts  3.92 us
  transfers between devices with their start and end apart: 31, of which 14 were waited for; matrix products, arithmetic and copies ran while one was open for 1% of the time, Pallas kernels for 6%

profile of v1, /device:TPU:0, one launch (start us, length us, event | category | flops | bytes accessed | tf_op | source)
XLA Modules:
  0.0 112.8 jit_solution(11209063555534961277)
XLA Ops:
  0.6 0.5 collective-permute-start.2
  1.1 1.0 constant_dynamic-slice_fusion
  2.1 2.6 %collective-permute-start = (bf16[128,512]{1,0:T(8,128)(2,1)S(1)}, bf16[128,512]{1,0:T(8,128)(2,1)S(1)}, u32[]{:S(2)}, u32[]{:S(2)}) collective-permute-start(bf16[128,512]{1,0:T(8,128)(2,1)S(1)} %get-tuple-element.37), channel_id=1, source_target_pairs={{0,16},{16,0},{1,17},{17,1},{2,18},{18,2},{3,19},{19,3},{4,20},{20... | collective-permute-start | bytes 393224 | tf_op jit(solution)/shard_map/ppermute | solution.py:335
  4.7 0.2 collective-permute-start.1
  4.9 0.1 pad_add_fusion.refs_0_
  5.0 1.1 collective-permute-done.1.refs_2_
  6.1 1.2 %copy-done.2 = bf16[128,3584]{1,0:T(8,128)(2,1)S(1)} copy-done((bf16[128,3584]{1,0:T(8,128)(2,1)S(1)}, bf16[128,3584]{1,0:T(8,128)(2,1)}, u32[]{:S(2)}) %copy-start.2) | copy-done | bytes 917528
  7.3 0.7 copy-done.4
  8.0 1.2 %pack.1 = (bf16[16,3584]{1,0:T(8,128)(2,1)S(1)}, bf16[16,3584]{1,0:T(8,128)(2,1)S(1)}, bf16[16,3584]{1,0:T(8,128)(2,1)S(1)}, bf16[16,3584]{1,0:T(8,128)(2,1)S(1)...) custom-call(s32[2]{0:T(128)S(1)} %pad_add_fusion.refs_0_, ...), custom_call_target="tpu_custom_call" | custom-call | flops 234881024 | bytes 3145728 | tf_op jit(solution)/shard_map/pack/pallas_call | solution.py:125
  9.2 1.6 %collective-permute-start.3 = (bf16[16,3584]{1,0:T(8,128)(2,1)S(1)}, bf16[16,3584]{1,0:T(8,128)(2,1)S(1)}, u32[]{:S(2)}, u32[]{:S(2)}) collective-permute-start(bf16[16,3584]{1,0:T(8,128)(2,1)S(1)} %get-tuple-element.21), channel_id=1, source_target_pairs={{0,2},{1,3},{2,0},{3,1},{4,6},{5,7},{6,4},{7,5},{8,10},{9,11},{10,... | collective-permute-start | bytes 344072 | tf_op jit(solution)/shard_map/ppermute | solution.py:340
  10.8 1.6 %collective-permute-start.4 = (bf16[16,3584]{1,0:T(8,128)(2,1)S(1)}, bf16[16,3584]{1,0:T(8,128)(2,1)S(1)}, u32[]{:S(2)}, u32[]{:S(2)}) collective-permute-start(bf16[16,3584]{1,0:T(8,128)(2,1)S(1)} %get-tuple-element.22), channel_id=1, source_target_pairs={{0,4},{1,5},{2,6},{3,7},{4,0},{5,1},{6,2},{7,3},{8,12},{9,13},{10,... | collective-permute-start | bytes 344072 | tf_op jit(solution)/shard_map/ppermute | solution.py:340
  12.3 0.5 collective-permute-start.5
  12.8 2.6 %collective-permute-start.7 = (bf16[16,3584]{1,0:T(8,128)(2,1)S(1)}, bf16[16,3584]{1,0:T(8,128)(2,1)S(1)}, u32[]{:S(2)}, u32[]{:S(2)}) collective-permute-start(bf16[16,3584]{1,0:T(8,128)(2,1)S(1)} %get-tuple-element.24), channel_id=1, source_target_pairs={{0,8},{1,9},{2,10},{3,11},{4,12},{5,13},{6,14},{7,15},{8,0},{9,1},... | collective-permute-start | bytes 344072 | tf_op jit(solution)/shard_map/ppermute | solution.py:340
  15.4 1.5 %collective-permute-start.8 = (bf16[16,3584]{1,0:T(8,128)(2,1)S(1)}, bf16[16,3584]{1,0:T(8,128)(2,1)S(1)}, u32[]{:S(2)}, u32[]{:S(2)}) collective-permute-start(bf16[16,3584]{1,0:T(8,128)(2,1)S(1)} %get-tuple-element.25), channel_id=1, source_target_pairs={{0,2},{1,3},{2,0},{3,1},{4,6},{5,7},{6,4},{7,5},{8,10},{9,11},{10,... | collective-permute-start | bytes 344072 | tf_op jit(solution)/shard_map/ppermute | solution.py:340
  16.9 0.5 collective-permute-start.11
  17.5 0.0 collective-permute-done.4.refs_6_
  17.5 2.9 %collective-permute-start.10 = (bf16[16,3584]{1,0:T(8,128)(2,1)S(1)}, bf16[16,3584]{1,0:T(8,128)(2,1)S(1)}, u32[]{:S(2)}, u32[]{:S(2)}) collective-permute-start(bf16[16,3584]{1,0:T(8,128)(2,1)S(1)} %get-tuple-element.26), channel_id=1, source_target_pairs={{0,12},{1,13},{2,14},{3,15},{4,8},{5,9},{6,10},{7,11},{8,4},{9,5},... | collective-permute-start | bytes 344072 | tf_op jit(solution)/shard_map/ppermute | solution.py:340
  20.4 0.0 collective-permute-done.5
  20.4 0.5 collective-permute-start.13
  20.9 1.4 %collective-permute-done.7.refs_8_ = bf16[16,3584]{1,0:T(8,128)(2,1)S(1)} collective-permute-done((bf16[16,3584]{1,0:T(8,128)(2,1)S(1)}, bf16[16,3584]{1,0:T(8,128)(2,1)S(1)}, u32[]{:S(2)}, u32[]{:S(2)}) %collective-permute-start.7) | collective-permute-done | bytes 114720 | tf_op jit(solution)/shard_map/ppermute | solution.py:340
  22.3 0.0 collective-permute-start.6
  22.4 0.0 collective-permute-done.8
  22.4 3.7 %collective-permute-start.9 = (bf16[16,3584]{1,0:T(8,128)(2,1)S(1)}, bf16[16,3584]{1,0:T(8,128)(2,1)S(1)}, u32[]{:S(2)}, u32[]{:S(2)}) collective-permute-start(bf16[16,3584]{1,0:T(8,128)(2,1)S(1)} %collective-permute-done.8), channel_id=1, source_target_pairs={{0,8},{1,9},{2,10},{3,11},{4,12},{5,13},{6,14},{7,15},{8,0},{9,1},... | collective-permute-start | bytes 344072 | tf_op jit(solution)/shard_map/ppermute | solution.py:340
  26.0 0.0 collective-permute-done.11
  26.0 0.7 collective-permute-start.12
  26.7 0.6 collective-permute-start.14
  27.3 1.5 %collective-permute-start.15 = (bf16[16,3584]{1,0:T(8,128)(2,1)S(1)}, bf16[16,3584]{1,0:T(8,128)(2,1)S(1)}, u32[]{:S(2)}, u32[]{:S(2)}) collective-permute-start(bf16[16,3584]{1,0:T(8,128)(2,1)S(1)} %collective-permute-done.4.refs_6_), channel_id=1, source_target_pairs={{0,16},{16,0},{1,17},{17,1},{2,18},{18,2},{3,19},{19,3},{4,20},{20... | collective-permute-start | bytes 344072 | tf_op jit(solution)/shard_map/ppermute | solution.py:335
  28.8 0.0 collective-permute-done.6.refs_7_
  28.8 1.0 collective-permute-start.17
  29.8 3.6 %collective-permute-done.9.refs_9_ = bf16[16,3584]{1,0:T(8,128)(2,1)S(1)} collective-permute-done((bf16[16,3584]{1,0:T(8,128)(2,1)S(1)}, bf16[16,3584]{1,0:T(8,128)(2,1)S(1)}, u32[]{:S(2)}, u32[]{:S(2)}) %collective-permute-start.9) | collective-permute-done | bytes 114720 | tf_op jit(solution)/shard_map/ppermute | solution.py:340
  33.4 0.6 collective-permute-start.19
  34.0 0.0 collective-permute-done.12.refs_11_
  34.0 1.5 %collective-permute-start.16 = (bf16[16,3584]{1,0:T(8,128)(2,1)S(1)}, bf16[16,3584]{1,0:T(8,128)(2,1)S(1)}, u32[]{:S(2)}, u32[]{:S(2)}) collective-permute-start(bf16[16,3584]{1,0:T(8,128)(2,1)S(1)} %collective-permute-done.6.refs_7_), channel_id=1, source_target_pairs={{0,16},{16,0},{1,17},{17,1},{2,18},{18,2},{3,19},{19,3},{4,20},{20... | collective-permute-start | bytes 344072 | tf_op jit(solution)/shard_map/ppermute | solution.py:335
  35.4 0.6 collective-permute-start.18
  36.0 1.5 %collective-permute-start.20 = (bf16[16,3584]{1,0:T(8,128)(2,1)S(1)}, bf16[16,3584]{1,0:T(8,128)(2,1)S(1)}, u32[]{:S(2)}, u32[]{:S(2)}) collective-permute-start(bf16[16,3584]{1,0:T(8,128)(2,1)S(1)} %collective-permute-done.12.refs_11_), channel_id=1, source_target_pairs={{0,16},{16,0},{1,17},{17,1},{2,18},{18,2},{3,19},{19,3},{4,20},{20... | collective-permute-start | bytes 344072 | tf_op jit(solution)/shard_map/ppermute | solution.py:335
  37.5 0.0 collective-permute-done.17.refs_16_
  37.5 2.0 %collective-permute-done.19.refs_18_ = bf16[16,3584]{1,0:T(8,128)(2,1)S(1)} collective-permute-done((bf16[16,3584]{1,0:T(8,128)(2,1)S(1)}, bf16[16,3584]{1,0:T(8,128)(2,1)S(1)}, u32[]{:S(2)}, u32[]{:S(2)}) %collective-permute-start.19) | collective-permute-done | bytes 114720 | tf_op jit(solution)/shard_map/ppermute | solution.py:335
  39.5 2.4 %collective-permute-done.16.refs_15_ = bf16[16,3584]{1,0:T(8,128)(2,1)S(1)} collective-permute-done((bf16[16,3584]{1,0:T(8,128)(2,1)S(1)}, bf16[16,3584]{1,0:T(8,128)(2,1)S(1)}, u32[]{:S(2)}, u32[]{:S(2)}) %collective-permute-start.16) | collective-permute-done | bytes 114720 | tf_op jit(solution)/shard_map/ppermute | solution.py:335
  41.9 1.2 %collective-permute-done.18.refs_17_ = bf16[16,3584]{1,0:T(8,128)(2,1)S(1)} collective-permute-done((bf16[16,3584]{1,0:T(8,128)(2,1)S(1)}, bf16[16,3584]{1,0:T(8,128)(2,1)S(1)}, u32[]{:S(2)}, u32[]{:S(2)}) %collective-permute-start.18) | collective-permute-done | bytes 114720 | tf_op jit(solution)/shard_map/ppermute | solution.py:335
  43.1 1.2 %collective-permute-done.20.refs_19_ = bf16[16,3584]{1,0:T(8,128)(2,1)S(1)} collective-permute-done((bf16[16,3584]{1,0:T(8,128)(2,1)S(1)}, bf16[16,3584]{1,0:T(8,128)(2,1)S(1)}, u32[]{:S(2)}, u32[]{:S(2)}) %collective-permute-start.20) | collective-permute-done | bytes 114720 | tf_op jit(solution)/shard_map/ppermute | solution.py:335
  44.3 2.0 %copy-done = bf16[1,512,3584]{2,1,0:T(8,128)(2,1)S(1)} copy-done((bf16[1,512,3584]{2,1,0:T(8,128)(2,1)S(1)}, bf16[1,512,3584]{2,1,0:T(8,128)(2,1)}, u32[]{:S(2)}) %copy-start) | copy-done | bytes 3670040
  46.4 3.8 %grads.1 = (f32[128,512]{1,0:T(8,128)S(1)}, bf16[128,512]{1,0:T(8,128)(2,1)S(1)}, f32[32,1,128]{2,1,0:T(1,128)}) custom-call(s32[2]{0:T(128)S(1)} %pad_add_fusion.refs_0_, bf16[128,512]{1,0:T(8,128)(2,1)S(1)} %get-tuple-element.38.refs_1_, bf16[128,512]{1,0:T(8,128)(2,1)S(1)} %collective-permute-done.refs_2_, bf16[512,3584]{1,0:T(8,128)(2,1)S(1)} %bitcast.15, ...), custom_call_target="tpu_custom_call" | custom-call | flops 939524096 | bytes 6291456 | tf_op jit(solution)/shard_map/grads/pallas_call | solution.py:125
  50.1 5.1 %all-to-all-start = ((f32[32,1,128]{2,1,0:T(1,128)}), f32[32,1,128]{2,1,0:T(1,128)S(1)}, u32[]{:S(2)}, u32[]{:S(2)}) async-start(f32[32,1,128]{2,1,0:T(1,128)} %get-tuple-element.33), calls=%async_computation | async-start | bytes 32768 | tf_op jit(solution)/shard_map/all_to_all | solution.py:410
  55.2 1.2 %turn.1 = bf16[3584,128]{1,0:T(8,128)(2,1)} custom-call(bf16[128,3584]{1,0:T(8,128)(2,1)S(1)} %copy-done.1), custom_call_target="tpu_custom_call" | custom-call | flops 1048576 | bytes 2097152 | tf_op jit(solution)/shard_map/turn/pallas_call | solution.py:125
  56.5 5.8 %all-to-all-done.refs_3_ = f32[32,1,128]{2,1,0:T(1,128)S(1)} async-done(((f32[32,1,128]{2,1,0:T(1,128)}), f32[32,1,128]{2,1,0:T(1,128)S(1)}, u32[]{:S(2)}, u32[]{:S(2)}) %all-to-all-start) | async-done | bytes 16416 | tf_op jit(solution)/shard_map/all_to_all | solution.py:410
  62.3 3.6 %all-to-all-start.1 = ((bf16[16,224,128]{2,1,0:T(8,128)(2,1)}), bf16[16,224,128]{2,1,0:T(8,128)(2,1)S(1)}, u32[]{:S(2)}, u32[]{:S(2)}) async-start(bf16[16,224,128]{2,1,0:T(8,128)(2,1)} %bitcast.11), calls=%async_computation.1 | async-start | bytes 1835008 | tf_op jit(solution)/shard_map/all_to_all | solution.py:392
  66.0 0.3 route.1
  66.3 3.7 %collective-permute-start.24 = (bf16[272,128]{1,0:T(8,128)(2,1)S(1)}, bf16[272,128]{1,0:T(8,128)(2,1)S(1)}, u32[]{:S(2)}, u32[]{:S(2)}) collective-permute-start(bf16[272,128]{1,0:T(8,128)(2,1)S(1)} %get-tuple-element.30), channel_id=1, source_target_pairs={{0,12},{1,13},{2,14},{3,15},{4,8},{5,9},{6,10},{7,11},{8,4},{9,5},... | collective-permute-start | bytes 208904 | tf_op jit(solution)/shard_map/ppermute | solution.py:340
  70.0 0.0 collective-permute-start.23
  70.0 0.7 collective-permute-start.22
  70.7 17.1 %collective-permute-done.24 = bf16[272,128]{1,0:T(8,128)(2,1)S(1)} collective-permute-done((bf16[272,128]{1,0:T(8,128)(2,1)S(1)}, bf16[272,128]{1,0:T(8,128)(2,1)S(1)}, u32[]{:S(2)}, u32[]{:S(2)}) %collective-permute-start.24) | collective-permute-done | bytes 69664 | tf_op jit(solution)/shard_map/ppermute | solution.py:340
  87.8 7.8 %collective-permute-done.23 = bf16[272,128]{1,0:T(8,128)(2,1)S(1)} collective-permute-done((bf16[272,128]{1,0:T(8,128)(2,1)S(1)}, bf16[272,128]{1,0:T(8,128)(2,1)S(1)}, u32[]{:S(2)}, u32[]{:S(2)}) %collective-permute-start.23) | collective-permute-done | bytes 69664 | tf_op jit(solution)/shard_map/ppermute | solution.py:340
  95.6 0.0 collective-permute-done.22
  95.6 1.5 %collective-permute-start.26 = (bf16[4,272,128]{2,1,0:T(8,128)(2,1)S(1)}, bf16[4,272,128]{2,1,0:T(8,128)(2,1)S(1)}, u32[]{:S(2)}, u32[]{:S(2)}) collective-permute-start(bf16[4,272,128]{2,1,0:T(8,128)(2,1)S(1)} %pad_maximum_fusion.refs_3_.refs_5_), channel_id=1, source_target_pairs={{0,2},{1,3},{2,0},{3,1},{4,6},{5,7},{6,4},{7,5},{8,10},{9,11},{10,... | collective-permute-start | bytes 835592 | tf_op jit(solution)/shard_map/ppermute | solution.py:340
  97.2 0.0 collective-permute-start.25
  97.2 6.7 %collective-permute-done.26.refs_5_.refs_7_ = bf16[4,272,128]{2,1,0:T(8,128)(2,1)S(1)} collective-permute-done((bf16[4,272,128]{2,1,0:T(8,128)(2,1)S(1)}, bf16[4,272,128]{2,1,0:T(8,128)(2,1)S(1)}, u32[]{:S(2)}, u32[]{:S(2)}) %collective-permute-start.26) | collective-permute-done | bytes 278560 | tf_op jit(solution)/shard_map/ppermute | solution.py:340
  103.9 0.6 collective-permute-start.21
  104.5 1.0 collective-permute-done.27.refs_6_.refs_8_
  105.5 2.6 %panel.1 = (f32[192,128]{1,0:T(8,128)}, f32[96,224]{1,0:T(8,128)S(1)}, bf16[96,224]{1,0:T(8,128)(2,1)S(1)}) custom-call(s32[2]{0:T(128)S(1)} %pad_add_fusion.refs_0_, f32[192,128]{1,0:T(8,128)S(1)} %get-tuple-element.31.refs_1_, f32[192,128]{1,0:T(8,128)S(1)} %get-tuple-element.32.refs_2_, f32[32,1,128]{2,1,0:T(1,128)S(1)} %all-to-all-done.refs_3_, ...), custom_call_target="tpu_custom_call" | custom-call | flops 268435456 | bytes 4194304 | tf_op jit(solution)/shard_map/panel/pallas_call | solution.py:125
  108.1 0.6 collective-permute-start.28
  108.7 1.1 %collective-permute-done.21.refs_2_ = bf16[128,512]{1,0:T(8,128)(2,1)S(1)} collective-permute-done((bf16[128,512]{1,0:T(8,128)(2,1)S(1)}, bf16[128,512]{1,0:T(8,128)(2,1)S(1)}, u32[]{:S(2)}, u32[]{:S(2)}) %collective-permute-start.21) | collective-permute-done | bytes 131104 | tf_op jit(solution)/shard_map/ppermute | solution.py:335
  109.8 1.7 %hidden.1 = bf16[128,1024]{1,0:T(8,128)(2,1)} custom-call(s32[2]{0:T(128)S(1)} %pad_add_fusion.refs_0_, f32[128,512]{1,0:T(8,128)S(1)} %get-tuple-element.28.refs_1_, bf16[128,512]{1,0:T(8,128)(2,1)S(1)} %collective-permute-done.21.refs_2_, bf16[4,272,128]{2,1,0:T(8,128)(2,1)S(1)} %pad_maximum_fusion.refs_3_.refs_5_, ...), custom_call_target="tpu_custom_call" | custom-call | flops 16777216 | bytes 1048576 | tf_op jit(solution)/shard_map/hidden/pallas_call | solution.py:125
  111.5 0.7 collective-permute-done.28
  112.2 0.7 add_bitcast_fusion
  (20 shorter events, 0.1 us)
Async XLA Ops:
  0.6 5.5 %collective-permute-start.2 = (bf16[128,3584]{1,0:T(8,128)(2,1)}, bf16[128,3584]{1,0:T(8,128)(2,1)S(1)}, u32[]{:S(2)}, u32[]{:S(2)}) collective-permute-start(bf16[128,3584]{1,0:T(8,128)(2,1)} %refs_3_.1), channel_id=1, source_target_pairs={{0,1},{1,0},{2,3},{3,2},{4,5},{5,4},{6,7},{7,6},{8,9},{9,8},{10,11... | collective-permute-start | bytes 2752520 | tf_op jit(solution)/shard_map/ppermute | solution.py:340
  2.1 13.3 %collective-permute-start = (bf16[128,512]{1,0:T(8,128)(2,1)S(1)}, bf16[128,512]{1,0:T(8,128)(2,1)S(1)}, u32[]{:S(2)}, u32[]{:S(2)}) collective-permute-start(bf16[128,512]{1,0:T(8,128)(2,1)S(1)} %get-tuple-element.37), channel_id=1, source_target_pairs={{0,16},{16,0},{1,17},{17,1},{2,18},{18,2},{3,19},{19,3},{4,20},{20... | collective-permute-start | bytes 393224 | tf_op jit(solution)/shard_map/ppermute | solution.py:335
  4.7 1.4 %collective-permute-start.1 = (s32[8,128]{1,0:T(8,128)}, s32[8,128]{1,0:T(8,128)S(1)}, u32[]{:S(2)}, u32[]{:S(2)}) collective-permute-start(s32[8,128]{1,0:T(8,128)} %bitcast.18), channel_id=1, source_target_pairs={{0,1},{1,0},{2,3},{3,2},{4,5},{5,4},{6,7},{7,6},{8,9},{9,8},{10,11... | collective-permute-start | bytes 12296 | tf_op jit(solution)/shard_map/ppermute | solution.py:340
  5.0 50.2 %copy-start.1 = (bf16[128,3584]{1,0:T(8,128)(2,1)S(1)}, bf16[128,3584]{1,0:T(8,128)(2,1)}, u32[]{:S(2)}) copy-start(bf16[128,3584]{1,0:T(8,128)(2,1)} %tokens_ref.1) | copy-start | bytes 2752516
  6.1 1.2 %copy-start.2 = (bf16[128,3584]{1,0:T(8,128)(2,1)S(1)}, bf16[128,3584]{1,0:T(8,128)(2,1)}, u32[]{:S(2)}) copy-start(bf16[128,3584]{1,0:T(8,128)(2,1)} %refs_3_.1) | copy-start | bytes 2752516
  7.3 0.7 copy-start.4
  9.2 7.8 %collective-permute-start.3 = (bf16[16,3584]{1,0:T(8,128)(2,1)S(1)}, bf16[16,3584]{1,0:T(8,128)(2,1)S(1)}, u32[]{:S(2)}, u32[]{:S(2)}) collective-permute-start(bf16[16,3584]{1,0:T(8,128)(2,1)S(1)} %get-tuple-element.21), channel_id=1, source_target_pairs={{0,2},{1,3},{2,0},{3,1},{4,6},{5,7},{6,4},{7,5},{8,10},{9,11},{10,... | collective-permute-start | bytes 344072 | tf_op jit(solution)/shard_map/ppermute | solution.py:340
  10.8 6.7 %collective-permute-start.4 = (bf16[16,3584]{1,0:T(8,128)(2,1)S(1)}, bf16[16,3584]{1,0:T(8,128)(2,1)S(1)}, u32[]{:S(2)}, u32[]{:S(2)}) collective-permute-start(bf16[16,3584]{1,0:T(8,128)(2,1)S(1)} %get-tuple-element.22), channel_id=1, source_target_pairs={{0,4},{1,5},{2,6},{3,7},{4,0},{5,1},{6,2},{7,3},{8,12},{9,13},{10,... | collective-permute-start | bytes 344072 | tf_op jit(solution)/shard_map/ppermute | solution.py:340
  12.3 8.1 %collective-permute-start.5 = (bf16[16,3584]{1,0:T(8,128)(2,1)S(1)}, bf16[16,3584]{1,0:T(8,128)(2,1)S(1)}, u32[]{:S(2)}, u32[]{:S(2)}) collective-permute-start(bf16[16,3584]{1,0:T(8,128)(2,1)S(1)} %get-tuple-element.23), channel_id=1, source_target_pairs={{0,2},{1,3},{2,0},{3,1},{4,6},{5,7},{6,4},{7,5},{8,10},{9,11},{10,... | collective-permute-start | bytes 344072 | tf_op jit(solution)/shard_map/ppermute | solution.py:340
  12.8 9.5 %collective-permute-start.7 = (bf16[16,3584]{1,0:T(8,128)(2,1)S(1)}, bf16[16,3584]{1,0:T(8,128)(2,1)S(1)}, u32[]{:S(2)}, u32[]{:S(2)}) collective-permute-start(bf16[16,3584]{1,0:T(8,128)(2,1)S(1)} %get-tuple-element.24), channel_id=1, source_target_pairs={{0,8},{1,9},{2,10},{3,11},{4,12},{5,13},{6,14},{7,15},{8,0},{9,1},... | collective-permute-start | bytes 344072 | tf_op jit(solution)/shard_map/ppermute | solution.py:340
  15.4 6.9 %collective-permute-start.8 = (bf16[16,3584]{1,0:T(8,128)(2,1)S(1)}, bf16[16,3584]{1,0:T(8,128)(2,1)S(1)}, u32[]{:S(2)}, u32[]{:S(2)}) collective-permute-start(bf16[16,3584]{1,0:T(8,128)(2,1)S(1)} %get-tuple-element.25), channel_id=1, source_target_pairs={{0,2},{1,3},{2,0},{3,1},{4,6},{5,7},{6,4},{7,5},{8,10},{9,11},{10,... | collective-permute-start | bytes 344072 | tf_op jit(solution)/shard_map/ppermute | solution.py:340
  16.9 9.1 %collective-permute-start.11 = (bf16[16,3584]{1,0:T(8,128)(2,1)S(1)}, bf16[16,3584]{1,0:T(8,128)(2,1)S(1)}, u32[]{:S(2)}, u32[]{:S(2)}) collective-permute-start(bf16[16,3584]{1,0:T(8,128)(2,1)S(1)} %get-tuple-element.27), channel_id=1, source_target_pairs={{0,2},{1,3},{2,0},{3,1},{4,6},{5,7},{6,4},{7,5},{8,10},{9,11},{10,... | collective-permute-start | bytes 344072 | tf_op jit(solution)/shard_map/ppermute | solution.py:340
  17.5 9.3 %collective-permute-start.10 = (bf16[16,3584]{1,0:T(8,128)(2,1)S(1)}, bf16[16,3584]{1,0:T(8,128)(2,1)S(1)}, u32[]{:S(2)}, u32[]{:S(2)}) collective-permute-start(bf16[16,3584]{1,0:T(8,128)(2,1)S(1)} %get-tuple-element.26), channel_id=1, source_target_pairs={{0,12},{1,13},{2,14},{3,15},{4,8},{5,9},{6,10},{7,11},{8,4},{9,5},... | collective-permute-start | bytes 344072 | tf_op jit(solution)/shard_map/ppermute | solution.py:340
  20.4 6.9 %collective-permute-start.13 = (bf16[16,3584]{1,0:T(8,128)(2,1)S(1)}, bf16[16,3584]{1,0:T(8,128)(2,1)S(1)}, u32[]{:S(2)}, u32[]{:S(2)}) collective-permute-start(bf16[16,3584]{1,0:T(8,128)(2,1)S(1)} %get-tuple-element.20.refs_4_), channel_id=1, source_target_pairs={{0,16},{16,0},{1,17},{17,1},{2,18},{18,2},{3,19},{19,3},{4,20},{20... | collective-permute-start | bytes 344072 | tf_op jit(solution)/shard_map/ppermute | solution.py:335
  22.3 6.4 %collective-permute-start.6 = (bf16[16,3584]{1,0:T(8,128)(2,1)S(1)}, bf16[16,3584]{1,0:T(8,128)(2,1)S(1)}, u32[]{:S(2)}, u32[]{:S(2)}) collective-permute-start(bf16[16,3584]{1,0:T(8,128)(2,1)S(1)} %collective-permute-done.5), channel_id=1, source_target_pairs={{0,4},{1,5},{2,6},{3,7},{4,0},{5,1},{6,2},{7,3},{8,12},{9,13},{10,... | collective-permute-start | bytes 344072 | tf_op jit(solution)/shard_map/ppermute | solution.py:340
  22.4 11.1 %collective-permute-start.9 = (bf16[16,3584]{1,0:T(8,128)(2,1)S(1)}, bf16[16,3584]{1,0:T(8,128)(2,1)S(1)}, u32[]{:S(2)}, u32[]{:S(2)}) collective-permute-start(bf16[16,3584]{1,0:T(8,128)(2,1)S(1)} %collective-permute-done.8), channel_id=1, source_target_pairs={{0,8},{1,9},{2,10},{3,11},{4,12},{5,13},{6,14},{7,15},{8,0},{9,1},... | collective-permute-start | bytes 344072 | tf_op jit(solution)/shard_map/ppermute | solution.py:340
  26.0 8.0 %collective-permute-start.12 = (bf16[16,3584]{1,0:T(8,128)(2,1)S(1)}, bf16[16,3584]{1,0:T(8,128)(2,1)S(1)}, u32[]{:S(2)}, u32[]{:S(2)}) collective-permute-start(bf16[16,3584]{1,0:T(8,128)(2,1)S(1)} %collective-permute-done.11), channel_id=1, source_target_pairs={{0,12},{1,13},{2,14},{3,15},{4,8},{5,9},{6,10},{7,11},{8,4},{9,5},... | collective-permute-start | bytes 344072 | tf_op jit(solution)/shard_map/ppermute | solution.py:340
  26.7 8.7 %collective-permute-start.14 = (bf16[16,3584]{1,0:T(8,128)(2,1)S(1)}, bf16[16,3584]{1,0:T(8,128)(2,1)S(1)}, u32[]{:S(2)}, u32[]{:S(2)}) collective-permute-start(bf16[16,3584]{1,0:T(8,128)(2,1)S(1)} %collective-permute-done.3.refs_5_), channel_id=1, source_target_pairs={{0,16},{16,0},{1,17},{17,1},{2,18},{18,2},{3,19},{19,3},{4,20},{20... | collective-permute-start | bytes 344072 | tf_op jit(solution)/shard_map/ppermute | solution.py:335
  27.3 8.7 %collective-permute-start.15 = (bf16[16,3584]{1,0:T(8,128)(2,1)S(1)}, bf16[16,3584]{1,0:T(8,128)(2,1)S(1)}, u32[]{:S(2)}, u32[]{:S(2)}) collective-permute-start(bf16[16,3584]{1,0:T(8,128)(2,1)S(1)} %collective-permute-done.4.refs_6_), channel_id=1, source_target_pairs={{0,16},{16,0},{1,17},{17,1},{2,18},{18,2},{3,19},{19,3},{4,20},{20... | collective-permute-start | bytes 344072 | tf_op jit(solution)/shard_map/ppermute | solution.py:335
  28.8 8.7 %collective-permute-start.17 = (bf16[16,3584]{1,0:T(8,128)(2,1)S(1)}, bf16[16,3584]{1,0:T(8,128)(2,1)S(1)}, u32[]{:S(2)}, u32[]{:S(2)}) collective-permute-start(bf16[16,3584]{1,0:T(8,128)(2,1)S(1)} %collective-permute-done.7.refs_8_), channel_id=1, source_target_pairs={{0,16},{16,0},{1,17},{17,1},{2,18},{18,2},{3,19},{19,3},{4,20},{20... | collective-permute-start | bytes 344072 | tf_op jit(solution)/shard_map/ppermute | solution.py:335
  33.4 6.1 %collective-permute-start.19 = (bf16[16,3584]{1,0:T(8,128)(2,1)S(1)}, bf16[16,3584]{1,0:T(8,128)(2,1)S(1)}, u32[]{:S(2)}, u32[]{:S(2)}) collective-permute-start(bf16[16,3584]{1,0:T(8,128)(2,1)S(1)} %collective-permute-done.10.refs_10_), channel_id=1, source_target_pairs={{0,16},{16,0},{1,17},{17,1},{2,18},{18,2},{3,19},{19,3},{4,20},{20... | collective-permute-start | bytes 344072 | tf_op jit(solution)/shard_map/ppermute | solution.py:335
  34.0 7.9 %collective-permute-start.16 = (bf16[16,3584]{1,0:T(8,128)(2,1)S(1)}, bf16[16,3584]{1,0:T(8,128)(2,1)S(1)}, u32[]{:S(2)}, u32[]{:S(2)}) collective-permute-start(bf16[16,3584]{1,0:T(8,128)(2,1)S(1)} %collective-permute-done.6.refs_7_), channel_id=1, source_target_pairs={{0,16},{16,0},{1,17},{17,1},{2,18},{18,2},{3,19},{19,3},{4,20},{20... | collective-permute-start | bytes 344072 | tf_op jit(solution)/shard_map/ppermute | solution.py:335
  35.4 7.7 %collective-permute-start.18 = (bf16[16,3584]{1,0:T(8,128)(2,1)S(1)}, bf16[16,3584]{1,0:T(8,128)(2,1)S(1)}, u32[]{:S(2)}, u32[]{:S(2)}) collective-permute-start(bf16[16,3584]{1,0:T(8,128)(2,1)S(1)} %collective-permute-done.9.refs_9_), channel_id=1, source_target_pairs={{0,16},{16,0},{1,17},{17,1},{2,18},{18,2},{3,19},{19,3},{4,20},{20... | collective-permute-start | bytes 344072 | tf_op jit(solution)/shard_map/ppermute | solution.py:335
  36.0 8.3 %collective-permute-start.20 = (bf16[16,3584]{1,0:T(8,128)(2,1)S(1)}, bf16[16,3584]{1,0:T(8,128)(2,1)S(1)}, u32[]{:S(2)}, u32[]{:S(2)}) collective-permute-start(bf16[16,3584]{1,0:T(8,128)(2,1)S(1)} %collective-permute-done.12.refs_11_), channel_id=1, source_target_pairs={{0,16},{16,0},{1,17},{17,1},{2,18},{18,2},{3,19},{19,3},{4,20},{20... | collective-permute-start | bytes 344072 | tf_op jit(solution)/shard_map/ppermute | solution.py:335
  44.3 2.0 %copy-start = (bf16[1,512,3584]{2,1,0:T(8,128)(2,1)S(1)}, bf16[1,512,3584]{2,1,0:T(8,128)(2,1)}, u32[]{:S(2)}) copy-start(bf16[1,512,3584]{2,1,0:T(8,128)(2,1)} %param.11) | copy-start | bytes 11010052
  46.4 19.6 %copy-start.3 = (f32[128,192]{0,1:T(8,128)S(1)}, f32[128,192]{0,1:T(8,128)}, u32[]{:S(2)}) copy-start(f32[128,192]{0,1:T(8,128)} %param.8) | copy-start | bytes 294916
  46.4 19.6 %copy-start.5 = (s32[128,8]{0,1:T(8,128)S(1)}, s32[128,8]{0,1:T(8,128)}, u32[]{:S(2)}) copy-start(s32[128,8]{0,1:T(8,128)} %param.9) | copy-start | bytes 12292
  50.1 12.2 %all-to-all-start = ((f32[32,1,128]{2,1,0:T(1,128)}), f32[32,1,128]{2,1,0:T(1,128)S(1)}, u32[]{:S(2)}, u32[]{:S(2)}) async-start(f32[32,1,128]{2,1,0:T(1,128)} %get-tuple-element.33), calls=%async_computation | async-start | bytes 32768 | tf_op jit(solution)/shard_map/all_to_all | solution.py:410
  62.3 43.1 %all-to-all-start.1 = ((bf16[16,224,128]{2,1,0:T(8,128)(2,1)}), bf16[16,224,128]{2,1,0:T(8,128)(2,1)S(1)}, u32[]{:S(2)}, u32[]{:S(2)}) async-start(bf16[16,224,128]{2,1,0:T(8,128)(2,1)} %bitcast.11), calls=%async_computation.1 | async-start | bytes 1835008 | tf_op jit(solution)/shard_map/all_to_all | solution.py:392
  66.3 21.5 %collective-permute-start.24 = (bf16[272,128]{1,0:T(8,128)(2,1)S(1)}, bf16[272,128]{1,0:T(8,128)(2,1)S(1)}, u32[]{:S(2)}, u32[]{:S(2)}) collective-permute-start(bf16[272,128]{1,0:T(8,128)(2,1)S(1)} %get-tuple-element.30), channel_id=1, source_target_pairs={{0,12},{1,13},{2,14},{3,15},{4,8},{5,9},{6,10},{7,11},{8,4},{9,5},... | collective-permute-start | bytes 208904 | tf_op jit(solution)/shard_map/ppermute | solution.py:340
  70.0 25.6 %collective-permute-start.23 = (bf16[272,128]{1,0:T(8,128)(2,1)S(1)}, bf16[272,128]{1,0:T(8,128)(2,1)S(1)}, u32[]{:S(2)}, u32[]{:S(2)}) collective-permute-start(bf16[272,128]{1,0:T(8,128)(2,1)S(1)} %get-tuple-element.30), channel_id=1, source_target_pairs={{0,8},{1,9},{2,10},{3,11},{4,12},{5,13},{6,14},{7,15},{8,0},{9,1},... | collective-permute-start | bytes 208904 | tf_op jit(solution)/shard_map/ppermute | solution.py:340
  70.0 25.6 %collective-permute-start.22 = (bf16[272,128]{1,0:T(8,128)(2,1)S(1)}, bf16[272,128]{1,0:T(8,128)(2,1)S(1)}, u32[]{:S(2)}, u32[]{:S(2)}) collective-permute-start(bf16[272,128]{1,0:T(8,128)(2,1)S(1)} %get-tuple-element.30), channel_id=1, source_target_pairs={{0,4},{1,5},{2,6},{3,7},{4,0},{5,1},{6,2},{7,3},{8,12},{9,13},{10,... | collective-permute-start | bytes 208904 | tf_op jit(solution)/shard_map/ppermute | solution.py:340
  95.6 8.3 %collective-permute-start.26 = (bf16[4,272,128]{2,1,0:T(8,128)(2,1)S(1)}, bf16[4,272,128]{2,1,0:T(8,128)(2,1)S(1)}, u32[]{:S(2)}, u32[]{:S(2)}) collective-permute-start(bf16[4,272,128]{2,1,0:T(8,128)(2,1)S(1)} %pad_maximum_fusion.refs_3_.refs_5_), channel_id=1, source_target_pairs={{0,2},{1,3},{2,0},{3,1},{4,6},{5,7},{6,4},{7,5},{8,10},{9,11},{10,... | collective-permute-start | bytes 835592 | tf_op jit(solution)/shard_map/ppermute | solution.py:340
  97.2 7.3 %collective-permute-start.25 = (bf16[4,272,128]{2,1,0:T(8,128)(2,1)S(1)}, bf16[4,272,128]{2,1,0:T(8,128)(2,1)S(1)}, u32[]{:S(2)}, u32[]{:S(2)}) collective-permute-start(bf16[4,272,128]{2,1,0:T(8,128)(2,1)S(1)} %pad_maximum_fusion.refs_3_.refs_5_), channel_id=1, source_target_pairs={{0,1},{1,0},{2,3},{3,2},{4,5},{5,4},{6,7},{7,6},{8,9},{9,8},{10,11... | collective-permute-start | bytes 835592 | tf_op jit(solution)/shard_map/ppermute | solution.py:340
  103.9 1.6 %collective-permute-start.27 = (bf16[4,272,128]{2,1,0:T(8,128)(2,1)S(1)}, bf16[4,272,128]{2,1,0:T(8,128)(2,1)S(1)}, u32[]{:S(2)}, u32[]{:S(2)}) collective-permute-start(bf16[4,272,128]{2,1,0:T(8,128)(2,1)S(1)} %collective-permute-done.26.refs_5_.refs_7_), channel_id=1, source_target_pairs={{0,1},{1,0},{2,3},{3,2},{4,5},{5,4},{6,7},{7,6},{8,9},{9,8},{10,11... | collective-permute-start | bytes 835592 | tf_op jit(solution)/shard_map/ppermute | solution.py:340
  103.9 5.9 %collective-permute-start.21 = (bf16[128,512]{1,0:T(8,128)(2,1)S(1)}, bf16[128,512]{1,0:T(8,128)(2,1)S(1)}, u32[]{:S(2)}, u32[]{:S(2)}) collective-permute-start(bf16[128,512]{1,0:T(8,128)(2,1)S(1)} %get-tuple-element.29), channel_id=1, source_target_pairs={{0,16},{16,0},{1,17},{17,1},{2,18},{18,2},{3,19},{19,3},{4,20},{20... | collective-permute-start | bytes 393224 | tf_op jit(solution)/shard_map/ppermute | solution.py:335
  108.1 4.1 %collective-permute-start.28 = (bf16[96,224]{1,0:T(8,128)(2,1)S(1)}, bf16[96,224]{1,0:T(8,128)(2,1)S(1)}, u32[]{:S(2)}, u32[]{:S(2)}) collective-permute-start(bf16[96,224]{1,0:T(8,128)(2,1)S(1)} %get-tuple-element.36), channel_id=1, source_target_pairs={{0,16},{16,0},{1,17},{17,1},{2,18},{18,2},{3,19},{19,3},{4,20},{20... | collective-permute-start | bytes 129032 | tf_op jit(solution)/shard_map/ppermute | solution.py:335

commit v2 on v1

--- a/solution.py
+++ b/solution.py
@@ -114,20 +114,21 @@
 
 NT = (((1,), (1,)), ((), ()))
 NN = (((1,), (0,)), ((), ()))
-VMEM_LIMIT = 48 * 1024 * 1024
-
-
-def kernel_call(body, out_shape, name, flops, touched, *operands, smem=0):
-    specs = [
-        pl.BlockSpec(memory_space=pltpu.SMEM if k < smem else pltpu.VMEM)
-        for k in range(len(operands))
-    ]
+
+
+def kernel_call(body, out_shape, name, flops, touched, *operands, far=(), scratch=(), room=24):
+    def space(k, operand):
+        if operand.shape == (2,):
+            return pltpu.SMEM
+        return pltpu.HBM if k in far else pltpu.VMEM
+
     return pl.pallas_call(
         body,
         out_shape=out_shape,
-        in_specs=specs,
+        in_specs=[pl.BlockSpec(memory_space=space(k, x)) for k, x in enumerate(operands)],
         out_specs=jax.tree.map(lambda _: pl.BlockSpec(memory_space=pltpu.VMEM), out_shape),
-        compiler_params=pltpu.CompilerParams(vmem_limit_bytes=VMEM_LIMIT),
+        scratch_shapes=scratch,
+        compiler_params=pltpu.CompilerParams(vmem_limit_bytes=room * 1024 * 1024),
         cost_estimate=pl.CostEstimate(flops=flops, bytes_accessed=touched, transcendentals=0),
         name=name,
     )(*operands)
@@ -153,7 +154,12 @@
     )
 
 
-def route_body(logits_ref, ids_ref, z_ref, a_ref, bundle_ref, *, flight):
+def first_body(place_ref, logits_ref, ids_ref, tokens_ref, saved_ref, *outs, flight, cap):
+    z_ref, a_ref, gate_ref, saved_own_ref, saved_other_ref, *parcels, turned_ref = outs
+    half = saved_own_ref.shape[1]
+    for k, out in enumerate((saved_own_ref, saved_other_ref)):
+        start = (place_ref[0] if k == 0 else 1 - place_ref[0]) * half
+        out[...] = saved_ref[:, pl.ds(pl.multiple_of(start, 128), half)]
     logits = logits_ref[...]
     ids = ids_ref[...]
     experts, tokens = logits.shape
@@ -184,20 +190,32 @@
     a_ref[...] = dense
     slot = jnp.where(picked > 0.0, ranks(picked), -1.0)
     high, middle, low = three_halves(gate_te)
-    bundle_ref[0:experts] = z.astype(jnp.bfloat16)
-    bundle_ref[experts : experts + 16] = jnp.concatenate(
-        [ids.astype(jnp.float32), slope], axis=0
-    ).astype(jnp.bfloat16)
-    bundle_ref[experts + 16 : experts + 32] = slot.astype(jnp.bfloat16)
-    bundle_ref[experts + 32 : experts + 48] = high
-    bundle_ref[experts + 48 : experts + 64] = middle
-    bundle_ref[experts + 64 : experts + 80] = low
+    lanes = iota((flight, tokens), 1)
+    slot_gates = jnp.zeros((flight, tokens), jnp.float32)
+    for c in range(cap):
+        here = jnp.sum(
+            jnp.where(slot == float(c), high.astype(jnp.float32), 0.0), axis=1, keepdims=True
+        )
+        slot_gates = jnp.where(lanes == c, here, slot_gates)
+    gate_ref[...] = slot_gates
+    pairs = jnp.concatenate([ids.astype(jnp.float32), slope], axis=0).astype(jnp.bfloat16)
+    parts = (z.astype(jnp.bfloat16), pairs, slot.astype(jnp.bfloat16), high, middle, low)
+    bundle = jnp.concatenate(parts, axis=0)
+    count = len(parcels)
+    block = tokens_ref.shape[1] // flight
+    turned_ref[...] = tokens_ref[...].T
+    for j, parcel in enumerate(parcels):
+        there = (place_ref[1] ^ j) & (count - 1)
+        for h in range(2):
+            start = pl.multiple_of((there + h * count) * block, 32)
+            parcel[h * block : (h + 1) * block] = turned_ref[pl.ds(start, block)]
+        parcel[2 * block : 2 * block + experts + 80] = bundle
 
 
 def pack_body(place_ref, ids_ref, ids_peer_ref, out_grad_ref, out_grad_peer_ref, *outs, cap):
     me = place_ref[1]
-    parts = []
-    for ids_one, grad_one in ((ids_ref, out_grad_ref), (ids_peer_ref, out_grad_peer_ref)):
+    selects = []
+    for ids_one in (ids_ref, ids_peer_ref):
         ids = ids_one[...]
         topk, tokens = ids.shape
         wanted = (iota((8, tokens), 0) * 2) ^ me
@@ -209,65 +227,59 @@
         select = jnp.concatenate(
             [jnp.where(slot[q : q + 1] == place, 1.0, 0.0) for q in range(8)], axis=0
         )
-        parts.append(
-            lax.dot_general(
-                select.astype(jnp.bfloat16), grad_one[...], NN, preferred_element_type=jnp.float32
-            )
-        )
+        selects.append(select.astype(jnp.bfloat16))
+    parts = [
+        lax.dot_general(select, grad_one[...], NN, preferred_element_type=jnp.float32)
+        for select, grad_one in zip(selects, (out_grad_ref, out_grad_peer_ref))
+    ]
     for q, out in enumerate(outs):
         rows = slice(q * cap, (q + 1) * cap)
         out[...] = jnp.concatenate([parts[0][rows], parts[1][rows]], axis=0).astype(jnp.bfloat16)
 
 
-def turn_body(tokens_ref, out_ref):
-    out_ref[...] = tokens_ref[...].T
-
-
 def swap_matrix(me, size, cap, dtype):
     return (iota((size, size), 1) == (iota((size, size), 0) ^ (me * cap))).astype(dtype)
 
 
-def grads_body(place_ref, saved_ref, saved_other_ref, weight_ref, *refs, cap):
-    pieces, (own_ref, other_ref, gate_ref) = refs[:16], refs[16:]
-    dp, me = place_ref[0], place_ref[1]
-    weight = weight_ref[...]
+def finish_grads(me, grads, saved_ref, grads_ref, cap):
     slots = saved_ref.shape[0]
     swap = swap_matrix(me, slots, cap, jnp.bfloat16)
     where_to = swap_matrix(me, slots, cap, jnp.float32)
-    lines = []
-    for half, saved_one in enumerate((saved_ref, saved_other_ref)):
-        rows = jnp.concatenate([p[...] for p in pieces[half * 8 : half * 8 + 8]], axis=0)
-        grads = lax.dot_general(rows, weight, NT, preferred_element_type=jnp.float32)
-        saved = lax.dot_general(swap, saved_one[...], NN, preferred_element_type=jnp.float32)
-        if half == 0:
-            own_ref[...] = grads
-        else:
-            other_ref[...] = grads.astype(jnp.bfloat16)
-        sums = jnp.sum(saved * grads, axis=1, keepdims=True)
-        lines.append(jnp.sum(where_to * sums, axis=0, keepdims=True))
-    count = gate_ref.shape[0] // 2
+    saved = lax.dot_general(swap, saved_ref[...], NN, preferred_element_type=jnp.float32)
+    grads_ref[...] = grads.astype(grads_ref.dtype)
+    sums = jnp.sum(saved * grads, axis=1, keepdims=True)
+    return jnp.sum(where_to * sums, axis=0, keepdims=True)
+
+
+def grads_own_body(place_ref, saved_ref, weight_ref, *refs, cap):
+    pieces, (grads_ref, line_ref) = refs[:8], refs[8:]
+    rows = jnp.concatenate([p[...] for p in pieces], axis=0)
+    grads = lax.dot_general(rows, weight_ref[...], NT, preferred_element_type=jnp.float32)
+    line_ref[...] = finish_grads(place_ref[1], grads, saved_ref, grads_ref, cap)
+
+
+def grads_other_body(place_ref, saved_ref, weight_ref, line_own_ref, gate_ref, *refs, cap):
+    pieces, (grads_ref, message_ref) = refs[:8], refs[8:]
+    rows = jnp.concatenate([p[...] for p in pieces], axis=0)
+    grads = lax.dot_general(rows, weight_ref[...], NT, preferred_element_type=jnp.float32)
+    other = finish_grads(place_ref[1], grads, saved_ref, grads_ref, cap)
+    own = line_own_ref[...]
+    dp = place_ref[0]
+    count = message_ref.shape[0] // 2
     for k in range(2):
-        line = jnp.where(dp == k, lines[0], lines[1])
-        gate_ref[k * count : (k + 1) * count] = jnp.broadcast_to(
-            line[None], (count, 1, line.shape[1])
-        )
-
-
-def hidden_body(place_ref, own_ref, other_ref, *refs, cap, experts):
-    bundles, out_ref = refs[:4], refs[4]
+        line = jnp.where(dp == k, own, other)
+        for e in range(count):
+            message_ref[k * count + e] = jnp.concatenate([line, gate_ref[e : e + 1]], axis=0)
+
+
+def hidden_body(place_ref, own_ref, other_ref, message_ref, out_ref, *, cap):
     dp, me = place_ref[0], place_ref[1]
     slots, half = own_ref.shape
-    tokens = bundles[0].shape[2]
-    mine = iota((16, tokens), 0) == me
-    place = iota((cap, tokens), 0).astype(jnp.float32)
+    diagonal = iota((cap, slots), 0) == iota((cap, slots), 1)
     columns = []
     for r in range(16):
-        bundle = bundles[r % 4]
-        slot = bundle[r // 4, experts + 16 : experts + 32].astype(jnp.float32)
-        gate = bundle[r // 4, experts + 32 : experts + 48].astype(jnp.float32)
-        slot = jnp.sum(jnp.where(mine, slot, 0.0), axis=0, keepdims=True)
-        gate = jnp.sum(jnp.where(mine, gate, 0.0), axis=0, keepdims=True)
-        columns.append(jnp.sum(jnp.where(slot == place, gate, 0.0), axis=1, keepdims=True))
+        line = message_ref[dp * 16 + (me ^ r), 1:2]
+        columns.append(jnp.sum(jnp.where(diagonal, line, 0.0), axis=1, keepdims=True))
     gates = jnp.concatenate(columns, axis=0)
     swap = swap_matrix(me, slots, cap, jnp.bfloat16)
     for k, part in enumerate((own_ref, other_ref)):
@@ -277,45 +289,47 @@
         out_ref[:, pl.ds(start, half)] = value.astype(jnp.bfloat16)
 
 
-def panel_body(place_ref, z_ref, a_ref, gate_ref, turned_ref, *refs, cap, experts):
-    bundles, (logit_ref, keep_ref, send_ref) = refs[:4], refs[4:7]
+def panel_body(place_ref, z_ref, a_ref, message_ref, *refs, cap):
+    parcels, logit_ref, outs = refs[:8], refs[8], refs[9:]
     dp, me = place_ref[0], place_ref[1]
-    tokens = z_ref.shape[1]
-    both = jnp.concatenate([gate_ref[k] for k in range(gate_ref.shape[0])], axis=0)
-    gate_abs = both[:16] + both[16:]
-    swap = swap_matrix(me, gate_abs.shape[1], cap, jnp.bfloat16)
+    experts, tokens = z_ref.shape
+    sources = len(parcels)
+    base = parcels[0].shape[0] - experts - 80
+    gate_all = jnp.concatenate(
+        [message_ref[e, 0:1] + message_ref[16 + e, 0:1] for e in range(16)], axis=0
+    )
+    upper = me >= sources
+    swap = swap_matrix(me, gate_all.shape[1], cap, jnp.bfloat16)
     gate_rel = sum(
         lax.dot_general(part, swap, NN, preferred_element_type=jnp.float32)
-        for part in three_halves(gate_abs)
+        for part in three_halves(gate_all)
     )
     rows = iota((experts, tokens), 0).astype(jnp.float32)
     lines, blocks = [], []
     total = None
-    for r in range(16):
-        bundle = bundles[r % 4]
-        slot = bundle[r // 4, experts + 16 : experts + 32].astype(jnp.float32)
+    for q, parcel_ref in enumerate(parcels):
+        at = base + experts
+        pairs = parcel_ref[at : at + 16].astype(jnp.float32)
+        slot = parcel_ref[at + 16 : at + 32].astype(jnp.float32)
         gate = sum(
-            bundle[r // 4, experts + 32 + 16 * k : experts + 48 + 16 * k].astype(jnp.float32)
+            parcel_ref[at + 32 + 16 * k : at + 48 + 16 * k].astype(jnp.float32)
             for k in (2, 1, 0)
         )
         grad = jnp.zeros((16, tokens), jnp.float32)
         for c in range(cap):
-            grad = jnp.where(slot == float(c), gate_rel[:, r * cap + c : r * cap + c + 1], grad)
+            grad = jnp.where(slot == float(c), gate_rel[:, q * cap + c : q * cap + c + 1], grad)
         mixed = jnp.sum(grad * gate, axis=0, keepdims=True) / RSCALE
         spread = jnp.concatenate(
             [grad - mixed, jnp.broadcast_to(-mixed, (experts - 16, tokens))], axis=0
         )
-        if r == 0:
-            line = z_ref[...] + a_ref[...] * spread
-            logit_ref[...] = line
-        else:
-            pairs = bundle[r // 4, experts : experts + 16].astype(jnp.float32)
-            dense = jnp.zeros((experts, tokens), jnp.float32)
-            for k in range(8):
-                dense = jnp.where(rows == pairs[k : k + 1], pairs[8 + k : 9 + k], dense)
-            line = bundle[r // 4, 0:experts].astype(jnp.float32) + dense * spread
+        if q == 0:
+            logit_ref[...] = z_ref[...] + a_ref[...] * spread
+        dense = jnp.zeros((experts, tokens), jnp.float32)
+        for k in range(8):
+            dense = jnp.where(rows == pairs[k : k + 1], pairs[8 + k : 9 + k], dense)
+        line = parcel_ref[base:at].astype(jnp.float32) + dense * spread
         lines.append(line.astype(jnp.bfloat16))
-        blocks.append(turned_ref[me ^ r])
+        blocks.append(parcel_ref[:base])
         if len(lines) == 2:
             part = lax.dot_general(
                 jnp.concatenate(lines, axis=1),
@@ -325,10 +339,14 @@
             )
             total = part if total is None else total + part
             lines, blocks = [], []
-    count = keep_ref.shape[0]
-    first, second = total[:count], total[count:]
-    keep_ref[...] = jnp.where(dp == 0, first, second)
-    send_ref[...] = jnp.where(dp == 0, second, first).astype(jnp.bfloat16)
+    columns, width = outs[0].shape
+    for k, out in enumerate(outs):
+        other_half, other_dp = k // 2, k % 2
+        from_upper = upper if other_half == 0 else jnp.logical_not(upper)
+        from_second = (dp == 1) if other_dp == 0 else (dp == 0)
+        low = jnp.where(from_second, total[columns:, :width], total[:columns, :width])
+        high = jnp.where(from_second, total[columns:, width:], total[:columns, width:])
+        out[...] = jnp.where(from_upper, high, low).astype(out.dtype)
 
 
 def over_dp(value):
@@ -338,6 +356,17 @@
 def over_expert(value, bits):
     count = lax.axis_size("expert")
     return lax.ppermute(value, "expert", [(k, k ^ bits) for k in range(count)])
+
+
+def over_both(value, dp_bit, bits):
+    count = lax.axis_size("expert")
+    return lax.ppermute(
+        value, ("dp", "expert"), [(k, k ^ (dp_bit * count + bits)) for k in range(2 * count)]
+    )
+
+
+def after(value, *earlier):
+    return lax.optimization_barrier((value, *earlier))[0]
 
 
 def paired_local(tokens_in, out_grad, router_logits, expert_ids, saved_hidden, down_weight):
@@ -345,8 +374,9 @@
     cap, hidden = saved_hidden.shape[3:]
     tokens, width = out_grad.shape
     experts = router_logits.shape[1]
-    half = hidden // 2
+    half, group = hidden // 2, flight // 2
     slots = flight * cap
+    block = width // flight
     f32, bf16 = jnp.float32, jnp.bfloat16
     dp, me = lax.axis_index("dp"), lax.axis_index("expert")
     place = jnp.stack([dp, me]).astype(jnp.int32)
@@ -354,78 +384,74 @@
     logits_t, ids_t = router_logits.T, expert_ids.T
     saved = saved_hidden.reshape(slots, hidden)
 
+    grad_peer = over_expert(out_grad, 1)
     ids_peer = over_expert(ids_t, 1)
-    grad_peer = over_expert(out_grad, 1)
-    saved_own = lax.dynamic_slice_in_dim(saved, dp * half, half, 1)
-    saved_other = over_dp(lax.dynamic_slice_in_dim(saved, (1 - dp) * half, half, 1))
-
-    bundle_rows = experts + 80
-    z, a, bundle = kernel_call(
-        lambda *refs: route_body(*refs, flight=flight),
-        (
-            jax.ShapeDtypeStruct((experts, tokens), f32),
-            jax.ShapeDtypeStruct((experts, tokens), f32),
-            jax.ShapeDtypeStruct((bundle_rows, tokens), bf16),
-        ),
-        "route", 1 << 22, 1 << 19, logits_t, ids_t,
-    )
     blocks = kernel_call(
         lambda *refs: pack_body(*refs, cap=cap),
         tuple(jax.ShapeDtypeStruct((2 * cap, width), bf16) for _ in range(8)),
         "pack", 4 * slots * tokens * width, 3 << 20,
-        place, ids_t, ids_peer, out_grad, grad_peer, smem=1,
-    )
-    own = [None] * 8
-    own[0] = blocks[0]
-    turn = [None] * 4
-    for rz in (3, 2, 1):
-        own[2 * rz] = over_expert(blocks[2 * rz], 4 * rz)
-        turn[rz] = over_expert(blocks[2 * rz + 1], 2)
-    own[1] = over_expert(blocks[1], 2)
-    for rz in (3, 2, 1):
-        own[2 * rz + 1] = over_expert(turn[rz], 4 * rz)
-    other = [over_dp(piece) for piece in own]
-
-    turned = kernel_call(
-        turn_body, jax.ShapeDtypeStruct((width, tokens), bf16), "turn", 1 << 20, 2 << 20, tokens_in
-    )
-    turned = lax.all_to_all(
-        turned.reshape(flight, width // flight, tokens), "expert", 0, 0, tiled=True
-    )
-
-    ring = jnp.stack([bundle] + [over_expert(bundle, 4 * rz) for rz in (1, 2, 3)])
-    ring_y = over_expert(ring, 2)
-    bundles = (ring, over_expert(ring, 1), ring_y, over_expert(ring_y, 1))
-
-    grads_own, grads_other, gate_part = kernel_call(
-        lambda *refs: grads_body(*refs, cap=cap),
+        place, ids_t, ids_peer, out_grad, grad_peer,
+    )
+    logits_t, tokens_in, saved = after((logits_t, tokens_in, saved), blocks[0])
+    z, a, slot_gates, saved_own, saved_other, *parcels = kernel_call(
+        lambda *refs: first_body(*refs, flight=flight, cap=cap),
         (
-            jax.ShapeDtypeStruct((slots, half), f32),
+            jax.ShapeDtypeStruct((experts, tokens), f32),
+            jax.ShapeDtypeStruct((experts, tokens), f32),
+            jax.ShapeDtypeStruct((flight, tokens), f32),
             jax.ShapeDtypeStruct((slots, half), bf16),
-            jax.ShapeDtypeStruct((2 * flight, 1, slots), f32),
+            jax.ShapeDtypeStruct((slots, half), bf16),
+            *(jax.ShapeDtypeStruct((2 * block + experts + 80, tokens), bf16) for _ in range(group)),
         ),
-        "grads", 4 * slots * width * half, 6 << 20,
-        place, saved_own, saved_other, weight, *own, *other, smem=1,
-    )
-    gate_all = lax.all_to_all(gate_part, ("dp", "expert"), 0, 0, tiled=True)
+        "first", 1 << 33, 3 << 20, place, logits_t, ids_t, tokens_in, saved,
+        scratch=[pltpu.VMEM((width, tokens), bf16)],
+    )
+    own, other = [blocks[0]] + [None] * 7, [None] * 8
+    sending = ((6, None), (1, None), (2, None), (7, 1), (3, 2), (4, 6), (5, 7))
+    for q, gate in sending:
+        piece = blocks[q] if gate is None else after(blocks[q], own[gate], slot_gates)
+        own[q] = over_expert(piece, 2 * q)
+    for q in range(8):
+        other[q] = over_dp(own[q])
+    saved_other = over_dp(saved_other)
+    parcels = [parcels[0]] + [
+        over_expert(after(parcels[j], own[4], own[7]), j) for j in range(1, group)
+    ]
+    grads_own, line_own = kernel_call(
+        lambda *refs: grads_own_body(*refs, cap=cap),
+        (jax.ShapeDtypeStruct((slots, half), f32), jax.ShapeDtypeStruct((1, slots), f32)),
+        "grads_own", 40 * slots * width * half, 5 << 20, place, saved_own, weight, *own,
+    )
+    grads_other, message = kernel_call(
+        lambda *refs: grads_other_body(*refs, cap=cap),
+        (
+            jax.ShapeDtypeStruct((slots, half), bf16),
+            jax.ShapeDtypeStruct((2 * flight, 2, slots), f32),
+        ),
+        "grads_other", 40 * slots * width * half, 5 << 20,
+        place, saved_other, weight, line_own, slot_gates, *other,
+    )
     grads_back = over_dp(grads_other)
+    message = lax.all_to_all(message, ("dp", "expert"), 0, 0, tiled=True)
+    message, grads_back = lax.optimization_barrier((message, grads_back))
+    logit_t, *sums = kernel_call(
+        lambda *refs: panel_body(*refs, cap=cap),
+        (
+            jax.ShapeDtypeStruct((experts, tokens), f32),
+            jax.ShapeDtypeStruct((experts // 2, block), f32),
+            *(jax.ShapeDtypeStruct((experts // 2, block), bf16) for _ in range(3)),
+        ),
+        "panel", 1 << 28, 4 << 20,
+        place, z, a, message, *parcels,
+    )
     hidden_grad = kernel_call(
-        lambda *refs: hidden_body(*refs, cap=cap, experts=experts),
+        lambda *refs: hidden_body(*refs, cap=cap),
         jax.ShapeDtypeStruct((slots, hidden), bf16),
         "hidden", 1 << 24, 1 << 20,
-        place, grads_own, grads_back, *bundles, smem=1,
-    )
-    logit_t, keep, send = kernel_call(
-        lambda *refs: panel_body(*refs, cap=cap, experts=experts),
-        (
-            jax.ShapeDtypeStruct((experts, tokens), f32),
-            jax.ShapeDtypeStruct((experts // 2, width // flight), f32),
-            jax.ShapeDtypeStruct((experts // 2, width // flight), bf16),
-        ),
-        "panel", 1 << 28, 4 << 20,
-        place, z, a, gate_all, turned, *bundles, smem=1,
-    )
-    router_t = keep + over_dp(send).astype(f32)
+        place, grads_own, grads_back, message,
+    )
+    far = [over_both(sums[3], 1, group), over_both(sums[2], 0, group), over_both(sums[1], 1, 0)]
+    router_t = after(sums[0], hidden_grad) + sum(part.astype(f32) for part in far)
     return (
         hidden_grad.reshape(1, 1, flight, cap, hidden),
         logit_t.T,

time: 113 us -> 75.9 us (0.67)
  waiting for transfers between devices: 53.3 us -> 10.2 us
  blocking collectives: 0 us -> 10.5 us
  starting transfers between devices: 42.4 us -> 38.4 us
    ppermute x18 -> x16, waiting for transfers between devices: 38.7 us -> 7.1 us  [over_expert(): return lax.ppermute(value, 'expert', [(k, k ^ bits) for k in range(count)])]
    all_to_all x0 -> x1, blocking collectives: none -> 10.5 us  [paired_local(): message = lax.all_to_all(message, ('dp', 'expert'), 0, 0, tiled=True)]
    all_to_all x2 -> x0, starting transfers between devices: 8.71 us -> none  [the longest x1 5.08 us: paired_local(): gate_all = lax.all_to_all(gate_part, ('dp', 'expert'), 0, 0, tiled=True)]
    ppermute x11 -> x10, waiting for transfers between devices: 8.72 us -> 1.09 us  [over_dp(): return lax.ppermute(value, 'dp', [(0, 1), (1, 0)])]
    all_to_all x2 -> x0, waiting for transfers between devices: 5.84 us -> none  [the longest x1 5.83 us: paired_local(): gate_all = lax.all_to_all(gate_part, ('dp', 'expert'), 0, 0, tiled=True)]
    ppermute x0 -> x3, starting transfers between devices: none -> 4.39 us  [over_both(): lax.ppermute(value, ('dp', 'expert'), [(k, k ^ dp_bit * count + bits) for...]
    ppermute x0 -> x3, waiting for transfers between devices: none -> 2 us  [over_both(): lax.ppermute(value, ('dp', 'expert'), [(k, k ^ dp_bit * count + bits) for...]
    unnamed x12, local copies, waits for them, and re-layouts: 3.92 us -> 5.08 us
  transfers between devices with their start and end apart: 31 -> 29, of which waited for: 14 -> 8; matrix products, arithmetic and copies ran while one was open for 1% -> 0% of each run, Pallas kernels for 6% -> 9%
where the time goes in v2:
time: 75.9 us; the launch traced here: 75.6 us
  starting transfers between devices  38.4 us (51%)
  blocking collectives  10.5 us (14%)
  waiting for transfers between devices  10.2 us (13%)
  Pallas kernels  10 us (13%)
  local copies, waits for them, and re-layouts  5.08 us (7%)
    ppermute x16, starting transfers between devices, over_expert(): return lax.ppermute(value, 'expert', [(k, k ^ bits) for k in range(count)])  22.7 us
    ppermute x10, starting transfers between devices, over_dp(): return lax.ppermute(value, 'dp', [(0, 1), (1, 0)])  11.3 us
    all_to_all x1, blocking collectives, paired_local(): message = lax.all_to_all(message, ('dp', 'expert'), 0, 0, tiled=True)  10.5 us
    pallas_call x6, Pallas kernels, kernel_call(): pl.pallas_call(body, out_shape=out_shape, in_specs=[pl.BlockSpec(memory_s...  10 us
    ppermute x16, waiting for transfers between devices, over_expert(): return lax.ppermute(value, 'expert', [(k, k ^ bits) for k in range(count)])  7.1 us
    unnamed x12, local copies, waits for them, and re-layouts  5.08 us
    ppermute x3, starting transfers between devices, over_both(): lax.ppermute(value, ('dp', 'expert'), [(k, k ^ dp_bit * count + bits) for...  4.39 us
    ppermute x3, waiting for transfers between devices, over_both(): lax.ppermute(value, ('dp', 'expert'), [(k, k ^ dp_bit * count + bits) for...  2 us
  transfers between devices with their start and end apart: 29, of which 8 were waited for; matrix products, arithmetic and copies ran while one was open for 0% of the time, Pallas kernels for 9%

profile of v2, /device:TPU:0, one launch (start us, length us, event | category | flops | bytes accessed | tf_op | source)
XLA Modules:
  0.0 75.6 jit_solution(12116718442469374264)
XLA Ops:
  0.6 0.5 collective-permute-start.1
  1.1 0.1 collective-permute-start
  1.2 0.1 pad_add_fusion.refs_0_
  1.3 2.2 %collective-permute-done.refs_2_ = s32[8,128]{1,0:T(8,128)S(1)} collective-permute-done((s32[8,128]{1,0:T(8,128)}, s32[8,128]{1,0:T(8,128)S(1)}, u32[]{:S(2)}, u32[]{:S(2)}) %collective-permute-start) | collective-permute-done | bytes 4128 | tf_op jit(solution)/shard_map/ppermute | solution.py:358
  3.5 0.0 collective-permute-done.1.refs_4_
  3.5 1.2 %copy-done = bf16[128,3584]{1,0:T(8,128)(2,1)S(1)} copy-done((bf16[128,3584]{1,0:T(8,128)(2,1)S(1)}, bf16[128,3584]{1,0:T(8,128)(2,1)}, u32[]{:S(2)}) %copy-start) | copy-done | bytes 917528
  4.6 0.7 copy-done.1
  5.3 1.0 %pack.1 = (bf16[16,3584]{1,0:T(8,128)(2,1)S(1)}, bf16[16,3584]{1,0:T(8,128)(2,1)S(1)}, bf16[16,3584]{1,0:T(8,128)(2,1)S(1)}, bf16[16,3584]{1,0:T(8,128)(2,1)S(1)...) custom-call(s32[2]{0:T(128)S(1)} %pad_add_fusion.refs_0_, ...), custom_call_target="tpu_custom_call" | custom-call | flops 234881024 | bytes 3145728 | tf_op jit(solution)/shard_map/pack/pallas_call | solution.py:125
  6.4 3.0 %collective-permute-start.2 = (bf16[16,3584]{1,0:T(8,128)(2,1)S(1)}, bf16[16,3584]{1,0:T(8,128)(2,1)S(1)}, u32[]{:S(2)}, u32[]{:S(2)}) collective-permute-start(bf16[16,3584]{1,0:T(8,128)(2,1)S(1)} %get-tuple-element.55), channel_id=1, source_target_pairs={{0,2},{1,3},{2,0},{3,1},{4,6},{5,7},{6,4},{7,5},{8,10},{9,11},{10,... | collective-permute-start | bytes 344072 | tf_op jit(solution)/shard_map/ppermute | solution.py:358
  9.3 3.6 %collective-permute-start.5 = (bf16[16,3584]{1,0:T(8,128)(2,1)S(1)}, bf16[16,3584]{1,0:T(8,128)(2,1)S(1)}, u32[]{:S(2)}, u32[]{:S(2)}) collective-permute-start(bf16[16,3584]{1,0:T(8,128)(2,1)S(1)} %get-tuple-element.61), channel_id=1, source_target_pairs={{0,12},{1,13},{2,14},{3,15},{4,8},{5,9},{6,10},{7,11},{8,4},{9,5},... | collective-permute-start | bytes 344072 | tf_op jit(solution)/shard_map/ppermute | solution.py:358
  12.9 0.0 collective-permute-start.3
  12.9 1.3 %copy-done.3 = bf16[128,3584]{1,0:T(8,128)(2,1)S(1)} copy-done((bf16[128,3584]{1,0:T(8,128)(2,1)S(1)}, bf16[128,3584]{1,0:T(8,128)(2,1)}, u32[]{:S(2)}) %copy-start.3) | copy-done | bytes 917528
  14.3 1.0 %copy-done.4 = bf16[1,1,16,8,1024]{4,3,2,1,0:T(8,128)(2,1)S(1)} copy-done((bf16[1,1,16,8,1024]{4,3,2,1,0:T(8,128)(2,1)S(1)}, bf16[1,1,16,8,1024]{4,3,2,1,0:T(8,128)(2,1)}, u32[]{:S(2)}) %copy-start.4) | copy-done | bytes 262168
  15.3 0.9 %copy-done.5 = f32[128,192]{0,1:T(8,128)S(1)} copy-done((f32[128,192]{0,1:T(8,128)S(1)}, f32[128,192]{0,1:T(8,128)}, u32[]{:S(2)}) %copy-start.5) | copy-done | bytes 98328
  16.2 1.2 %first.1 = (f32[192,128]{1,0:T(8,128)S(1)}, f32[192,128]{1,0:T(8,128)S(1)}, f32[16,128]{1,0:T(8,128)S(1)}, bf16[128,512]{1,0:T(8,128)(2,1)S(1)}, bf16[128,512]{1...) custom-call(s32[2]{0:T(128)S(1)} %pad_add_fusion.refs_0_, ...), custom_call_target="tpu_custom_call" | custom-call | flops 8589934592 | bytes 3145728 | tf_op jit(solution)/shard_map/first/pallas_call | solution.py:125
  17.4 0.0 collective-permute-done.2.refs_4_
  17.4 0.9 %collective-permute-start.7 = (bf16[16,3584]{1,0:T(8,128)(2,1)S(1)}, bf16[16,3584]{1,0:T(8,128)(2,1)S(1)}, u32[]{:S(2)}, u32[]{:S(2)}) collective-permute-start(bf16[16,3584]{1,0:T(8,128)(2,1)S(1)} %get-tuple-element.65), channel_id=1, source_target_pairs={{0,14},{1,15},{2,12},{3,13},{4,10},{5,11},{6,8},{7,9},{8,6},{9,7},... | collective-permute-start | bytes 344072 | tf_op jit(solution)/shard_map/ppermute | solution.py:358
  18.3 1.6 %collective-permute-start.10 = (bf16[16,3584]{1,0:T(8,128)(2,1)S(1)}, bf16[16,3584]{1,0:T(8,128)(2,1)S(1)}, u32[]{:S(2)}, u32[]{:S(2)}) collective-permute-start(bf16[16,3584]{1,0:T(8,128)(2,1)S(1)} %get-tuple-element.50.refs_3_), channel_id=1, source_target_pairs={{0,16},{16,0},{1,17},{17,1},{2,18},{18,2},{3,19},{19,3},{4,20},{20... | collective-permute-start | bytes 344072 | tf_op jit(solution)/shard_map/ppermute | solution.py:353
  19.9 0.0 collective-permute-done.5.refs_9_
  19.9 2.3 %collective-permute-start.6 = (bf16[16,3584]{1,0:T(8,128)(2,1)S(1)}, bf16[16,3584]{1,0:T(8,128)(2,1)S(1)}, u32[]{:S(2)}, u32[]{:S(2)}) collective-permute-start(bf16[16,3584]{1,0:T(8,128)(2,1)S(1)} %get-tuple-element.62), channel_id=1, source_target_pairs={{0,8},{1,9},{2,10},{3,11},{4,12},{5,13},{6,14},{7,15},{8,0},{9,1},... | collective-permute-start | bytes 344072 | tf_op jit(solution)/shard_map/ppermute | solution.py:358
  22.2 0.5 collective-permute-start.9
  22.7 0.0 collective-permute-done.3.refs_5_
  22.7 2.1 %collective-permute-start.4 = (bf16[16,3584]{1,0:T(8,128)(2,1)S(1)}, bf16[16,3584]{1,0:T(8,128)(2,1)S(1)}, u32[]{:S(2)}, u32[]{:S(2)}) collective-permute-start(bf16[16,3584]{1,0:T(8,128)(2,1)S(1)} %get-tuple-element.59), channel_id=1, source_target_pairs={{0,6},{1,7},{2,4},{3,5},{4,2},{5,3},{6,0},{7,1},{8,14},{9,15},{10,... | collective-permute-start | bytes 344072 | tf_op jit(solution)/shard_map/ppermute | solution.py:358
  24.8 1.5 %collective-permute-done.7.refs_10_ = bf16[16,3584]{1,0:T(8,128)(2,1)S(1)} collective-permute-done((bf16[16,3584]{1,0:T(8,128)(2,1)S(1)}, bf16[16,3584]{1,0:T(8,128)(2,1)S(1)}, u32[]{:S(2)}, u32[]{:S(2)}) %collective-permute-start.7) | collective-permute-done | bytes 114720 | tf_op jit(solution)/shard_map/ppermute | solution.py:358
  26.3 1.5 %collective-permute-start.11 = (bf16[16,3584]{1,0:T(8,128)(2,1)S(1)}, bf16[16,3584]{1,0:T(8,128)(2,1)S(1)}, u32[]{:S(2)}, u32[]{:S(2)}) collective-permute-start(bf16[16,3584]{1,0:T(8,128)(2,1)S(1)} %collective-permute-done.2.refs_4_), channel_id=1, source_target_pairs={{0,16},{16,0},{1,17},{17,1},{2,18},{18,2},{3,19},{19,3},{4,20},{20... | collective-permute-start | bytes 344072 | tf_op jit(solution)/shard_map/ppermute | solution.py:353
  27.7 0.0 collective-permute-done.10.refs_5_
  27.7 0.5 collective-permute-start.12
  28.3 2.2 %collective-permute-done.6.refs_7_ = bf16[16,3584]{1,0:T(8,128)(2,1)S(1)} collective-permute-done((bf16[16,3584]{1,0:T(8,128)(2,1)S(1)}, bf16[16,3584]{1,0:T(8,128)(2,1)S(1)}, u32[]{:S(2)}, u32[]{:S(2)}) %collective-permute-start.6) | collective-permute-done | bytes 114720 | tf_op jit(solution)/shard_map/ppermute | solution.py:358
  30.5 1.3 %collective-permute-start.8 = (bf16[16,3584]{1,0:T(8,128)(2,1)S(1)}, bf16[16,3584]{1,0:T(8,128)(2,1)S(1)}, u32[]{:S(2)}, u32[]{:S(2)}) collective-permute-start(bf16[16,3584]{1,0:T(8,128)(2,1)S(1)} %get-tuple-element.66), channel_id=1, source_target_pairs={{0,10},{1,11},{2,8},{3,9},{4,14},{5,15},{6,12},{7,13},{8,2},{9,3},... | collective-permute-start | bytes 344072 | tf_op jit(solution)/shard_map/ppermute | solution.py:358
  31.8 0.0 collective-permute-done.9.refs_1_
  31.8 2.0 %collective-permute-start.16 = (bf16[16,3584]{1,0:T(8,128)(2,1)S(1)}, bf16[16,3584]{1,0:T(8,128)(2,1)S(1)}, u32[]{:S(2)}, u32[]{:S(2)}) collective-permute-start(bf16[16,3584]{1,0:T(8,128)(2,1)S(1)} %collective-permute-done.5.refs_9_), channel_id=1, source_target_pairs={{0,16},{16,0},{1,17},{17,1},{2,18},{18,2},{3,19},{19,3},{4,20},{20... | collective-permute-start | bytes 344072 | tf_op jit(solution)/shard_map/ppermute | solution.py:353
  33.8 0.0 collective-permute-done.4.refs_6_
  33.8 0.1 collective-permute-start.17
  33.8 0.0 collective-permute-done.11.refs_6_
  33.9 2.0 %collective-permute-start.14 = (bf16[16,3584]{1,0:T(8,128)(2,1)S(1)}, bf16[16,3584]{1,0:T(8,128)(2,1)S(1)}, u32[]{:S(2)}, u32[]{:S(2)}) collective-permute-start(bf16[16,3584]{1,0:T(8,128)(2,1)S(1)} %collective-permute-done.6.refs_7_), channel_id=1, source_target_pairs={{0,16},{16,0},{1,17},{17,1},{2,18},{18,2},{3,19},{19,3},{4,20},{20... | collective-permute-start | bytes 344072 | tf_op jit(solution)/shard_map/ppermute | solution.py:353
  35.8 0.1 collective-permute-start.13
  35.9 1.2 %collective-permute-done.8.refs_8_ = bf16[16,3584]{1,0:T(8,128)(2,1)S(1)} collective-permute-done((bf16[16,3584]{1,0:T(8,128)(2,1)S(1)}, bf16[16,3584]{1,0:T(8,128)(2,1)S(1)}, u32[]{:S(2)}, u32[]{:S(2)}) %collective-permute-start.8) | collective-permute-done | bytes 114720 | tf_op jit(solution)/shard_map/ppermute | solution.py:358
  37.1 1.5 %collective-permute-start.15 = (bf16[16,3584]{1,0:T(8,128)(2,1)S(1)}, bf16[16,3584]{1,0:T(8,128)(2,1)S(1)}, u32[]{:S(2)}, u32[]{:S(2)}) collective-permute-start(bf16[16,3584]{1,0:T(8,128)(2,1)S(1)} %collective-permute-done.8.refs_8_), channel_id=1, source_target_pairs={{0,16},{16,0},{1,17},{17,1},{2,18},{18,2},{3,19},{19,3},{4,20},{20... | collective-permute-start | bytes 344072 | tf_op jit(solution)/shard_map/ppermute | solution.py:353
  38.6 2.0 %grads_own.1 = (f32[128,512]{1,0:T(8,128)S(1)}, f32[1,128]{1,0:T(1,128)S(1)}) custom-call(s32[2]{0:T(128)S(1)} %pad_add_fusion.refs_0_, bf16[128,512]{1,0:T(8,128)(2,1)S(1)} %get-tuple-element.54.refs_1_, bf16[512,3584]{1,0:T(8,128)(2,1)S(1)} %bitcast.13, bf16[16,3584]{1,0:T(8,128)(2,1)S(1)} %get-tuple-element.50.refs_3_, ...), custom_call_target="tpu_custom_call" | custom-call | flops 9395240960 | bytes 5242880 | tf_op jit(solution)/shard_map/grads_own/pallas_call | solution.py:125
  40.6 0.1 collective-permute-start.25
  40.6 0.0 collective-permute-done.17.refs_12_
  40.7 3.2 %collective-permute-start.24 = (bf16[720,128]{1,0:T(8,128)(2,1)S(1)}, bf16[720,128]{1,0:T(8,128)(2,1)S(1)}, u32[]{:S(2)}, u32[]{:S(2)}) collective-permute-start(bf16[720,128]{1,0:T(8,128)(2,1)S(1)} %get-tuple-element.88), channel_id=1, source_target_pairs={{0,6},{1,7},{2,4},{3,5},{4,2},{5,3},{6,0},{7,1},{8,14},{9,15},{10,... | collective-permute-start | bytes 552968 | tf_op jit(solution)/shard_map/ppermute | solution.py:358
  43.8 0.0 collective-permute-done.13.refs_8_
  43.8 1.1 %collective-permute-done.15.refs_10_ = bf16[16,3584]{1,0:T(8,128)(2,1)S(1)} collective-permute-done((bf16[16,3584]{1,0:T(8,128)(2,1)S(1)}, bf16[16,3584]{1,0:T(8,128)(2,1)S(1)}, u32[]{:S(2)}, u32[]{:S(2)}) %collective-permute-start.15) | collective-permute-done | bytes 114720 | tf_op jit(solution)/shard_map/ppermute | solution.py:353
  44.9 2.0 %grads_other.1 = (bf16[128,512]{1,0:T(8,128)(2,1)S(1)}, f32[32,2,128]{2,1,0:T(2,128)S(1)}) custom-call(s32[2]{0:T(128)S(1)} %pad_add_fusion.refs_0_, bf16[128,512]{1,0:T(8,128)(2,1)S(1)} %collective-permute-done.9.refs_1_, bf16[512,3584]{1,0:T(8,128)(2,1)S(1)} %bitcast.14, f32[1,128]{1,0:T(1,128)S(1)} %get-tuple-element.69.refs_3_, ...), custom_call_target="tpu_custom_call" | custom-call | flops 9395240960 | bytes 5242880 | tf_op jit(solution)/shard_map/grads_other/pallas_call | solution.py:125
  46.9 1.6 %collective-permute-start.18 = (bf16[128,512]{1,0:T(8,128)(2,1)S(1)}, bf16[128,512]{1,0:T(8,128)(2,1)S(1)}, u32[]{:S(2)}, u32[]{:S(2)}) collective-permute-start(bf16[128,512]{1,0:T(8,128)(2,1)S(1)} %get-tuple-element.71), channel_id=1, source_target_pairs={{0,16},{16,0},{1,17},{17,1},{2,18},{18,2},{3,19},{19,3},{4,20},{20... | collective-permute-start | bytes 393224 | tf_op jit(solution)/shard_map/ppermute | solution.py:353
  48.5 0.9 %collective-permute-start.23 = (bf16[720,128]{1,0:T(8,128)(2,1)S(1)}, bf16[720,128]{1,0:T(8,128)(2,1)S(1)}, u32[]{:S(2)}, u32[]{:S(2)}) collective-permute-start(bf16[720,128]{1,0:T(8,128)(2,1)S(1)} %get-tuple-element.86), channel_id=1, source_target_pairs={{0,5},{1,4},{2,7},{3,6},{4,1},{5,0},{6,3},{7,2},{8,13},{9,12},{10,... | collective-permute-start | bytes 552968 | tf_op jit(solution)/shard_map/ppermute | solution.py:358
  49.3 3.0 %collective-permute-start.22 = (bf16[720,128]{1,0:T(8,128)(2,1)S(1)}, bf16[720,128]{1,0:T(8,128)(2,1)S(1)}, u32[]{:S(2)}, u32[]{:S(2)}) collective-permute-start(bf16[720,128]{1,0:T(8,128)(2,1)S(1)} %get-tuple-element.84), channel_id=1, source_target_pairs={{0,4},{1,5},{2,6},{3,7},{4,0},{5,1},{6,2},{7,3},{8,12},{9,13},{10,... | collective-permute-start | bytes 552968 | tf_op jit(solution)/shard_map/ppermute | solution.py:358
  52.3 0.7 collective-permute-start.21
  53.1 0.0 collective-permute-done.24.refs_10_
  53.1 1.0 %collective-permute-start.20 = (bf16[720,128]{1,0:T(8,128)(2,1)S(1)}, bf16[720,128]{1,0:T(8,128)(2,1)S(1)}, u32[]{:S(2)}, u32[]{:S(2)}) collective-permute-start(bf16[720,128]{1,0:T(8,128)(2,1)S(1)} %get-tuple-element.80), channel_id=1, source_target_pairs={{0,2},{1,3},{2,0},{3,1},{4,6},{5,7},{6,4},{7,5},{8,10},{9,11},{10,... | collective-permute-start | bytes 552968 | tf_op jit(solution)/shard_map/ppermute | solution.py:358
  54.0 0.0 collective-permute-done.18.refs_2_
  54.0 0.2 collective-permute-start.19
  54.2 10.5 %all_to_all.5.refs_3_ = f32[32,2,128]{2,1,0:T(2,128)S(1)} all-to-all(f32[32,2,128]{2,1,0:T(2,128)S(1)} %get-tuple-element.70), channel_id=1, replica_groups=mesh['dp'=2,'expert'=16] {'dp','expert'}, dimensions={0} | all-to-all | bytes 65536 | tf_op jit(solution)/shard_map/all_to_all | solution.py:435
  64.7 0.0 collective-permute-done.20.refs_6_
  64.7 2.2 %panel.1 = (f32[192,128]{1,0:T(8,128)}, f32[96,224]{1,0:T(8,128)S(1)}, bf16[96,224]{1,0:T(8,128)(2,1)S(1)}, bf16[96,224]{1,0:T(8,128)(2,1)S(1)}, bf16[96,224]{1,0:T(8,128)(2,1)S(1)}) custom-call(s32[2]{0:T(128)S(1)} %pad_add_fusion.refs_0_, f32[192,128]{1,0:T(8,128)S(1)} %get-tuple-element.74.refs_1_, f32[192,128]{1,0:T(8,128)S(1)} %get-tuple-element.75.refs_2_, ...), custom_call_target="tpu_custom_call" | custom-call | flops 268435456 | bytes 4194304 | tf_op jit(solution)/shard_map/panel/pallas_call | solution.py:125
  67.0 0.6 collective-permute-start.26
  67.6 2.3 %collective-permute-start.27 = (bf16[96,224]{1,0:T(8,128)(2,1)S(1)}, bf16[96,224]{1,0:T(8,128)(2,1)S(1)}, u32[]{:S(2)}, u32[]{:S(2)}) collective-permute-start(bf16[96,224]{1,0:T(8,128)(2,1)S(1)} %get-tuple-element.95), channel_id=1, source_target_pairs={{0,8},{1,9},{2,10},{3,11},{4,12},{5,13},{6,14},{7,15},{8,0},{9,1},... | collective-permute-start | bytes 129032 | tf_op jit(solution)/shard_map/ppermute | solution.py:363
  69.9 1.4 %collective-permute-start.28 = (bf16[96,224]{1,0:T(8,128)(2,1)S(1)}, bf16[96,224]{1,0:T(8,128)(2,1)S(1)}, u32[]{:S(2)}, u32[]{:S(2)}) collective-permute-start(bf16[96,224]{1,0:T(8,128)(2,1)S(1)} %get-tuple-element.96), channel_id=1, source_target_pairs={{0,16},{1,17},{2,18},{3,19},{4,20},{5,21},{6,22},{7,23},{8,24},{9,... | collective-permute-start | bytes 129032 | tf_op jit(solution)/shard_map/ppermute | solution.py:363
  71.3 1.6 %hidden.1 = bf16[128,1024]{1,0:T(8,128)(2,1)} custom-call(s32[2]{0:T(128)S(1)} %pad_add_fusion.refs_0_, f32[128,512]{1,0:T(8,128)S(1)} %get-tuple-element.67.refs_1_, bf16[128,512]{1,0:T(8,128)(2,1)S(1)} %collective-permute-done.18.refs_2_, f32[32,2,128]{2,1,0:T(2,128)S(1)} %all_to_all.5.refs_3_), custom_call_target="tpu_custom_call" | custom-call | flops 16777216 | bytes 1048576 | tf_op jit(solution)/shard_map/hidden/pallas_call | solution.py:125
  73.0 1.6 %collective-permute-done.26 = bf16[96,224]{1,0:T(8,128)(2,1)S(1)} collective-permute-done((bf16[96,224]{1,0:T(8,128)(2,1)S(1)}, bf16[96,224]{1,0:T(8,128)(2,1)S(1)}, u32[]{:S(2)}, u32[]{:S(2)}) %collective-permute-start.26) | collective-permute-done | bytes 43040 | tf_op jit(solution)/shard_map/ppermute | solution.py:363
  74.6 0.1 collective-permute-done.27
  74.7 0.3 collective-permute-done.28
  75.0 0.7 add_bitcast_fusion
  (15 shorter events, 0.0 us)
Async XLA Ops:
  0.6 2.8 %collective-permute-start.1 = (bf16[128,3584]{1,0:T(8,128)(2,1)}, bf16[128,3584]{1,0:T(8,128)(2,1)S(1)}, u32[]{:S(2)}, u32[]{:S(2)}) collective-permute-start(bf16[128,3584]{1,0:T(8,128)(2,1)} %refs_3_.1), channel_id=1, source_target_pairs={{0,1},{1,0},{2,3},{3,2},{4,5},{5,4},{6,7},{7,6},{8,9},{9,8},{10,11... | collective-permute-start | bytes 2752520 | tf_op jit(solution)/shard_map/ppermute | solution.py:358
  1.1 2.3 %collective-permute-start = (s32[8,128]{1,0:T(8,128)}, s32[8,128]{1,0:T(8,128)S(1)}, u32[]{:S(2)}, u32[]{:S(2)}) collective-permute-start(s32[8,128]{1,0:T(8,128)} %bitcast.10), channel_id=1, source_target_pairs={{0,1},{1,0},{2,3},{3,2},{4,5},{5,4},{6,7},{7,6},{8,9},{9,8},{10,11... | collective-permute-start | bytes 12296 | tf_op jit(solution)/shard_map/ppermute | solution.py:358
  3.5 1.2 %copy-start = (bf16[128,3584]{1,0:T(8,128)(2,1)S(1)}, bf16[128,3584]{1,0:T(8,128)(2,1)}, u32[]{:S(2)}) copy-start(bf16[128,3584]{1,0:T(8,128)(2,1)} %refs_3_.1) | copy-start | bytes 2752516
  4.6 0.7 copy-start.1
  6.4 11.0 %collective-permute-start.2 = (bf16[16,3584]{1,0:T(8,128)(2,1)S(1)}, bf16[16,3584]{1,0:T(8,128)(2,1)S(1)}, u32[]{:S(2)}, u32[]{:S(2)}) collective-permute-start(bf16[16,3584]{1,0:T(8,128)(2,1)S(1)} %get-tuple-element.55), channel_id=1, source_target_pairs={{0,2},{1,3},{2,0},{3,1},{4,6},{5,7},{6,4},{7,5},{8,10},{9,11},{10,... | collective-permute-start | bytes 344072 | tf_op jit(solution)/shard_map/ppermute | solution.py:358
  9.3 10.6 %collective-permute-start.5 = (bf16[16,3584]{1,0:T(8,128)(2,1)S(1)}, bf16[16,3584]{1,0:T(8,128)(2,1)S(1)}, u32[]{:S(2)}, u32[]{:S(2)}) collective-permute-start(bf16[16,3584]{1,0:T(8,128)(2,1)S(1)} %get-tuple-element.61), channel_id=1, source_target_pairs={{0,12},{1,13},{2,14},{3,15},{4,8},{5,9},{6,10},{7,11},{8,4},{9,5},... | collective-permute-start | bytes 344072 | tf_op jit(solution)/shard_map/ppermute | solution.py:358
  12.9 25.6 %copy-start.2 = (bf16[1,512,3584]{2,1,0:T(8,128)(2,1)S(1)}, bf16[1,512,3584]{2,1,0:T(8,128)(2,1)}, u32[]{:S(2)}) copy-start(bf16[1,512,3584]{2,1,0:T(8,128)(2,1)} %param.11) | copy-start | bytes 11010052
  12.9 9.8 %collective-permute-start.3 = (bf16[16,3584]{1,0:T(8,128)(2,1)S(1)}, bf16[16,3584]{1,0:T(8,128)(2,1)S(1)}, u32[]{:S(2)}, u32[]{:S(2)}) collective-permute-start(bf16[16,3584]{1,0:T(8,128)(2,1)S(1)} %get-tuple-element.56), channel_id=1, source_target_pairs={{0,4},{1,5},{2,6},{3,7},{4,0},{5,1},{6,2},{7,3},{8,12},{9,13},{10,... | collective-permute-start | bytes 344072 | tf_op jit(solution)/shard_map/ppermute | solution.py:358
  12.9 1.3 %copy-start.3 = (bf16[128,3584]{1,0:T(8,128)(2,1)S(1)}, bf16[128,3584]{1,0:T(8,128)(2,1)}, u32[]{:S(2)}) copy-start(bf16[128,3584]{1,0:T(8,128)(2,1)} %refs_3_.2) | copy-start | bytes 2752516
  14.3 1.0 %copy-start.4 = (bf16[1,1,16,8,1024]{4,3,2,1,0:T(8,128)(2,1)S(1)}, bf16[1,1,16,8,1024]{4,3,2,1,0:T(8,128)(2,1)}, u32[]{:S(2)}) copy-start(bf16[1,1,16,8,1024]{4,3,2,1,0:T(8,128)(2,1)} %param.10) | copy-start | bytes 786436
  15.3 0.9 %copy-start.5 = (f32[128,192]{0,1:T(8,128)S(1)}, f32[128,192]{0,1:T(8,128)}, u32[]{:S(2)}) copy-start(f32[128,192]{0,1:T(8,128)} %param.8) | copy-start | bytes 294916
  17.4 8.8 %collective-permute-start.7 = (bf16[16,3584]{1,0:T(8,128)(2,1)S(1)}, bf16[16,3584]{1,0:T(8,128)(2,1)S(1)}, u32[]{:S(2)}, u32[]{:S(2)}) collective-permute-start(bf16[16,3584]{1,0:T(8,128)(2,1)S(1)} %get-tuple-element.65), channel_id=1, source_target_pairs={{0,14},{1,15},{2,12},{3,13},{4,10},{5,11},{6,8},{7,9},{8,6},{9,7},... | collective-permute-start | bytes 344072 | tf_op jit(solution)/shard_map/ppermute | solution.py:358
  18.3 9.4 %collective-permute-start.10 = (bf16[16,3584]{1,0:T(8,128)(2,1)S(1)}, bf16[16,3584]{1,0:T(8,128)(2,1)S(1)}, u32[]{:S(2)}, u32[]{:S(2)}) collective-permute-start(bf16[16,3584]{1,0:T(8,128)(2,1)S(1)} %get-tuple-element.50.refs_3_), channel_id=1, source_target_pairs={{0,16},{16,0},{1,17},{17,1},{2,18},{18,2},{3,19},{19,3},{4,20},{20... | collective-permute-start | bytes 344072 | tf_op jit(solution)/shard_map/ppermute | solution.py:353
  19.9 10.6 %collective-permute-start.6 = (bf16[16,3584]{1,0:T(8,128)(2,1)S(1)}, bf16[16,3584]{1,0:T(8,128)(2,1)S(1)}, u32[]{:S(2)}, u32[]{:S(2)}) collective-permute-start(bf16[16,3584]{1,0:T(8,128)(2,1)S(1)} %get-tuple-element.62), channel_id=1, source_target_pairs={{0,8},{1,9},{2,10},{3,11},{4,12},{5,13},{6,14},{7,15},{8,0},{9,1},... | collective-permute-start | bytes 344072 | tf_op jit(solution)/shard_map/ppermute | solution.py:358
  22.2 9.6 %collective-permute-start.9 = (bf16[128,512]{1,0:T(8,128)(2,1)S(1)}, bf16[128,512]{1,0:T(8,128)(2,1)S(1)}, u32[]{:S(2)}, u32[]{:S(2)}) collective-permute-start(bf16[128,512]{1,0:T(8,128)(2,1)S(1)} %get-tuple-element.68), channel_id=1, source_target_pairs={{0,16},{16,0},{1,17},{17,1},{2,18},{18,2},{3,19},{19,3},{4,20},{20... | collective-permute-start | bytes 393224 | tf_op jit(solution)/shard_map/ppermute | solution.py:353
  22.7 11.0 %collective-permute-start.4 = (bf16[16,3584]{1,0:T(8,128)(2,1)S(1)}, bf16[16,3584]{1,0:T(8,128)(2,1)S(1)}, u32[]{:S(2)}, u32[]{:S(2)}) collective-permute-start(bf16[16,3584]{1,0:T(8,128)(2,1)S(1)} %get-tuple-element.59), channel_id=1, source_target_pairs={{0,6},{1,7},{2,4},{3,5},{4,2},{5,3},{6,0},{7,1},{8,14},{9,15},{10,... | collective-permute-start | bytes 344072 | tf_op jit(solution)/shard_map/ppermute | solution.py:358
  26.3 7.6 %collective-permute-start.11 = (bf16[16,3584]{1,0:T(8,128)(2,1)S(1)}, bf16[16,3584]{1,0:T(8,128)(2,1)S(1)}, u32[]{:S(2)}, u32[]{:S(2)}) collective-permute-start(bf16[16,3584]{1,0:T(8,128)(2,1)S(1)} %collective-permute-done.2.refs_4_), channel_id=1, source_target_pairs={{0,16},{16,0},{1,17},{17,1},{2,18},{18,2},{3,19},{19,3},{4,20},{20... | collective-permute-start | bytes 344072 | tf_op jit(solution)/shard_map/ppermute | solution.py:353
  27.7 8.1 %collective-permute-start.12 = (bf16[16,3584]{1,0:T(8,128)(2,1)S(1)}, bf16[16,3584]{1,0:T(8,128)(2,1)S(1)}, u32[]{:S(2)}, u32[]{:S(2)}) collective-permute-start(bf16[16,3584]{1,0:T(8,128)(2,1)S(1)} %collective-permute-done.3.refs_5_), channel_id=1, source_target_pairs={{0,16},{16,0},{1,17},{17,1},{2,18},{18,2},{3,19},{19,3},{4,20},{20... | collective-permute-start | bytes 344072 | tf_op jit(solution)/shard_map/ppermute | solution.py:353
  30.5 6.6 %collective-permute-start.8 = (bf16[16,3584]{1,0:T(8,128)(2,1)S(1)}, bf16[16,3584]{1,0:T(8,128)(2,1)S(1)}, u32[]{:S(2)}, u32[]{:S(2)}) collective-permute-start(bf16[16,3584]{1,0:T(8,128)(2,1)S(1)} %get-tuple-element.66), channel_id=1, source_target_pairs={{0,10},{1,11},{2,8},{3,9},{4,14},{5,15},{6,12},{7,13},{8,2},{9,3},... | collective-permute-start | bytes 344072 | tf_op jit(solution)/shard_map/ppermute | solution.py:358
  31.8 8.7 %collective-permute-start.16 = (bf16[16,3584]{1,0:T(8,128)(2,1)S(1)}, bf16[16,3584]{1,0:T(8,128)(2,1)S(1)}, u32[]{:S(2)}, u32[]{:S(2)}) collective-permute-start(bf16[16,3584]{1,0:T(8,128)(2,1)S(1)} %collective-permute-done.5.refs_9_), channel_id=1, source_target_pairs={{0,16},{16,0},{1,17},{17,1},{2,18},{18,2},{3,19},{19,3},{4,20},{20... | collective-permute-start | bytes 344072 | tf_op jit(solution)/shard_map/ppermute | solution.py:353
  33.8 6.9 %collective-permute-start.17 = (bf16[16,3584]{1,0:T(8,128)(2,1)S(1)}, bf16[16,3584]{1,0:T(8,128)(2,1)S(1)}, u32[]{:S(2)}, u32[]{:S(2)}) collective-permute-start(bf16[16,3584]{1,0:T(8,128)(2,1)S(1)} %collective-permute-done.7.refs_10_), channel_id=1, source_target_pairs={{0,16},{16,0},{1,17},{17,1},{2,18},{18,2},{3,19},{19,3},{4,20},{20... | collective-permute-start | bytes 344072 | tf_op jit(solution)/shard_map/ppermute | solution.py:353
  33.9 10.0 %collective-permute-start.14 = (bf16[16,3584]{1,0:T(8,128)(2,1)S(1)}, bf16[16,3584]{1,0:T(8,128)(2,1)S(1)}, u32[]{:S(2)}, u32[]{:S(2)}) collective-permute-start(bf16[16,3584]{1,0:T(8,128)(2,1)S(1)} %collective-permute-done.6.refs_7_), channel_id=1, source_target_pairs={{0,16},{16,0},{1,17},{17,1},{2,18},{18,2},{3,19},{19,3},{4,20},{20... | collective-permute-start | bytes 344072 | tf_op jit(solution)/shard_map/ppermute | solution.py:353
  35.8 8.0 %collective-permute-start.13 = (bf16[16,3584]{1,0:T(8,128)(2,1)S(1)}, bf16[16,3584]{1,0:T(8,128)(2,1)S(1)}, u32[]{:S(2)}, u32[]{:S(2)}) collective-permute-start(bf16[16,3584]{1,0:T(8,128)(2,1)S(1)} %collective-permute-done.4.refs_6_), channel_id=1, source_target_pairs={{0,16},{16,0},{1,17},{17,1},{2,18},{18,2},{3,19},{19,3},{4,20},{20... | collective-permute-start | bytes 344072 | tf_op jit(solution)/shard_map/ppermute | solution.py:353
  37.1 7.8 %collective-permute-start.15 = (bf16[16,3584]{1,0:T(8,128)(2,1)S(1)}, bf16[16,3584]{1,0:T(8,128)(2,1)S(1)}, u32[]{:S(2)}, u32[]{:S(2)}) collective-permute-start(bf16[16,3584]{1,0:T(8,128)(2,1)S(1)} %collective-permute-done.8.refs_8_), channel_id=1, source_target_pairs={{0,16},{16,0},{1,17},{17,1},{2,18},{18,2},{3,19},{19,3},{4,20},{20... | collective-permute-start | bytes 344072 | tf_op jit(solution)/shard_map/ppermute | solution.py:353
  40.6 11.8 %collective-permute-start.25 = (bf16[720,128]{1,0:T(8,128)(2,1)S(1)}, bf16[720,128]{1,0:T(8,128)(2,1)S(1)}, u32[]{:S(2)}, u32[]{:S(2)}) collective-permute-start(bf16[720,128]{1,0:T(8,128)(2,1)S(1)} %get-tuple-element.90), channel_id=1, source_target_pairs={{0,7},{1,6},{2,5},{3,4},{4,3},{5,2},{6,1},{7,0},{8,15},{9,14},{10,... | collective-permute-start | bytes 552968 | tf_op jit(solution)/shard_map/ppermute | solution.py:358
  40.7 12.4 %collective-permute-start.24 = (bf16[720,128]{1,0:T(8,128)(2,1)S(1)}, bf16[720,128]{1,0:T(8,128)(2,1)S(1)}, u32[]{:S(2)}, u32[]{:S(2)}) collective-permute-start(bf16[720,128]{1,0:T(8,128)(2,1)S(1)} %get-tuple-element.88), channel_id=1, source_target_pairs={{0,6},{1,7},{2,4},{3,5},{4,2},{5,3},{6,0},{7,1},{8,14},{9,15},{10,... | collective-permute-start | bytes 552968 | tf_op jit(solution)/shard_map/ppermute | solution.py:358
  46.9 7.2 %collective-permute-start.18 = (bf16[128,512]{1,0:T(8,128)(2,1)S(1)}, bf16[128,512]{1,0:T(8,128)(2,1)S(1)}, u32[]{:S(2)}, u32[]{:S(2)}) collective-permute-start(bf16[128,512]{1,0:T(8,128)(2,1)S(1)} %get-tuple-element.71), channel_id=1, source_target_pairs={{0,16},{16,0},{1,17},{17,1},{2,18},{18,2},{3,19},{19,3},{4,20},{20... | collective-permute-start | bytes 393224 | tf_op jit(solution)/shard_map/ppermute | solution.py:353
  48.5 16.3 %collective-permute-start.23 = (bf16[720,128]{1,0:T(8,128)(2,1)S(1)}, bf16[720,128]{1,0:T(8,128)(2,1)S(1)}, u32[]{:S(2)}, u32[]{:S(2)}) collective-permute-start(bf16[720,128]{1,0:T(8,128)(2,1)S(1)} %get-tuple-element.86), channel_id=1, source_target_pairs={{0,5},{1,4},{2,7},{3,6},{4,1},{5,0},{6,3},{7,2},{8,13},{9,12},{10,... | collective-permute-start | bytes 552968 | tf_op jit(solution)/shard_map/ppermute | solution.py:358
  49.3 15.4 %collective-permute-start.22 = (bf16[720,128]{1,0:T(8,128)(2,1)S(1)}, bf16[720,128]{1,0:T(8,128)(2,1)S(1)}, u32[]{:S(2)}, u32[]{:S(2)}) collective-permute-start(bf16[720,128]{1,0:T(8,128)(2,1)S(1)} %get-tuple-element.84), channel_id=1, source_target_pairs={{0,4},{1,5},{2,6},{3,7},{4,0},{5,1},{6,2},{7,3},{8,12},{9,13},{10,... | collective-permute-start | bytes 552968 | tf_op jit(solution)/shard_map/ppermute | solution.py:358
  52.3 12.4 %collective-permute-start.21 = (bf16[720,128]{1,0:T(8,128)(2,1)S(1)}, bf16[720,128]{1,0:T(8,128)(2,1)S(1)}, u32[]{:S(2)}, u32[]{:S(2)}) collective-permute-start(bf16[720,128]{1,0:T(8,128)(2,1)S(1)} %get-tuple-element.82), channel_id=1, source_target_pairs={{0,3},{1,2},{2,1},{3,0},{4,7},{5,6},{6,5},{7,4},{8,11},{9,10},{10,... | collective-permute-start | bytes 552968 | tf_op jit(solution)/shard_map/ppermute | solution.py:358
  53.1 11.7 %collective-permute-start.20 = (bf16[720,128]{1,0:T(8,128)(2,1)S(1)}, bf16[720,128]{1,0:T(8,128)(2,1)S(1)}, u32[]{:S(2)}, u32[]{:S(2)}) collective-permute-start(bf16[720,128]{1,0:T(8,128)(2,1)S(1)} %get-tuple-element.80), channel_id=1, source_target_pairs={{0,2},{1,3},{2,0},{3,1},{4,6},{5,7},{6,4},{7,5},{8,10},{9,11},{10,... | collective-permute-start | bytes 552968 | tf_op jit(solution)/shard_map/ppermute | solution.py:358
  54.0 10.7 %collective-permute-start.19 = (bf16[720,128]{1,0:T(8,128)(2,1)S(1)}, bf16[720,128]{1,0:T(8,128)(2,1)S(1)}, u32[]{:S(2)}, u32[]{:S(2)}) collective-permute-start(bf16[720,128]{1,0:T(8,128)(2,1)S(1)} %get-tuple-element.78), channel_id=1, source_target_pairs={{0,1},{1,0},{2,3},{3,2},{4,5},{5,4},{6,7},{7,6},{8,9},{9,8},{10,11... | collective-permute-start | bytes 552968 | tf_op jit(solution)/shard_map/ppermute | solution.py:358
  67.0 7.7 %collective-permute-start.26 = (bf16[96,224]{1,0:T(8,128)(2,1)S(1)}, bf16[96,224]{1,0:T(8,128)(2,1)S(1)}, u32[]{:S(2)}, u32[]{:S(2)}) collective-permute-start(bf16[96,224]{1,0:T(8,128)(2,1)S(1)} %get-tuple-element.94), channel_id=1, source_target_pairs={{0,24},{1,25},{2,26},{3,27},{4,28},{5,29},{6,30},{7,31},{8,16},{9,... | collective-permute-start | bytes 129032 | tf_op jit(solution)/shard_map/ppermute | solution.py:363
  67.6 7.1 %collective-permute-start.27 = (bf16[96,224]{1,0:T(8,128)(2,1)S(1)}, bf16[96,224]{1,0:T(8,128)(2,1)S(1)}, u32[]{:S(2)}, u32[]{:S(2)}) collective-permute-start(bf16[96,224]{1,0:T(8,128)(2,1)S(1)} %get-tuple-element.95), channel_id=1, source_target_pairs={{0,8},{1,9},{2,10},{3,11},{4,12},{5,13},{6,14},{7,15},{8,0},{9,1},... | collective-permute-start | bytes 129032 | tf_op jit(solution)/shard_map/ppermute | solution.py:363
  69.9 5.0 %collective-permute-start.28 = (bf16[96,224]{1,0:T(8,128)(2,1)S(1)}, bf16[96,224]{1,0:T(8,128)(2,1)S(1)}, u32[]{:S(2)}, u32[]{:S(2)}) collective-permute-start(bf16[96,224]{1,0:T(8,128)(2,1)S(1)} %get-tuple-element.96), channel_id=1, source_target_pairs={{0,16},{1,17},{2,18},{3,19},{4,20},{5,21},{6,22},{7,23},{8,24},{9,... | collective-permute-start | bytes 129032 | tf_op jit(solution)/shard_map/ppermute | solution.py:363

commit v3 on v2

--- a/solution.py
+++ b/solution.py
@@ -112,6 +112,26 @@
     return (hidden_grad, logit_grad, router_grad)
 
 
+HINT = {
+    "pack_own": 1 << 28, "pack": 1 << 28, "first": 1 << 33, "join": 1 << 20, "merge": 1 << 10,
+    "grads_own": 40 << 28, "grads_other": 400 << 28, "prepare": 1 << 33, "panel": 1 << 28,
+    "hidden": 1 << 24,
+}
+ORDER = (
+    ("send", 0), ("forward", (0,)), ("send", 6), ("send", 1), ("send", 2), ("send", 7), ("send", 3),
+    ("forward", (1,)), ("forward", (2,)), ("send", 4), ("first", 0), ("send", 5), ("forward", (3,)),
+    ("forward", (6,)), ("forward", (7,)), ("forward", (4,)), ("forward", (5,)),
+)
+SEND = {
+    7: (("own", 1),), 3: (("own", 2), ("other", 0)), 4: (("own", 6), ("other", 0)),
+    5: (("own", 7), ("other", 1), ("first", 0)),
+}
+FORWARD = {}
+FIRST = (("block", 0),)
+SAVED = ()
+MERGE = (("own", 5),)
+
+
 NT = (((1,), (1,)), ((), ()))
 NN = (((1,), (0,)), ((), ()))
 
@@ -155,7 +175,7 @@
 
 
 def first_body(place_ref, logits_ref, ids_ref, tokens_ref, saved_ref, *outs, flight, cap):
-    z_ref, a_ref, gate_ref, saved_own_ref, saved_other_ref, *parcels, turned_ref = outs
+    z_ref, a_ref, gate_ref, saved_own_ref, saved_other_ref, keep_ref, send_ref, turned_ref = outs
     half = saved_own_ref.shape[1]
     for k, out in enumerate((saved_own_ref, saved_other_ref)):
         start = (place_ref[0] if k == 0 else 1 - place_ref[0]) * half
@@ -201,40 +221,49 @@
     pairs = jnp.concatenate([ids.astype(jnp.float32), slope], axis=0).astype(jnp.bfloat16)
     parts = (z.astype(jnp.bfloat16), pairs, slot.astype(jnp.bfloat16), high, middle, low)
     bundle = jnp.concatenate(parts, axis=0)
-    count = len(parcels)
+    count = 2 * keep_ref.shape[0]
     block = tokens_ref.shape[1] // flight
     turned_ref[...] = tokens_ref[...].T
-    for j, parcel in enumerate(parcels):
+    for j in range(count):
+        parcel = (keep_ref, send_ref)[j % 2]
         there = (place_ref[1] ^ j) & (count - 1)
         for h in range(2):
             start = pl.multiple_of((there + h * count) * block, 32)
-            parcel[h * block : (h + 1) * block] = turned_ref[pl.ds(start, block)]
-        parcel[2 * block : 2 * block + experts + 80] = bundle
-
-
-def pack_body(place_ref, ids_ref, ids_peer_ref, out_grad_ref, out_grad_peer_ref, *outs, cap):
-    me = place_ref[1]
-    selects = []
-    for ids_one in (ids_ref, ids_peer_ref):
-        ids = ids_one[...]
-        topk, tokens = ids.shape
-        wanted = (iota((8, tokens), 0) * 2) ^ me
-        picked = jnp.zeros((8, tokens), jnp.float32)
-        for k in range(topk):
-            picked = jnp.where(wanted == ids[k : k + 1], 1.0, picked)
-        slot = jnp.where(picked > 0.0, ranks(picked), -1.0)
-        place = iota((cap, tokens), 0).astype(jnp.float32)
-        select = jnp.concatenate(
-            [jnp.where(slot[q : q + 1] == place, 1.0, 0.0) for q in range(8)], axis=0
-        )
-        selects.append(select.astype(jnp.bfloat16))
-    parts = [
-        lax.dot_general(select, grad_one[...], NN, preferred_element_type=jnp.float32)
-        for select, grad_one in zip(selects, (out_grad_ref, out_grad_peer_ref))
-    ]
+            parcel[j // 2, h * block : (h + 1) * block] = turned_ref[pl.ds(start, block)]
+        parcel[j // 2, 2 * block : 2 * block + experts + 80] = bundle
+
+
+def merge_body(keep_ref, got_ref, *outs):
+    for q, out in enumerate(outs):
+        out[0] = keep_ref[q + 1]
+        out[1] = got_ref[q + 1]
+
+
+def pack_one(me, ids, grad, cap):
+    topk, tokens = ids.shape
+    wanted = (iota((8, tokens), 0) * 2) ^ me
+    picked = jnp.zeros((8, tokens), jnp.float32)
+    for k in range(topk):
+        picked = jnp.where(wanted == ids[k : k + 1], 1.0, picked)
+    slot = jnp.where(picked > 0.0, ranks(picked), -1.0)
+    place = iota((cap, tokens), 0).astype(jnp.float32)
+    select = jnp.concatenate(
+        [jnp.where(slot[q : q + 1] == place, 1.0, 0.0) for q in range(8)], axis=0
+    )
+    return lax.dot_general(
+        select.astype(jnp.bfloat16), grad, NN, preferred_element_type=jnp.float32
+    )
+
+
+def pack_own_body(place_ref, ids_ref, grad_ref, out_ref, *, cap):
+    out_ref[...] = pack_one(place_ref[1], ids_ref[...], grad_ref[...], cap)
+
+
+def pack_body(place_ref, own_ref, ids_ref, grad_ref, *outs, cap):
+    peer = pack_one(place_ref[1], ids_ref[...], grad_ref[...], cap)
     for q, out in enumerate(outs):
         rows = slice(q * cap, (q + 1) * cap)
-        out[...] = jnp.concatenate([parts[0][rows], parts[1][rows]], axis=0).astype(jnp.bfloat16)
+        out[...] = jnp.concatenate([own_ref[rows], peer[rows]], axis=0).astype(jnp.bfloat16)
 
 
 def swap_matrix(me, size, cap, dtype):
@@ -252,14 +281,14 @@
 
 
 def grads_own_body(place_ref, saved_ref, weight_ref, *refs, cap):
-    pieces, (grads_ref, line_ref) = refs[:8], refs[8:]
+    pieces, (grads_ref, line_ref) = refs[:-2], refs[-2:]
     rows = jnp.concatenate([p[...] for p in pieces], axis=0)
     grads = lax.dot_general(rows, weight_ref[...], NT, preferred_element_type=jnp.float32)
     line_ref[...] = finish_grads(place_ref[1], grads, saved_ref, grads_ref, cap)
 
 
 def grads_other_body(place_ref, saved_ref, weight_ref, line_own_ref, gate_ref, *refs, cap):
-    pieces, (grads_ref, message_ref) = refs[:8], refs[8:]
+    pieces, (grads_ref, message_ref) = refs[:-2], refs[-2:]
     rows = jnp.concatenate([p[...] for p in pieces], axis=0)
     grads = lax.dot_general(rows, weight_ref[...], NT, preferred_element_type=jnp.float32)
     other = finish_grads(place_ref[1], grads, saved_ref, grads_ref, cap)
@@ -289,47 +318,57 @@
         out_ref[:, pl.ds(start, half)] = value.astype(jnp.bfloat16)
 
 
-def panel_body(place_ref, z_ref, a_ref, message_ref, *refs, cap):
-    parcels, logit_ref, outs = refs[:8], refs[8], refs[9:]
+def views(parcels):
+    return [(parcels[0], 0), (parcels[1], 0)] + [(p, k) for p in parcels[2:] for k in range(2)]
+
+
+def prepare_body(*refs, experts):
+    parcels, (dense_ref, gate_ref) = refs[:5], refs[5:]
+    tokens = dense_ref.shape[2]
+    at = parcels[0].shape[1] - 80
+    rows = iota((experts, tokens), 0).astype(jnp.float32)
+    for q, (parcel, here) in enumerate(views(parcels)):
+        pairs = parcel[here, at : at + 16].astype(jnp.float32)
+        dense = jnp.zeros((experts, tokens), jnp.float32)
+        for k in range(8):
+            dense = jnp.where(rows == pairs[k : k + 1], pairs[8 + k : 9 + k], dense)
+        dense_ref[q] = dense
+        gate_ref[q] = sum(
+            parcel[here, at + 32 + 16 * k : at + 48 + 16 * k].astype(jnp.float32)
+            for k in (2, 1, 0)
+        )
+
+
+def panel_body(place_ref, z_ref, a_ref, message_ref, dense_ref, gate_ref, *refs, cap):
+    parcels, logit_ref, outs = refs[:5], refs[5], refs[6:]
     dp, me = place_ref[0], place_ref[1]
     experts, tokens = z_ref.shape
-    sources = len(parcels)
-    base = parcels[0].shape[0] - experts - 80
+    base = parcels[0].shape[1] - experts - 80
+    at = base + experts
     gate_all = jnp.concatenate(
         [message_ref[e, 0:1] + message_ref[16 + e, 0:1] for e in range(16)], axis=0
     )
-    upper = me >= sources
     swap = swap_matrix(me, gate_all.shape[1], cap, jnp.bfloat16)
     gate_rel = sum(
         lax.dot_general(part, swap, NN, preferred_element_type=jnp.float32)
         for part in three_halves(gate_all)
     )
-    rows = iota((experts, tokens), 0).astype(jnp.float32)
     lines, blocks = [], []
     total = None
-    for q, parcel_ref in enumerate(parcels):
-        at = base + experts
-        pairs = parcel_ref[at : at + 16].astype(jnp.float32)
-        slot = parcel_ref[at + 16 : at + 32].astype(jnp.float32)
-        gate = sum(
-            parcel_ref[at + 32 + 16 * k : at + 48 + 16 * k].astype(jnp.float32)
-            for k in (2, 1, 0)
-        )
+    for q, (parcel, here) in enumerate(views(parcels)):
+        slot = parcel[here, at + 16 : at + 32].astype(jnp.float32)
         grad = jnp.zeros((16, tokens), jnp.float32)
         for c in range(cap):
             grad = jnp.where(slot == float(c), gate_rel[:, q * cap + c : q * cap + c + 1], grad)
-        mixed = jnp.sum(grad * gate, axis=0, keepdims=True) / RSCALE
+        mixed = jnp.sum(grad * gate_ref[q], axis=0, keepdims=True) / RSCALE
         spread = jnp.concatenate(
             [grad - mixed, jnp.broadcast_to(-mixed, (experts - 16, tokens))], axis=0
         )
         if q == 0:
             logit_ref[...] = z_ref[...] + a_ref[...] * spread
-        dense = jnp.zeros((experts, tokens), jnp.float32)
-        for k in range(8):
-            dense = jnp.where(rows == pairs[k : k + 1], pairs[8 + k : 9 + k], dense)
-        line = parcel_ref[base:at].astype(jnp.float32) + dense * spread
+        line = parcel[here, base:at].astype(jnp.float32) + dense_ref[q] * spread
         lines.append(line.astype(jnp.bfloat16))
-        blocks.append(parcel_ref[:base])
+        blocks.append(parcel[here, :base])
         if len(lines) == 2:
             part = lax.dot_general(
                 jnp.concatenate(lines, axis=1),
@@ -339,6 +378,7 @@
             )
             total = part if total is None else total + part
             lines, blocks = [], []
+    upper = me >= len(views(parcels))
     columns, width = outs[0].shape
     for k, out in enumerate(outs):
         other_half, other_dp = k // 2, k % 2
@@ -347,6 +387,10 @@
         low = jnp.where(from_second, total[columns:, :width], total[:columns, :width])
         high = jnp.where(from_second, total[columns:, width:], total[:columns, width:])
         out[...] = jnp.where(from_upper, high, low).astype(out.dtype)
+
+
+def join_body(*refs):
+    refs[-1][...] = jnp.concatenate([ref[...] for ref in refs[:-1]], axis=0)
 
 
 def over_dp(value):
@@ -386,41 +430,77 @@
 
     grad_peer = over_expert(out_grad, 1)
     ids_peer = over_expert(ids_t, 1)
+    packed = kernel_call(
+        lambda *refs: pack_own_body(*refs, cap=cap),
+        jax.ShapeDtypeStruct((slots // 2, width), f32),
+        "pack_own", HINT["pack_own"], 3 << 20, place, ids_t, out_grad,
+    )
     blocks = kernel_call(
         lambda *refs: pack_body(*refs, cap=cap),
         tuple(jax.ShapeDtypeStruct((2 * cap, width), bf16) for _ in range(8)),
-        "pack", 4 * slots * tokens * width, 3 << 20,
-        place, ids_t, ids_peer, out_grad, grad_peer,
-    )
-    logits_t, tokens_in, saved = after((logits_t, tokens_in, saved), blocks[0])
-    z, a, slot_gates, saved_own, saved_other, *parcels = kernel_call(
-        lambda *refs: first_body(*refs, flight=flight, cap=cap),
-        (
-            jax.ShapeDtypeStruct((experts, tokens), f32),
-            jax.ShapeDtypeStruct((experts, tokens), f32),
-            jax.ShapeDtypeStruct((flight, tokens), f32),
-            jax.ShapeDtypeStruct((slots, half), bf16),
-            jax.ShapeDtypeStruct((slots, half), bf16),
-            *(jax.ShapeDtypeStruct((2 * block + experts + 80, tokens), bf16) for _ in range(group)),
-        ),
-        "first", 1 << 33, 3 << 20, place, logits_t, ids_t, tokens_in, saved,
-        scratch=[pltpu.VMEM((width, tokens), bf16)],
-    )
-    own, other = [blocks[0]] + [None] * 7, [None] * 8
-    sending = ((6, None), (1, None), (2, None), (7, 1), (3, 2), (4, 6), (5, 7))
-    for q, gate in sending:
-        piece = blocks[q] if gate is None else after(blocks[q], own[gate], slot_gates)
-        own[q] = over_expert(piece, 2 * q)
-    for q in range(8):
-        other[q] = over_dp(own[q])
-    saved_other = over_dp(saved_other)
-    parcels = [parcels[0]] + [
-        over_expert(after(parcels[j], own[4], own[7]), j) for j in range(1, group)
-    ]
+        "pack", HINT["pack"], 3 << 20, place, packed, ids_peer, grad_peer,
+    )
+    known = {("block", 0): blocks[0]}
+
+    def parcel_shape(count):
+        return jax.ShapeDtypeStruct((count, 2 * block + experts + 80, tokens), bf16)
+
+    def held(value, waits):
+        return after(value, *(known[w] for w in waits)) if waits else value
+
+    def send(q):
+        known["own", q] = over_expert(held(blocks[q], SEND.get(q, ())), 2 * q) if q else blocks[0]
+
+    def forward(group):
+        pieces = [known["own", q] for q in group]
+        if len(pieces) > 1:
+            pieces = [
+                kernel_call(
+                    join_body,
+                    jax.ShapeDtypeStruct((2 * cap * len(pieces), width), bf16),
+                    "join", HINT["join"], 1 << 20, *pieces,
+                )
+            ]
+        known["other", group[0]] = over_dp(held(pieces[0], FORWARD.get(group[0], ())))
+
+    def first():
+        nonlocal logits_t, tokens_in, saved
+        logits_t, tokens_in, saved = held((logits_t, tokens_in, saved), FIRST)
+        outs = kernel_call(
+            lambda *refs: first_body(*refs, flight=flight, cap=cap),
+            (
+                jax.ShapeDtypeStruct((experts, tokens), f32),
+                jax.ShapeDtypeStruct((experts, tokens), f32),
+                jax.ShapeDtypeStruct((flight, tokens), f32),
+                jax.ShapeDtypeStruct((slots, half), bf16),
+                jax.ShapeDtypeStruct((slots, half), bf16),
+                *(parcel_shape(group // 2),) * 2,
+            ),
+            "first", HINT["first"], 3 << 20, place, logits_t, ids_t, tokens_in, saved,
+            scratch=[pltpu.VMEM((width, tokens), bf16)],
+        )
+        known["first", 0] = outs[2]
+        known["results", 0] = outs
+
+    for kind, which in ORDER:
+        {"send": send, "forward": forward, "first": lambda _: first()}[kind](which)
+    z, a, slot_gates, saved_own, saved_other, parcel_keep, parcel_send = known["results", 0]
+    own = [known["own", q] for q in range(8)]
+    groups = [which for kind, which in ORDER if kind == "forward"]
+    arrival = [q for members in sorted(groups) for q in members]
+    other = [known["other", members[0]] for members in sorted(groups)]
+    assert arrival == list(range(8))
+    saved_other = over_dp(held(saved_other, SAVED))
+    parcel_got = over_expert(parcel_send, 1)
+    merged = kernel_call(
+        merge_body, (parcel_shape(2),) * 3, "merge", HINT["merge"], 4 << 20,
+        held(parcel_keep, MERGE), parcel_got,
+    )
+    parcels = (parcel_keep, parcel_got, *(over_expert(m, 2 * q + 2) for q, m in enumerate(merged)))
     grads_own, line_own = kernel_call(
         lambda *refs: grads_own_body(*refs, cap=cap),
         (jax.ShapeDtypeStruct((slots, half), f32), jax.ShapeDtypeStruct((1, slots), f32)),
-        "grads_own", 40 * slots * width * half, 5 << 20, place, saved_own, weight, *own,
+        "grads_own", HINT["grads_own"], 5 << 20, place, saved_own, weight, *own,
     )
     grads_other, message = kernel_call(
         lambda *refs: grads_other_body(*refs, cap=cap),
@@ -428,12 +508,20 @@
             jax.ShapeDtypeStruct((slots, half), bf16),
             jax.ShapeDtypeStruct((2 * flight, 2, slots), f32),
         ),
-        "grads_other", 40 * slots * width * half, 5 << 20,
+        "grads_other", HINT["grads_other"], 5 << 20,
         place, saved_other, weight, line_own, slot_gates, *other,
     )
     grads_back = over_dp(grads_other)
     message = lax.all_to_all(message, ("dp", "expert"), 0, 0, tiled=True)
     message, grads_back = lax.optimization_barrier((message, grads_back))
+    dense, gates = kernel_call(
+        lambda *refs: prepare_body(*refs, experts=experts),
+        (
+            jax.ShapeDtypeStruct((group, experts, tokens), f32),
+            jax.ShapeDtypeStruct((group, 16, tokens), f32),
+        ),
+        "prepare", HINT["prepare"], 1 << 20, *parcels,
+    )
     logit_t, *sums = kernel_call(
         lambda *refs: panel_body(*refs, cap=cap),
         (
@@ -441,13 +529,13 @@
             jax.ShapeDtypeStruct((experts // 2, block), f32),
             *(jax.ShapeDtypeStruct((experts // 2, block), bf16) for _ in range(3)),
         ),
-        "panel", 1 << 28, 4 << 20,
-        place, z, a, message, *parcels,
+        "panel", HINT["panel"], 4 << 20,
+        place, z, a, message, dense, gates, *parcels,
     )
     hidden_grad = kernel_call(
         lambda *refs: hidden_body(*refs, cap=cap),
         jax.ShapeDtypeStruct((slots, hidden), bf16),
-        "hidden", 1 << 24, 1 << 20,
+        "hidden", HINT["hidden"], 1 << 20,
         place, grads_own, grads_back, message,
     )
     far = [over_both(sums[3], 1, group), over_both(sums[2], 0, group), over_both(sums[1], 1, 0)]

time: 75.9 us -> 72.1 us (0.950)
  starting transfers between devices: 38.4 us -> 33.6 us
  local copies, waits for them, and re-layouts: 5.08 us -> 1.88 us
  blocking collectives: 10.5 us -> 12.6 us
  Pallas kernels: 10 us -> 11.1 us
  waiting for transfers between devices: 10.2 us -> 11.2 us
    ppermute x16 -> x13, starting transfers between devices: 22.7 us -> 18.3 us  [over_expert(): return lax.ppermute(value, 'expert', [(k, k ^ bits) for k in range(count)])]
    unnamed x12, local copies, waits for them, and re-layouts: 5.08 us -> 1.88 us
    ppermute x10, waiting for transfers between devices: 1.09 us -> 3.62 us  [over_dp(): return lax.ppermute(value, 'dp', [(0, 1), (1, 0)])]
    all_to_all x1, blocking collectives: 10.5 us -> 12.6 us  [paired_local(): message = lax.all_to_all(message, ('dp', 'expert'), 0, 0, tiled=True)]
    ppermute x16 -> x13, waiting for transfers between devices: 7.1 us -> 5.73 us  [over_expert(): return lax.ppermute(value, 'expert', [(k, k ^ bits) for k in range(count)])]
    pallas_call x6 -> x9, Pallas kernels: 10 us -> 11.1 us  [kernel_call(): pl.pallas_call(body, out_shape=out_shape, in_specs=[pl.BlockSpec(memory_s...]
  transfers between devices with their start and end apart: 29 -> 26, of which waited for: 8 -> 7; matrix products, arithmetic and copies ran while one was open for 0% -> 0% of each run, Pallas kernels for 9% -> 9%
where the time goes in v3:
time: 72.1 us; the launch traced here: 71.9 us
  starting transfers between devices  33.6 us (47%)
  blocking collectives  12.6 us (17%)
  waiting for transfers between devices  11.2 us (16%)
  Pallas kernels  11.1 us (15%)
  local copies, waits for them, and re-layouts  1.88 us (3%)
  between operations  0.77 us (1%)
  other arithmetic  0.74 us (1%)
    ppermute x13, starting transfers between devices, over_expert(): return lax.ppermute(value, 'expert', [(k, k ^ bits) for k in range(count)])  18.3 us
    all_to_all x1, blocking collectives, paired_local(): message = lax.all_to_all(message, ('dp', 'expert'), 0, 0, tiled=True)  12.6 us
    pallas_call x9, Pallas kernels, kernel_call(): pl.pallas_call(body, out_shape=out_shape, in_specs=[pl.BlockSpec(memory_s...  11.1 us
    ppermute x10, starting transfers between devices, over_dp(): return lax.ppermute(value, 'dp', [(0, 1), (1, 0)])  10.9 us
    ppermute x13, waiting for transfers between devices, over_expert(): return lax.ppermute(value, 'expert', [(k, k ^ bits) for k in range(count)])  5.73 us
    ppermute x3, starting transfers between devices, over_both(): lax.ppermute(value, ('dp', 'expert'), [(k, k ^ dp_bit * count + bits) for...  4.39 us
    ppermute x10, waiting for transfers between devices, over_dp(): return lax.ppermute(value, 'dp', [(0, 1), (1, 0)])  3.62 us
    unnamed x12, local copies, waits for them, and re-layouts  1.88 us
  transfers between devices with their start and end apart: 26, of which 7 were waited for; matrix products, arithmetic and copies ran while one was open for 0% of the time, Pallas kernels for 9%

profile of v3, /device:TPU:0, one launch (start us, length us, event | category | flops | bytes accessed | tf_op | source)
XLA Modules:
  0.0 71.9 jit_solution(16642288751189597622)
XLA Ops:
  0.6 0.5 collective-permute-start.1
  1.1 0.1 collective-permute-start
  1.2 0.1 pad_add_fusion.refs_0_
  1.3 1.2 %copy-done = bf16[128,3584]{1,0:T(8,128)(2,1)S(1)} copy-done((bf16[128,3584]{1,0:T(8,128)(2,1)S(1)}, bf16[128,3584]{1,0:T(8,128)(2,1)}, u32[]{:S(2)}) %copy-start) | copy-done | bytes 917528
  2.5 0.7 copy-done.1
  3.2 0.9 %pack_own.1.refs_1_ = f32[64,3584]{1,0:T(8,128)S(1)} custom-call(s32[2]{0:T(128)S(1)} %pad_add_fusion.refs_0_, s32[8,128]{1,0:T(8,128)S(1)} %bitcast.11, bf16[128,3584]{1,0:T(8,128)(2,1)S(1)} %copy-done), custom_call_target="tpu_custom_call" | custom-call | flops 268435456 | bytes 3145728 | tf_op jit(solution)/shard_map/pack_own/pallas_call | solution.py:145
  4.1 0.0 collective-permute-done.refs_2_
  4.1 0.0 collective-permute-done.1.refs_3_
  4.1 0.9 %pack.1 = (bf16[16,3584]{1,0:T(8,128)(2,1)S(1)}, bf16[16,3584]{1,0:T(8,128)(2,1)S(1)}, bf16[16,3584]{1,0:T(8,128)(2,1)S(1)}, bf16[16,3584]{1,0:T(8,128)(2,1)S(1)...) custom-call(s32[2]{0:T(128)S(1)} %pad_add_fusion.refs_0_, ...), custom_call_target="tpu_custom_call" | custom-call | flops 268435456 | bytes 3145728 | tf_op jit(solution)/shard_map/pack/pallas_call | solution.py:145
  5.1 0.0 copy-start.2
  5.1 1.2 %first.1 = (f32[192,128]{1,0:T(8,128)S(1)}, f32[192,128]{1,0:T(8,128)S(1)}, f32[16,128]{1,0:T(8,128)S(1)}, bf16[128,512]{1,0:T(8,128)(2,1)S(1)}, bf16[128,512]{1...) custom-call(s32[2]{0:T(128)S(1)} %pad_add_fusion.refs_0_, ...), custom_call_target="tpu_custom_call" | custom-call | flops 8589934592 | bytes 3145728 | tf_op jit(solution)/shard_map/first/pallas_call | solution.py:145
  6.4 0.5 collective-permute-start.19
  6.8 2.6 %collective-permute-start.2 = (bf16[16,3584]{1,0:T(8,128)(2,1)S(1)}, bf16[16,3584]{1,0:T(8,128)(2,1)S(1)}, u32[]{:S(2)}, u32[]{:S(2)}) collective-permute-start(bf16[16,3584]{1,0:T(8,128)(2,1)S(1)} %get-tuple-element.48), channel_id=1, source_target_pairs={{0,2},{1,3},{2,0},{3,1},{4,6},{5,7},{6,4},{7,5},{8,10},{9,11},{10,... | collective-permute-start | bytes 344072 | tf_op jit(solution)/shard_map/ppermute | solution.py:402
  9.5 3.6 %collective-permute-start.6 = (bf16[16,3584]{1,0:T(8,128)(2,1)S(1)}, bf16[16,3584]{1,0:T(8,128)(2,1)S(1)}, u32[]{:S(2)}, u32[]{:S(2)}) collective-permute-start(bf16[16,3584]{1,0:T(8,128)(2,1)S(1)} %get-tuple-element.53), channel_id=1, source_target_pairs={{0,12},{1,13},{2,14},{3,15},{4,8},{5,9},{6,10},{7,11},{8,4},{9,5},... | collective-permute-start | bytes 344072 | tf_op jit(solution)/shard_map/ppermute | solution.py:402
  13.0 1.5 %collective-permute-start.4 = (bf16[16,3584]{1,0:T(8,128)(2,1)S(1)}, bf16[16,3584]{1,0:T(8,128)(2,1)S(1)}, u32[]{:S(2)}, u32[]{:S(2)}) collective-permute-start(bf16[16,3584]{1,0:T(8,128)(2,1)S(1)} %get-tuple-element.43.refs_3_), channel_id=1, source_target_pairs={{0,16},{16,0},{1,17},{17,1},{2,18},{18,2},{3,19},{19,3},{4,20},{20... | collective-permute-start | bytes 344072 | tf_op jit(solution)/shard_map/ppermute | solution.py:397
  14.5 0.5 collective-permute-start.11
  15.1 0.0 collective-permute-done.2.refs_4_
  15.1 0.0 collective-permute-start.3
  15.1 1.5 %collective-permute-done.6.refs_9_ = bf16[16,3584]{1,0:T(8,128)(2,1)S(1)} collective-permute-done((bf16[16,3584]{1,0:T(8,128)(2,1)S(1)}, bf16[16,3584]{1,0:T(8,128)(2,1)S(1)}, u32[]{:S(2)}, u32[]{:S(2)}) %collective-permute-start.6) | collective-permute-done | bytes 114720 | tf_op jit(solution)/shard_map/ppermute | solution.py:402
  16.6 3.5 %collective-permute-start.8 = (bf16[16,3584]{1,0:T(8,128)(2,1)S(1)}, bf16[16,3584]{1,0:T(8,128)(2,1)S(1)}, u32[]{:S(2)}, u32[]{:S(2)}) collective-permute-start(bf16[16,3584]{1,0:T(8,128)(2,1)S(1)} %get-tuple-element.57), channel_id=1, source_target_pairs={{0,14},{1,15},{2,12},{3,13},{4,10},{5,11},{6,8},{7,9},{8,6},{9,7},... | collective-permute-start | bytes 344072 | tf_op jit(solution)/shard_map/ppermute | solution.py:402
  20.1 0.0 collective-permute-done.4.refs_5_
  20.1 1.5 %collective-permute-start.9 = (bf16[16,3584]{1,0:T(8,128)(2,1)S(1)}, bf16[16,3584]{1,0:T(8,128)(2,1)S(1)}, u32[]{:S(2)}, u32[]{:S(2)}) collective-permute-start(bf16[16,3584]{1,0:T(8,128)(2,1)S(1)} %collective-permute-done.2.refs_4_), channel_id=1, source_target_pairs={{0,16},{16,0},{1,17},{17,1},{2,18},{18,2},{3,19},{19,3},{4,20},{20... | collective-permute-start | bytes 344072 | tf_op jit(solution)/shard_map/ppermute | solution.py:397
  21.6 0.0 collective-permute-done.3.refs_5_
  21.6 0.8 %collective-permute-start.5 = (bf16[16,3584]{1,0:T(8,128)(2,1)S(1)}, bf16[16,3584]{1,0:T(8,128)(2,1)S(1)}, u32[]{:S(2)}, u32[]{:S(2)}) collective-permute-start(bf16[16,3584]{1,0:T(8,128)(2,1)S(1)} %get-tuple-element.51), channel_id=1, source_target_pairs={{0,6},{1,7},{2,4},{3,5},{4,2},{5,3},{6,0},{7,1},{8,14},{9,15},{10,... | collective-permute-start | bytes 344072 | tf_op jit(solution)/shard_map/ppermute | solution.py:402
  22.4 2.6 %collective-permute-done.8.refs_10_ = bf16[16,3584]{1,0:T(8,128)(2,1)S(1)} collective-permute-done((bf16[16,3584]{1,0:T(8,128)(2,1)S(1)}, bf16[16,3584]{1,0:T(8,128)(2,1)S(1)}, u32[]{:S(2)}, u32[]{:S(2)}) %collective-permute-start.8) | collective-permute-done | bytes 114720 | tf_op jit(solution)/shard_map/ppermute | solution.py:402
  25.0 2.1 %collective-permute-start.7 = (bf16[16,3584]{1,0:T(8,128)(2,1)S(1)}, bf16[16,3584]{1,0:T(8,128)(2,1)S(1)}, u32[]{:S(2)}, u32[]{:S(2)}) collective-permute-start(bf16[16,3584]{1,0:T(8,128)(2,1)S(1)} %get-tuple-element.54), channel_id=1, source_target_pairs={{0,8},{1,9},{2,10},{3,11},{4,12},{5,13},{6,14},{7,15},{8,0},{9,1},... | collective-permute-start | bytes 344072 | tf_op jit(solution)/shard_map/ppermute | solution.py:402
  27.1 0.0 collective-permute-done.9.refs_6_
  27.1 1.6 %collective-permute-start.12 = (bf16[16,3584]{1,0:T(8,128)(2,1)S(1)}, bf16[16,3584]{1,0:T(8,128)(2,1)S(1)}, u32[]{:S(2)}, u32[]{:S(2)}) collective-permute-start(bf16[16,3584]{1,0:T(8,128)(2,1)S(1)} %collective-permute-done.3.refs_5_), channel_id=1, source_target_pairs={{0,16},{16,0},{1,17},{17,1},{2,18},{18,2},{3,19},{19,3},{4,20},{20... | collective-permute-start | bytes 344072 | tf_op jit(solution)/shard_map/ppermute | solution.py:397
  28.7 0.0 collective-permute-done.11.refs_1_
  28.7 1.0 %collective-permute-start.10 = (bf16[16,3584]{1,0:T(8,128)(2,1)S(1)}, bf16[16,3584]{1,0:T(8,128)(2,1)S(1)}, u32[]{:S(2)}, u32[]{:S(2)}) collective-permute-start(bf16[16,3584]{1,0:T(8,128)(2,1)S(1)} %get-tuple-element.59), channel_id=1, source_target_pairs={{0,10},{1,11},{2,8},{3,9},{4,14},{5,15},{6,12},{7,13},{8,2},{9,3},... | collective-permute-start | bytes 344072 | tf_op jit(solution)/shard_map/ppermute | solution.py:402
  29.7 3.4 %collective-permute-done.12.refs_7_ = bf16[16,3584]{1,0:T(8,128)(2,1)S(1)} collective-permute-done((bf16[16,3584]{1,0:T(8,128)(2,1)S(1)}, bf16[16,3584]{1,0:T(8,128)(2,1)S(1)}, u32[]{:S(2)}, u32[]{:S(2)}) %collective-permute-start.12) | collective-permute-done | bytes 114720 | tf_op jit(solution)/shard_map/ppermute | solution.py:397
  33.1 1.6 %collective-permute-start.16 = (bf16[16,3584]{1,0:T(8,128)(2,1)S(1)}, bf16[16,3584]{1,0:T(8,128)(2,1)S(1)}, u32[]{:S(2)}, u32[]{:S(2)}) collective-permute-start(bf16[16,3584]{1,0:T(8,128)(2,1)S(1)} %collective-permute-done.6.refs_9_), channel_id=1, source_target_pairs={{0,16},{16,0},{1,17},{17,1},{2,18},{18,2},{3,19},{19,3},{4,20},{20... | collective-permute-start | bytes 344072 | tf_op jit(solution)/shard_map/ppermute | solution.py:397
  34.7 0.0 collective-permute-done.5.refs_6_
  34.7 0.4 collective-permute-start.17
  35.1 1.5 %collective-permute-done.7.refs_7_ = bf16[16,3584]{1,0:T(8,128)(2,1)S(1)} collective-permute-done((bf16[16,3584]{1,0:T(8,128)(2,1)S(1)}, bf16[16,3584]{1,0:T(8,128)(2,1)S(1)}, u32[]{:S(2)}, u32[]{:S(2)}) %collective-permute-start.7) | collective-permute-done | bytes 114720 | tf_op jit(solution)/shard_map/ppermute | solution.py:402
  36.6 0.6 collective-permute-start.13
  37.3 0.1 collective-permute-done.10.refs_8_
  37.3 1.3 %collective-permute-start.14 = (bf16[16,3584]{1,0:T(8,128)(2,1)S(1)}, bf16[16,3584]{1,0:T(8,128)(2,1)S(1)}, u32[]{:S(2)}, u32[]{:S(2)}) collective-permute-start(bf16[16,3584]{1,0:T(8,128)(2,1)S(1)} %collective-permute-done.7.refs_7_), channel_id=1, source_target_pairs={{0,16},{16,0},{1,17},{17,1},{2,18},{18,2},{3,19},{19,3},{4,20},{20... | collective-permute-start | bytes 344072 | tf_op jit(solution)/shard_map/ppermute | solution.py:397
  38.7 0.0 collective-permute-done.19.got_ref.refs_1_.refs_7_
  38.7 0.7 collective-permute-start.15
  39.4 2.0 %grads_own.1 = (f32[128,512]{1,0:T(8,128)S(1)}, f32[1,128]{1,0:T(1,128)S(1)}) custom-call(s32[2]{0:T(128)S(1)} %pad_add_fusion.refs_0_, bf16[128,512]{1,0:T(8,128)(2,1)S(1)} %get-tuple-element.47.refs_1_, bf16[512,3584]{1,0:T(8,128)(2,1)S(1)} %bitcast.13, bf16[16,3584]{1,0:T(8,128)(2,1)S(1)} %get-tuple-element.43.refs_3_, ...), custom_call_target="tpu_custom_call" | custom-call | flops 10737418240 | bytes 5242880 | tf_op jit(solution)/shard_map/grads_own/pallas_call | solution.py:145
  41.3 0.1 merge.1
  41.4 0.0 collective-permute-done.16.refs_11_
  41.4 2.1 %collective-permute-start.20 = (bf16[2,720,128]{2,1,0:T(8,128)(2,1)S(1)}, bf16[2,720,128]{2,1,0:T(8,128)(2,1)S(1)}, u32[]{:S(2)}, u32[]{:S(2)}) collective-permute-start(bf16[2,720,128]{2,1,0:T(8,128)(2,1)S(1)} %get-tuple-element.72), channel_id=1, source_target_pairs={{0,2},{1,3},{2,0},{3,1},{4,6},{5,7},{6,4},{7,5},{8,10},{9,11},{10,... | collective-permute-start | bytes 1105928 | tf_op jit(solution)/shard_map/ppermute | solution.py:402
  43.5 0.0 collective-permute-done.17.refs_12_
  43.5 0.0 collective-permute-start.21
  43.5 0.0 collective-permute-done.13.refs_8_
  43.5 1.5 %collective-permute-start.22 = (bf16[2,720,128]{2,1,0:T(8,128)(2,1)S(1)}, bf16[2,720,128]{2,1,0:T(8,128)(2,1)S(1)}, u32[]{:S(2)}, u32[]{:S(2)}) collective-permute-start(bf16[2,720,128]{2,1,0:T(8,128)(2,1)S(1)} %get-tuple-element.74), channel_id=1, source_target_pairs={{0,6},{1,7},{2,4},{3,5},{4,2},{5,3},{6,0},{7,1},{8,14},{9,15},{10,... | collective-permute-start | bytes 1105928 | tf_op jit(solution)/shard_map/ppermute | solution.py:402
  45.0 0.2 collective-permute-done.15.refs_10_
  45.3 2.0 %grads_other.1 = (bf16[128,512]{1,0:T(8,128)(2,1)S(1)}, f32[32,2,128]{2,1,0:T(2,128)S(1)}) custom-call(s32[2]{0:T(128)S(1)} %pad_add_fusion.refs_0_, bf16[128,512]{1,0:T(8,128)(2,1)S(1)} %collective-permute-done.11.refs_1_, bf16[512,3584]{1,0:T(8,128)(2,1)S(1)} %bitcast.14, f32[1,128]{1,0:T(1,128)S(1)} %get-tuple-element.62.refs_3_, ...), custom_call_target="tpu_custom_call" | custom-call | flops 107374182400 | bytes 5242880 | tf_op jit(solution)/shard_map/grads_other/pallas_call | solution.py:145
  47.2 1.1 %collective-permute-start.18 = (bf16[128,512]{1,0:T(8,128)(2,1)S(1)}, bf16[128,512]{1,0:T(8,128)(2,1)S(1)}, u32[]{:S(2)}, u32[]{:S(2)}) collective-permute-start(bf16[128,512]{1,0:T(8,128)(2,1)S(1)} %get-tuple-element.64), channel_id=1, source_target_pairs={{0,16},{16,0},{1,17},{17,1},{2,18},{18,2},{3,19},{19,3},{4,20},{20... | collective-permute-start | bytes 393224 | tf_op jit(solution)/shard_map/ppermute | solution.py:397
  48.3 12.6 %all_to_all.5.refs_3_ = f32[32,2,128]{2,1,0:T(2,128)S(1)} all-to-all(f32[32,2,128]{2,1,0:T(2,128)S(1)} %get-tuple-element.63), channel_id=1, replica_groups=mesh['dp'=2,'expert'=16] {'dp','expert'}, dimensions={0} | all-to-all | bytes 65536 | tf_op jit(solution)/shard_map/all_to_all | solution.py:515
  60.9 0.0 collective-permute-done.18.refs_2_
  60.9 0.0 collective-permute-done.20.refs_2_.refs_8_
  61.0 0.0 collective-permute-done.21.refs_3_.refs_9_
  61.0 0.4 prepare.1
  61.4 1.9 %panel.1 = (f32[192,128]{1,0:T(8,128)}, f32[96,224]{1,0:T(8,128)S(1)}, bf16[96,224]{1,0:T(8,128)(2,1)S(1)}, bf16[96,224]{1,0:T(8,128)(2,1)S(1)}, bf16[96,224]{1,0:T(8,128)(2,1)S(1)}) custom-call(s32[2]{0:T(128)S(1)} %pad_add_fusion.refs_0_, f32[192,128]{1,0:T(8,128)S(1)} %get-tuple-element.67.refs_1_, f32[192,128]{1,0:T(8,128)S(1)} %get-tuple-element.68.refs_2_, ...), custom_call_target="tpu_custom_call" | custom-call | flops 268435456 | bytes 4194304 | tf_op jit(solution)/shard_map/panel/pallas_call | solution.py:145
  63.4 1.0 %collective-permute-start.23 = (bf16[96,224]{1,0:T(8,128)(2,1)S(1)}, bf16[96,224]{1,0:T(8,128)(2,1)S(1)}, u32[]{:S(2)}, u32[]{:S(2)}) collective-permute-start(bf16[96,224]{1,0:T(8,128)(2,1)S(1)} %get-tuple-element.80), channel_id=1, source_target_pairs={{0,24},{1,25},{2,26},{3,27},{4,28},{5,29},{6,30},{7,31},{8,16},{9,... | collective-permute-start | bytes 129032 | tf_op jit(solution)/shard_map/ppermute | solution.py:407
  64.4 1.9 %collective-permute-start.24 = (bf16[96,224]{1,0:T(8,128)(2,1)S(1)}, bf16[96,224]{1,0:T(8,128)(2,1)S(1)}, u32[]{:S(2)}, u32[]{:S(2)}) collective-permute-start(bf16[96,224]{1,0:T(8,128)(2,1)S(1)} %get-tuple-element.81), channel_id=1, source_target_pairs={{0,8},{1,9},{2,10},{3,11},{4,12},{5,13},{6,14},{7,15},{8,0},{9,1},... | collective-permute-start | bytes 129032 | tf_op jit(solution)/shard_map/ppermute | solution.py:407
  66.4 1.4 %collective-permute-start.25 = (bf16[96,224]{1,0:T(8,128)(2,1)S(1)}, bf16[96,224]{1,0:T(8,128)(2,1)S(1)}, u32[]{:S(2)}, u32[]{:S(2)}) collective-permute-start(bf16[96,224]{1,0:T(8,128)(2,1)S(1)} %get-tuple-element.82), channel_id=1, source_target_pairs={{0,16},{1,17},{2,18},{3,19},{4,20},{5,21},{6,22},{7,23},{8,24},{9,... | collective-permute-start | bytes 129032 | tf_op jit(solution)/shard_map/ppermute | solution.py:407
  67.8 1.6 %hidden.1 = bf16[128,1024]{1,0:T(8,128)(2,1)} custom-call(s32[2]{0:T(128)S(1)} %pad_add_fusion.refs_0_, f32[128,512]{1,0:T(8,128)S(1)} %get-tuple-element.60.refs_1_, bf16[128,512]{1,0:T(8,128)(2,1)S(1)} %collective-permute-done.18.refs_2_, f32[32,2,128]{2,1,0:T(2,128)S(1)} %all_to_all.5.refs_3_), custom_call_target="tpu_custom_call" | custom-call | flops 16777216 | bytes 1048576 | tf_op jit(solution)/shard_map/hidden/pallas_call | solution.py:145
  69.4 1.9 %collective-permute-done.23 = bf16[96,224]{1,0:T(8,128)(2,1)S(1)} collective-permute-done((bf16[96,224]{1,0:T(8,128)(2,1)S(1)}, bf16[96,224]{1,0:T(8,128)(2,1)S(1)}, u32[]{:S(2)}, u32[]{:S(2)}) %collective-permute-start.23) | collective-permute-done | bytes 43040 | tf_op jit(solution)/shard_map/ppermute | solution.py:407
  71.3 0.0 collective-permute-done.25
  71.3 0.7 add_bitcast_fusion
  (12 shorter events, 0.0 us)
Async XLA Ops:
  0.6 3.5 %collective-permute-start.1 = (bf16[128,3584]{1,0:T(8,128)(2,1)}, bf16[128,3584]{1,0:T(8,128)(2,1)S(1)}, u32[]{:S(2)}, u32[]{:S(2)}) collective-permute-start(bf16[128,3584]{1,0:T(8,128)(2,1)} %refs_2_.1), channel_id=1, source_target_pairs={{0,1},{1,0},{2,3},{3,2},{4,5},{5,4},{6,7},{7,6},{8,9},{9,8},{10,11... | collective-permute-start | bytes 2752520 | tf_op jit(solution)/shard_map/ppermute | solution.py:402
  1.1 3.0 %collective-permute-start = (s32[8,128]{1,0:T(8,128)}, s32[8,128]{1,0:T(8,128)S(1)}, u32[]{:S(2)}, u32[]{:S(2)}) collective-permute-start(s32[8,128]{1,0:T(8,128)} %bitcast.10), channel_id=1, source_target_pairs={{0,1},{1,0},{2,3},{3,2},{4,5},{5,4},{6,7},{7,6},{8,9},{9,8},{10,11... | collective-permute-start | bytes 12296 | tf_op jit(solution)/shard_map/ppermute | solution.py:402
  1.3 1.2 %copy-start = (bf16[128,3584]{1,0:T(8,128)(2,1)S(1)}, bf16[128,3584]{1,0:T(8,128)(2,1)}, u32[]{:S(2)}) copy-start(bf16[128,3584]{1,0:T(8,128)(2,1)} %refs_2_.1) | copy-start | bytes 2752516
  2.5 0.7 copy-start.1
  3.2 1.9 %copy-start.3 = (bf16[128,3584]{1,0:T(8,128)(2,1)S(1)}, bf16[128,3584]{1,0:T(8,128)(2,1)}, u32[]{:S(2)}) copy-start(bf16[128,3584]{1,0:T(8,128)(2,1)} %refs_3_) | copy-start | bytes 2752516
  3.2 1.9 %copy-start.4 = (bf16[1,1,16,8,1024]{4,3,2,1,0:T(8,128)(2,1)S(1)}, bf16[1,1,16,8,1024]{4,3,2,1,0:T(8,128)(2,1)}, u32[]{:S(2)}) copy-start(bf16[1,1,16,8,1024]{4,3,2,1,0:T(8,128)(2,1)} %param.10) | copy-start | bytes 786436
  3.2 1.9 %copy-start.5 = (f32[128,192]{0,1:T(8,128)S(1)}, f32[128,192]{0,1:T(8,128)}, u32[]{:S(2)}) copy-start(f32[128,192]{0,1:T(8,128)} %param.8) | copy-start | bytes 294916
  5.1 34.2 %copy-start.2 = (bf16[1,512,3584]{2,1,0:T(8,128)(2,1)S(1)}, bf16[1,512,3584]{2,1,0:T(8,128)(2,1)}, u32[]{:S(2)}) copy-start(bf16[1,512,3584]{2,1,0:T(8,128)(2,1)} %param.11) | copy-start | bytes 11010052
  6.4 32.3 %collective-permute-start.19 = (bf16[4,720,128]{2,1,0:T(8,128)(2,1)S(1)}, bf16[4,720,128]{2,1,0:T(8,128)(2,1)S(1)}, u32[]{:S(2)}, u32[]{:S(2)}) collective-permute-start(bf16[4,720,128]{2,1,0:T(8,128)(2,1)S(1)} %get-tuple-element.70), channel_id=1, source_target_pairs={{0,1},{1,0},{2,3},{3,2},{4,5},{5,4},{6,7},{7,6},{8,9},{9,8},{10,11... | collective-permute-start | bytes 2211848 | tf_op jit(solution)/shard_map/ppermute | solution.py:402
  6.8 8.2 %collective-permute-start.2 = (bf16[16,3584]{1,0:T(8,128)(2,1)S(1)}, bf16[16,3584]{1,0:T(8,128)(2,1)S(1)}, u32[]{:S(2)}, u32[]{:S(2)}) collective-permute-start(bf16[16,3584]{1,0:T(8,128)(2,1)S(1)} %get-tuple-element.48), channel_id=1, source_target_pairs={{0,2},{1,3},{2,0},{3,1},{4,6},{5,7},{6,4},{7,5},{8,10},{9,11},{10,... | collective-permute-start | bytes 344072 | tf_op jit(solution)/shard_map/ppermute | solution.py:402
  9.5 7.2 %collective-permute-start.6 = (bf16[16,3584]{1,0:T(8,128)(2,1)S(1)}, bf16[16,3584]{1,0:T(8,128)(2,1)S(1)}, u32[]{:S(2)}, u32[]{:S(2)}) collective-permute-start(bf16[16,3584]{1,0:T(8,128)(2,1)S(1)} %get-tuple-element.53), channel_id=1, source_target_pairs={{0,12},{1,13},{2,14},{3,15},{4,8},{5,9},{6,10},{7,11},{8,4},{9,5},... | collective-permute-start | bytes 344072 | tf_op jit(solution)/shard_map/ppermute | solution.py:402
  13.0 7.1 %collective-permute-start.4 = (bf16[16,3584]{1,0:T(8,128)(2,1)S(1)}, bf16[16,3584]{1,0:T(8,128)(2,1)S(1)}, u32[]{:S(2)}, u32[]{:S(2)}) collective-permute-start(bf16[16,3584]{1,0:T(8,128)(2,1)S(1)} %get-tuple-element.43.refs_3_), channel_id=1, source_target_pairs={{0,16},{16,0},{1,17},{17,1},{2,18},{18,2},{3,19},{19,3},{4,20},{20... | collective-permute-start | bytes 344072 | tf_op jit(solution)/shard_map/ppermute | solution.py:397
  14.5 14.2 %collective-permute-start.11 = (bf16[128,512]{1,0:T(8,128)(2,1)S(1)}, bf16[128,512]{1,0:T(8,128)(2,1)S(1)}, u32[]{:S(2)}, u32[]{:S(2)}) collective-permute-start(bf16[128,512]{1,0:T(8,128)(2,1)S(1)} %get-tuple-element.61), channel_id=1, source_target_pairs={{0,16},{16,0},{1,17},{17,1},{2,18},{18,2},{3,19},{19,3},{4,20},{20... | collective-permute-start | bytes 393224 | tf_op jit(solution)/shard_map/ppermute | solution.py:397
  15.1 6.5 %collective-permute-start.3 = (bf16[16,3584]{1,0:T(8,128)(2,1)S(1)}, bf16[16,3584]{1,0:T(8,128)(2,1)S(1)}, u32[]{:S(2)}, u32[]{:S(2)}) collective-permute-start(bf16[16,3584]{1,0:T(8,128)(2,1)S(1)} %get-tuple-element.49), channel_id=1, source_target_pairs={{0,4},{1,5},{2,6},{3,7},{4,0},{5,1},{6,2},{7,3},{8,12},{9,13},{10,... | collective-permute-start | bytes 344072 | tf_op jit(solution)/shard_map/ppermute | solution.py:402
  16.6 8.4 %collective-permute-start.8 = (bf16[16,3584]{1,0:T(8,128)(2,1)S(1)}, bf16[16,3584]{1,0:T(8,128)(2,1)S(1)}, u32[]{:S(2)}, u32[]{:S(2)}) collective-permute-start(bf16[16,3584]{1,0:T(8,128)(2,1)S(1)} %get-tuple-element.57), channel_id=1, source_target_pairs={{0,14},{1,15},{2,12},{3,13},{4,10},{5,11},{6,8},{7,9},{8,6},{9,7},... | collective-permute-start | bytes 344072 | tf_op jit(solution)/shard_map/ppermute | solution.py:402
  20.1 7.0 %collective-permute-start.9 = (bf16[16,3584]{1,0:T(8,128)(2,1)S(1)}, bf16[16,3584]{1,0:T(8,128)(2,1)S(1)}, u32[]{:S(2)}, u32[]{:S(2)}) collective-permute-start(bf16[16,3584]{1,0:T(8,128)(2,1)S(1)} %collective-permute-done.2.refs_4_), channel_id=1, source_target_pairs={{0,16},{16,0},{1,17},{17,1},{2,18},{18,2},{3,19},{19,3},{4,20},{20... | collective-permute-start | bytes 344072 | tf_op jit(solution)/shard_map/ppermute | solution.py:397
  21.6 13.1 %collective-permute-start.5 = (bf16[16,3584]{1,0:T(8,128)(2,1)S(1)}, bf16[16,3584]{1,0:T(8,128)(2,1)S(1)}, u32[]{:S(2)}, u32[]{:S(2)}) collective-permute-start(bf16[16,3584]{1,0:T(8,128)(2,1)S(1)} %get-tuple-element.51), channel_id=1, source_target_pairs={{0,6},{1,7},{2,4},{3,5},{4,2},{5,3},{6,0},{7,1},{8,14},{9,15},{10,... | collective-permute-start | bytes 344072 | tf_op jit(solution)/shard_map/ppermute | solution.py:402
  25.0 11.6 %collective-permute-start.7 = (bf16[16,3584]{1,0:T(8,128)(2,1)S(1)}, bf16[16,3584]{1,0:T(8,128)(2,1)S(1)}, u32[]{:S(2)}, u32[]{:S(2)}) collective-permute-start(bf16[16,3584]{1,0:T(8,128)(2,1)S(1)} %get-tuple-element.54), channel_id=1, source_target_pairs={{0,8},{1,9},{2,10},{3,11},{4,12},{5,13},{6,14},{7,15},{8,0},{9,1},... | collective-permute-start | bytes 344072 | tf_op jit(solution)/shard_map/ppermute | solution.py:402
  27.1 6.0 %collective-permute-start.12 = (bf16[16,3584]{1,0:T(8,128)(2,1)S(1)}, bf16[16,3584]{1,0:T(8,128)(2,1)S(1)}, u32[]{:S(2)}, u32[]{:S(2)}) collective-permute-start(bf16[16,3584]{1,0:T(8,128)(2,1)S(1)} %collective-permute-done.3.refs_5_), channel_id=1, source_target_pairs={{0,16},{16,0},{1,17},{17,1},{2,18},{18,2},{3,19},{19,3},{4,20},{20... | collective-permute-start | bytes 344072 | tf_op jit(solution)/shard_map/ppermute | solution.py:397
  28.7 8.6 %collective-permute-start.10 = (bf16[16,3584]{1,0:T(8,128)(2,1)S(1)}, bf16[16,3584]{1,0:T(8,128)(2,1)S(1)}, u32[]{:S(2)}, u32[]{:S(2)}) collective-permute-start(bf16[16,3584]{1,0:T(8,128)(2,1)S(1)} %get-tuple-element.59), channel_id=1, source_target_pairs={{0,10},{1,11},{2,8},{3,9},{4,14},{5,15},{6,12},{7,13},{8,2},{9,3},... | collective-permute-start | bytes 344072 | tf_op jit(solution)/shard_map/ppermute | solution.py:402
  33.1 8.3 %collective-permute-start.16 = (bf16[16,3584]{1,0:T(8,128)(2,1)S(1)}, bf16[16,3584]{1,0:T(8,128)(2,1)S(1)}, u32[]{:S(2)}, u32[]{:S(2)}) collective-permute-start(bf16[16,3584]{1,0:T(8,128)(2,1)S(1)} %collective-permute-done.6.refs_9_), channel_id=1, source_target_pairs={{0,16},{16,0},{1,17},{17,1},{2,18},{18,2},{3,19},{19,3},{4,20},{20... | collective-permute-start | bytes 344072 | tf_op jit(solution)/shard_map/ppermute | solution.py:397
  34.7 8.8 %collective-permute-start.17 = (bf16[16,3584]{1,0:T(8,128)(2,1)S(1)}, bf16[16,3584]{1,0:T(8,128)(2,1)S(1)}, u32[]{:S(2)}, u32[]{:S(2)}) collective-permute-start(bf16[16,3584]{1,0:T(8,128)(2,1)S(1)} %collective-permute-done.8.refs_10_), channel_id=1, source_target_pairs={{0,16},{16,0},{1,17},{17,1},{2,18},{18,2},{3,19},{19,3},{4,20},{20... | collective-permute-start | bytes 344072 | tf_op jit(solution)/shard_map/ppermute | solution.py:397
  36.6 6.8 %collective-permute-start.13 = (bf16[16,3584]{1,0:T(8,128)(2,1)S(1)}, bf16[16,3584]{1,0:T(8,128)(2,1)S(1)}, u32[]{:S(2)}, u32[]{:S(2)}) collective-permute-start(bf16[16,3584]{1,0:T(8,128)(2,1)S(1)} %collective-permute-done.5.refs_6_), channel_id=1, source_target_pairs={{0,16},{16,0},{1,17},{17,1},{2,18},{18,2},{3,19},{19,3},{4,20},{20... | collective-permute-start | bytes 344072 | tf_op jit(solution)/shard_map/ppermute | solution.py:397
  37.3 7.7 %collective-permute-start.14 = (bf16[16,3584]{1,0:T(8,128)(2,1)S(1)}, bf16[16,3584]{1,0:T(8,128)(2,1)S(1)}, u32[]{:S(2)}, u32[]{:S(2)}) collective-permute-start(bf16[16,3584]{1,0:T(8,128)(2,1)S(1)} %collective-permute-done.7.refs_7_), channel_id=1, source_target_pairs={{0,16},{16,0},{1,17},{17,1},{2,18},{18,2},{3,19},{19,3},{4,20},{20... | collective-permute-start | bytes 344072 | tf_op jit(solution)/shard_map/ppermute | solution.py:397
  38.7 6.6 %collective-permute-start.15 = (bf16[16,3584]{1,0:T(8,128)(2,1)S(1)}, bf16[16,3584]{1,0:T(8,128)(2,1)S(1)}, u32[]{:S(2)}, u32[]{:S(2)}) collective-permute-start(bf16[16,3584]{1,0:T(8,128)(2,1)S(1)} %collective-permute-done.10.refs_8_), channel_id=1, source_target_pairs={{0,16},{16,0},{1,17},{17,1},{2,18},{18,2},{3,19},{19,3},{4,20},{20... | collective-permute-start | bytes 344072 | tf_op jit(solution)/shard_map/ppermute | solution.py:397
  41.4 19.5 %collective-permute-start.20 = (bf16[2,720,128]{2,1,0:T(8,128)(2,1)S(1)}, bf16[2,720,128]{2,1,0:T(8,128)(2,1)S(1)}, u32[]{:S(2)}, u32[]{:S(2)}) collective-permute-start(bf16[2,720,128]{2,1,0:T(8,128)(2,1)S(1)} %get-tuple-element.72), channel_id=1, source_target_pairs={{0,2},{1,3},{2,0},{3,1},{4,6},{5,7},{6,4},{7,5},{8,10},{9,11},{10,... | collective-permute-start | bytes 1105928 | tf_op jit(solution)/shard_map/ppermute | solution.py:402
  43.5 17.5 %collective-permute-start.21 = (bf16[2,720,128]{2,1,0:T(8,128)(2,1)S(1)}, bf16[2,720,128]{2,1,0:T(8,128)(2,1)S(1)}, u32[]{:S(2)}, u32[]{:S(2)}) collective-permute-start(bf16[2,720,128]{2,1,0:T(8,128)(2,1)S(1)} %get-tuple-element.73), channel_id=1, source_target_pairs={{0,4},{1,5},{2,6},{3,7},{4,0},{5,1},{6,2},{7,3},{8,12},{9,13},{10,... | collective-permute-start | bytes 1105928 | tf_op jit(solution)/shard_map/ppermute | solution.py:402
  43.5 17.5 %collective-permute-start.22 = (bf16[2,720,128]{2,1,0:T(8,128)(2,1)S(1)}, bf16[2,720,128]{2,1,0:T(8,128)(2,1)S(1)}, u32[]{:S(2)}, u32[]{:S(2)}) collective-permute-start(bf16[2,720,128]{2,1,0:T(8,128)(2,1)S(1)} %get-tuple-element.74), channel_id=1, source_target_pairs={{0,6},{1,7},{2,4},{3,5},{4,2},{5,3},{6,0},{7,1},{8,14},{9,15},{10,... | collective-permute-start | bytes 1105928 | tf_op jit(solution)/shard_map/ppermute | solution.py:402
  47.2 13.7 %collective-permute-start.18 = (bf16[128,512]{1,0:T(8,128)(2,1)S(1)}, bf16[128,512]{1,0:T(8,128)(2,1)S(1)}, u32[]{:S(2)}, u32[]{:S(2)}) collective-permute-start(bf16[128,512]{1,0:T(8,128)(2,1)S(1)} %get-tuple-element.64), channel_id=1, source_target_pairs={{0,16},{16,0},{1,17},{17,1},{2,18},{18,2},{3,19},{19,3},{4,20},{20... | collective-permute-start | bytes 393224 | tf_op jit(solution)/shard_map/ppermute | solution.py:397
  63.4 7.9 %collective-permute-start.23 = (bf16[96,224]{1,0:T(8,128)(2,1)S(1)}, bf16[96,224]{1,0:T(8,128)(2,1)S(1)}, u32[]{:S(2)}, u32[]{:S(2)}) collective-permute-start(bf16[96,224]{1,0:T(8,128)(2,1)S(1)} %get-tuple-element.80), channel_id=1, source_target_pairs={{0,24},{1,25},{2,26},{3,27},{4,28},{5,29},{6,30},{7,31},{8,16},{9,... | collective-permute-start | bytes 129032 | tf_op jit(solution)/shard_map/ppermute | solution.py:407
  64.4 6.8 %collective-permute-start.24 = (bf16[96,224]{1,0:T(8,128)(2,1)S(1)}, bf16[96,224]{1,0:T(8,128)(2,1)S(1)}, u32[]{:S(2)}, u32[]{:S(2)}) collective-permute-start(bf16[96,224]{1,0:T(8,128)(2,1)S(1)} %get-tuple-element.81), channel_id=1, source_target_pairs={{0,8},{1,9},{2,10},{3,11},{4,12},{5,13},{6,14},{7,15},{8,0},{9,1},... | collective-permute-start | bytes 129032 | tf_op jit(solution)/shard_map/ppermute | solution.py:407
  66.4 4.9 %collective-permute-start.25 = (bf16[96,224]{1,0:T(8,128)(2,1)S(1)}, bf16[96,224]{1,0:T(8,128)(2,1)S(1)}, u32[]{:S(2)}, u32[]{:S(2)}) collective-permute-start(bf16[96,224]{1,0:T(8,128)(2,1)S(1)} %get-tuple-element.82), channel_id=1, source_target_pairs={{0,16},{1,17},{2,18},{3,19},{4,20},{5,21},{6,22},{7,23},{8,24},{9,... | collective-permute-start | bytes 129032 | tf_op jit(solution)/shard_map/ppermute | solution.py:407

commit v4 on v3

--- a/solution.py
+++ b/solution.py
@@ -112,24 +112,29 @@
     return (hidden_grad, logit_grad, router_grad)
 
 
-HINT = {
-    "pack_own": 1 << 28, "pack": 1 << 28, "first": 1 << 33, "join": 1 << 20, "merge": 1 << 10,
-    "grads_own": 40 << 28, "grads_other": 400 << 28, "prepare": 1 << 33, "panel": 1 << 28,
-    "hidden": 1 << 24,
-}
-ORDER = (
-    ("send", 0), ("forward", (0,)), ("send", 6), ("send", 1), ("send", 2), ("send", 7), ("send", 3),
-    ("forward", (1,)), ("forward", (2,)), ("send", 4), ("first", 0), ("send", 5), ("forward", (3,)),
-    ("forward", (6,)), ("forward", (7,)), ("forward", (4,)), ("forward", (5,)),
-)
-SEND = {
-    7: (("own", 1),), 3: (("own", 2), ("other", 0)), 4: (("own", 6), ("other", 0)),
-    5: (("own", 7), ("other", 1), ("first", 0)),
-}
-FORWARD = {}
-FIRST = (("block", 0),)
+HINT = {'pack_own': 1073741824,
+ 'pack': 1073741824,
+ 'first': 34359738368,
+ 'join': 1048576,
+ 'merge': 1024,
+ 'grads_own': 10737418240,
+ 'grads_other': 107374182400,
+ 'prepare': 8589934592,
+ 'panel': 16777216,
+ 'hidden': 16777216}
+ORDER = (('send', 0), ('first', 0), ('forward', (0,)), ('send', 6), ('send', 1), ('send', 2), ('send', 7),
+ ('send', 3), ('forward', (1,)), ('forward', (2,)), ('send', 4), ('send', 5), ('forward', (3,)),
+ ('forward', (6,)), ('forward', (7,)), ('forward', (4,)), ('forward', (5,)))
+SEND = {7: (('own', 1), ('got', 0)),
+ 3: (('own', 2),),
+ 4: (('own', 6), ('other', 0)),
+ 5: (('own', 7), ('other', 1), ('got', 0), ('saved', 0)),
+ 2: (('other', 0),)}
+FORWARD = {7: (('first', 0),)}
+FIRST = (('block', 0),)
 SAVED = ()
-MERGE = (("own", 5),)
+PARCEL = ()
+MERGE = (('own', 5),)
 
 
 NT = (((1,), (1,)), ((), ()))
@@ -287,9 +292,10 @@
     line_ref[...] = finish_grads(place_ref[1], grads, saved_ref, grads_ref, cap)
 
 
-def grads_other_body(place_ref, saved_ref, weight_ref, line_own_ref, gate_ref, *refs, cap):
+def grads_other_body(place_ref, saved_ref, weight_ref, line_own_ref, gate_ref, *refs, cap, spots):
     pieces, (grads_ref, message_ref) = refs[:-2], refs[-2:]
-    rows = jnp.concatenate([p[...] for p in pieces], axis=0)
+    size = 2 * cap
+    rows = jnp.concatenate([pieces[g][k * size : (k + 1) * size] for g, k in spots], axis=0)
     grads = lax.dot_general(rows, weight_ref[...], NT, preferred_element_type=jnp.float32)
     other = finish_grads(place_ref[1], grads, saved_ref, grads_ref, cap)
     own = line_own_ref[...]
@@ -481,17 +487,18 @@
         )
         known["first", 0] = outs[2]
         known["results", 0] = outs
+        known["saved", 0] = over_dp(held(outs[4], SAVED))
+        known["got", 0] = over_expert(held(outs[6], PARCEL), 1)
 
     for kind, which in ORDER:
         {"send": send, "forward": forward, "first": lambda _: first()}[kind](which)
-    z, a, slot_gates, saved_own, saved_other, parcel_keep, parcel_send = known["results", 0]
+    z, a, slot_gates, saved_own, _, parcel_keep, _ = known["results", 0]
     own = [known["own", q] for q in range(8)]
     groups = [which for kind, which in ORDER if kind == "forward"]
-    arrival = [q for members in sorted(groups) for q in members]
-    other = [known["other", members[0]] for members in sorted(groups)]
-    assert arrival == list(range(8))
-    saved_other = over_dp(held(saved_other, SAVED))
-    parcel_got = over_expert(parcel_send, 1)
+    other = [known["other", members[0]] for members in groups]
+    found = {q: (g, k) for g, members in enumerate(groups) for k, q in enumerate(members)}
+    spots = [found[q] for q in range(8)]
+    saved_other, parcel_got = known["saved", 0], known["got", 0]
     merged = kernel_call(
         merge_body, (parcel_shape(2),) * 3, "merge", HINT["merge"], 4 << 20,
         held(parcel_keep, MERGE), parcel_got,
@@ -503,7 +510,7 @@
         "grads_own", HINT["grads_own"], 5 << 20, place, saved_own, weight, *own,
     )
     grads_other, message = kernel_call(
-        lambda *refs: grads_other_body(*refs, cap=cap),
+        lambda *refs: grads_other_body(*refs, cap=cap, spots=spots),
         (
             jax.ShapeDtypeStruct((slots, half), bf16),
             jax.ShapeDtypeStruct((2 * flight, 2, slots), f32),

time: 72.1 us -> 68.3 us (0.947)
  waiting for transfers between devices: 11.2 us -> 3.16 us
  starting transfers between devices: 33.6 us -> 40.1 us
  blocking collectives: 12.6 us -> 10.3 us
    ppermute x13, waiting for transfers between devices: 5.73 us -> 0.78 us  [over_expert(): return lax.ppermute(value, 'expert', [(k, k ^ bits) for k in range(count)])]
    ppermute x13, starting transfers between devices: 18.3 us -> 22.1 us  [over_expert(): return lax.ppermute(value, 'expert', [(k, k ^ bits) for k in range(count)])]
    ppermute x10, waiting for transfers between devices: 3.62 us -> 0.03 us  [over_dp(): return lax.ppermute(value, 'dp', [(0, 1), (1, 0)])]
    ppermute x10, starting transfers between devices: 10.9 us -> 13.6 us  [over_dp(): return lax.ppermute(value, 'dp', [(0, 1), (1, 0)])]
    all_to_all x1, blocking collectives: 12.6 us -> 10.3 us  [paired_local(): message = lax.all_to_all(message, ('dp', 'expert'), 0, 0, tiled=True)]
  transfers between devices with their start and end apart: 26 -> 26, of which waited for: 7 -> 3; matrix products, arithmetic and copies ran while one was open for 0% -> 0% of each run, Pallas kernels for 9% -> 10%
where the time goes in v4:
time: 68.3 us; the launch traced here: 68.1 us
  starting transfers between devices  40.1 us (59%)
  Pallas kernels  11.1 us (16%)
  blocking collectives  10.3 us (15%)
  waiting for transfers between devices  3.16 us (5%)
  local copies, waits for them, and re-layouts  1.88 us (3%)
  between operations  0.77 us (1%)
  other arithmetic  0.74 us (1%)
    ppermute x13, starting transfers between devices, over_expert(): return lax.ppermute(value, 'expert', [(k, k ^ bits) for k in range(count)])  22.1 us
    ppermute x10, starting transfers between devices, over_dp(): return lax.ppermute(value, 'dp', [(0, 1), (1, 0)])  13.6 us
    pallas_call x9, Pallas kernels, kernel_call(): pl.pallas_call(body, out_shape=out_shape, in_specs=[pl.BlockSpec(memory_s...  11.1 us
    all_to_all x1, blocking collectives, paired_local(): message = lax.all_to_all(message, ('dp', 'expert'), 0, 0, tiled=True)  10.3 us
    ppermute x3, starting transfers between devices, over_both(): lax.ppermute(value, ('dp', 'expert'), [(k, k ^ dp_bit * count + bits) for...  4.39 us
    ppermute x3, waiting for transfers between devices, over_both(): lax.ppermute(value, ('dp', 'expert'), [(k, k ^ dp_bit * count + bits) for...  2.34 us
    unnamed x12, local copies, waits for them, and re-layouts  1.88 us
  transfers between devices with their start and end apart: 26, of which 3 were waited for; matrix products, arithmetic and copies ran while one was open for 0% of the time, Pallas kernels for 10%

profile of v4, /device:TPU:0, one launch (start us, length us, event | category | flops | bytes accessed | tf_op | source)
XLA Modules:
  0.0 68.1 jit_solution(3428926054993483949)
XLA Ops:
  0.6 0.5 collective-permute-start.1
  1.1 0.1 collective-permute-start
  1.2 0.1 pad_add_fusion.refs_0_
  1.3 1.2 %copy-done.1 = bf16[128,3584]{1,0:T(8,128)(2,1)S(1)} copy-done((bf16[128,3584]{1,0:T(8,128)(2,1)S(1)}, bf16[128,3584]{1,0:T(8,128)(2,1)}, u32[]{:S(2)}) %copy-start.1) | copy-done | bytes 917528
  2.5 0.7 %copy-done.5 = s32[128,8]{0,1:T(8,128)S(1)} copy-done((s32[128,8]{0,1:T(8,128)S(1)}, s32[128,8]{0,1:T(8,128)}, u32[]{:S(2)}) %copy-start.5) | copy-done | bytes 4120
  3.2 0.9 %pack_own.1.refs_1_ = f32[64,3584]{1,0:T(8,128)S(1)} custom-call(s32[2]{0:T(128)S(1)} %pad_add_fusion.refs_0_, s32[8,128]{1,0:T(8,128)S(1)} %bitcast.15, bf16[128,3584]{1,0:T(8,128)(2,1)S(1)} %copy-done.1), custom_call_target="tpu_custom_call" | custom-call | flops 1073741824 | bytes 3145728 | tf_op jit(solution)/shard_map/pack_own/pallas_call | solution.py:150
  4.1 0.0 collective-permute-done.refs_2_
  4.1 0.0 collective-permute-done.1.refs_3_
  4.1 0.9 %pack.1 = (bf16[16,3584]{1,0:T(8,128)(2,1)S(1)}, bf16[16,3584]{1,0:T(8,128)(2,1)S(1)}, bf16[16,3584]{1,0:T(8,128)(2,1)S(1)}, bf16[16,3584]{1,0:T(8,128)(2,1)S(1)...) custom-call(s32[2]{0:T(128)S(1)} %pad_add_fusion.refs_0_, ...), custom_call_target="tpu_custom_call" | custom-call | flops 1073741824 | bytes 3145728 | tf_op jit(solution)/shard_map/pack/pallas_call | solution.py:150
  5.1 0.0 copy-start
  5.1 1.2 %first.1 = (f32[192,128]{1,0:T(8,128)S(1)}, f32[192,128]{1,0:T(8,128)S(1)}, f32[16,128]{1,0:T(8,128)S(1)}, bf16[128,512]{1,0:T(8,128)(2,1)S(1)}, bf16[128,512]{1...) custom-call(s32[2]{0:T(128)S(1)} %pad_add_fusion.refs_0_, ...), custom_call_target="tpu_custom_call" | custom-call | flops 34359738368 | bytes 3145728 | tf_op jit(solution)/shard_map/first/pallas_call | solution.py:150
  6.4 0.5 collective-permute-start.8
  6.8 2.6 %collective-permute-start.3 = (bf16[16,3584]{1,0:T(8,128)(2,1)S(1)}, bf16[16,3584]{1,0:T(8,128)(2,1)S(1)}, u32[]{:S(2)}, u32[]{:S(2)}) collective-permute-start(bf16[16,3584]{1,0:T(8,128)(2,1)S(1)} %get-tuple-element.45.refs_3_), channel_id=1, source_target_pairs={{0,16},{16,0},{1,17},{17,1},{2,18},{18,2},{3,19},{19,3},{4,20},{20... | collective-permute-start | bytes 344072 | tf_op jit(solution)/shard_map/ppermute | solution.py:403
  9.4 1.5 %collective-permute-start.2 = (bf16[16,3584]{1,0:T(8,128)(2,1)S(1)}, bf16[16,3584]{1,0:T(8,128)(2,1)S(1)}, u32[]{:S(2)}, u32[]{:S(2)}) collective-permute-start(bf16[16,3584]{1,0:T(8,128)(2,1)S(1)} %get-tuple-element.50), channel_id=1, source_target_pairs={{0,2},{1,3},{2,0},{3,1},{4,6},{5,7},{6,4},{7,5},{8,10},{9,11},{10,... | collective-permute-start | bytes 344072 | tf_op jit(solution)/shard_map/ppermute | solution.py:408
  10.9 0.5 collective-permute-start.11
  11.5 3.6 %collective-permute-start.6 = (bf16[16,3584]{1,0:T(8,128)(2,1)S(1)}, bf16[16,3584]{1,0:T(8,128)(2,1)S(1)}, u32[]{:S(2)}, u32[]{:S(2)}) collective-permute-start(bf16[16,3584]{1,0:T(8,128)(2,1)S(1)} %get-tuple-element.56), channel_id=1, source_target_pairs={{0,12},{1,13},{2,14},{3,15},{4,8},{5,9},{6,10},{7,11},{8,4},{9,5},... | collective-permute-start | bytes 344072 | tf_op jit(solution)/shard_map/ppermute | solution.py:408
  15.1 0.0 collective-permute-done.3.refs_5_
  15.1 0.0 collective-permute-start.4
  15.1 0.0 collective-permute-done.2.refs_4_
  15.1 1.9 %collective-permute-start.10 = (bf16[16,3584]{1,0:T(8,128)(2,1)S(1)}, bf16[16,3584]{1,0:T(8,128)(2,1)S(1)}, u32[]{:S(2)}, u32[]{:S(2)}) collective-permute-start(bf16[16,3584]{1,0:T(8,128)(2,1)S(1)} %collective-permute-done.2.refs_4_), channel_id=1, source_target_pairs={{0,16},{16,0},{1,17},{17,1},{2,18},{18,2},{3,19},{19,3},{4,20},{20... | collective-permute-start | bytes 344072 | tf_op jit(solution)/shard_map/ppermute | solution.py:403
  16.9 0.0 collective-permute-done.8.got_ref.refs_1_.refs_7_
  17.0 3.4 %collective-permute-start.9 = (bf16[16,3584]{1,0:T(8,128)(2,1)S(1)}, bf16[16,3584]{1,0:T(8,128)(2,1)S(1)}, u32[]{:S(2)}, u32[]{:S(2)}) collective-permute-start(bf16[16,3584]{1,0:T(8,128)(2,1)S(1)} %get-tuple-element.61), channel_id=1, source_target_pairs={{0,14},{1,15},{2,12},{3,13},{4,10},{5,11},{6,8},{7,9},{8,6},{9,7},... | collective-permute-start | bytes 344072 | tf_op jit(solution)/shard_map/ppermute | solution.py:408
  20.4 0.0 collective-permute-done.6.refs_9_
  20.4 0.2 collective-permute-start.7
  20.6 0.0 collective-permute-done.4.refs_5_
  20.6 2.7 %collective-permute-start.5 = (bf16[16,3584]{1,0:T(8,128)(2,1)S(1)}, bf16[16,3584]{1,0:T(8,128)(2,1)S(1)}, u32[]{:S(2)}, u32[]{:S(2)}) collective-permute-start(bf16[16,3584]{1,0:T(8,128)(2,1)S(1)} %get-tuple-element.54), channel_id=1, source_target_pairs={{0,6},{1,7},{2,4},{3,5},{4,2},{5,3},{6,0},{7,1},{8,14},{9,15},{10,... | collective-permute-start | bytes 344072 | tf_op jit(solution)/shard_map/ppermute | solution.py:408
  23.3 0.0 collective-permute-done.11.refs_1_
  23.3 1.5 %collective-permute-start.15 = (bf16[16,3584]{1,0:T(8,128)(2,1)S(1)}, bf16[16,3584]{1,0:T(8,128)(2,1)S(1)}, u32[]{:S(2)}, u32[]{:S(2)}) collective-permute-start(bf16[16,3584]{1,0:T(8,128)(2,1)S(1)} %collective-permute-done.6.refs_9_), channel_id=1, source_target_pairs={{0,16},{16,0},{1,17},{17,1},{2,18},{18,2},{3,19},{19,3},{4,20},{20... | collective-permute-start | bytes 344072 | tf_op jit(solution)/shard_map/ppermute | solution.py:403
  24.8 0.0 collective-permute-done.10.refs_6_
  24.8 0.8 %collective-permute-done.9.refs_10_ = bf16[16,3584]{1,0:T(8,128)(2,1)S(1)} collective-permute-done((bf16[16,3584]{1,0:T(8,128)(2,1)S(1)}, bf16[16,3584]{1,0:T(8,128)(2,1)S(1)}, u32[]{:S(2)}, u32[]{:S(2)}) %collective-permute-start.9) | collective-permute-done | bytes 114720 | tf_op jit(solution)/shard_map/ppermute | solution.py:408
  25.6 6.0 %collective-permute-start.12 = (bf16[16,3584]{1,0:T(8,128)(2,1)S(1)}, bf16[16,3584]{1,0:T(8,128)(2,1)S(1)}, u32[]{:S(2)}, u32[]{:S(2)}) collective-permute-start(bf16[16,3584]{1,0:T(8,128)(2,1)S(1)} %get-tuple-element.63), channel_id=1, source_target_pairs={{0,10},{1,11},{2,8},{3,9},{4,14},{5,15},{6,12},{7,13},{8,2},{9,3},... | collective-permute-start | bytes 344072 | tf_op jit(solution)/shard_map/ppermute | solution.py:408
  31.6 1.8 %collective-permute-start.13 = (bf16[16,3584]{1,0:T(8,128)(2,1)S(1)}, bf16[16,3584]{1,0:T(8,128)(2,1)S(1)}, u32[]{:S(2)}, u32[]{:S(2)}) collective-permute-start(bf16[16,3584]{1,0:T(8,128)(2,1)S(1)} %collective-permute-done.4.refs_5_), channel_id=1, source_target_pairs={{0,16},{16,0},{1,17},{17,1},{2,18},{18,2},{3,19},{19,3},{4,20},{20... | collective-permute-start | bytes 344072 | tf_op jit(solution)/shard_map/ppermute | solution.py:403
  33.3 0.0 collective-permute-done.7.refs_7_
  33.3 0.3 collective-permute-start.17
  33.6 0.0 collective-permute-done.5.refs_6_
  33.6 1.8 %collective-permute-start.14 = (bf16[16,3584]{1,0:T(8,128)(2,1)S(1)}, bf16[16,3584]{1,0:T(8,128)(2,1)S(1)}, u32[]{:S(2)}, u32[]{:S(2)}) collective-permute-start(bf16[16,3584]{1,0:T(8,128)(2,1)S(1)} %collective-permute-done.5.refs_6_), channel_id=1, source_target_pairs={{0,16},{16,0},{1,17},{17,1},{2,18},{18,2},{3,19},{19,3},{4,20},{20... | collective-permute-start | bytes 344072 | tf_op jit(solution)/shard_map/ppermute | solution.py:403
  35.3 0.0 collective-permute-done.15.refs_9_
  35.4 0.3 collective-permute-start.16
  35.6 0.0 collective-permute-done.12.refs_8_
  35.6 1.8 %collective-permute-start.18 = (bf16[16,3584]{1,0:T(8,128)(2,1)S(1)}, bf16[16,3584]{1,0:T(8,128)(2,1)S(1)}, u32[]{:S(2)}, u32[]{:S(2)}) collective-permute-start(bf16[16,3584]{1,0:T(8,128)(2,1)S(1)} %collective-permute-done.12.refs_8_), channel_id=1, source_target_pairs={{0,16},{16,0},{1,17},{17,1},{2,18},{18,2},{3,19},{19,3},{4,20},{20... | collective-permute-start | bytes 344072 | tf_op jit(solution)/shard_map/ppermute | solution.py:403
  37.4 2.0 %grads_own.1 = (f32[128,512]{1,0:T(8,128)S(1)}, f32[1,128]{1,0:T(1,128)S(1)}) custom-call(s32[2]{0:T(128)S(1)} %pad_add_fusion.refs_0_, bf16[128,512]{1,0:T(8,128)(2,1)S(1)} %get-tuple-element.49.refs_1_, bf16[512,3584]{1,0:T(8,128)(2,1)S(1)} %bitcast.10, bf16[16,3584]{1,0:T(8,128)(2,1)S(1)} %get-tuple-element.45.refs_3_, ...), custom_call_target="tpu_custom_call" | custom-call | flops 10737418240 | bytes 5242880 | tf_op jit(solution)/shard_map/grads_own/pallas_call | solution.py:150
  39.4 0.1 merge.1
  39.4 0.0 collective-permute-done.13.refs_7_
  39.4 0.6 collective-permute-start.20
  40.0 0.0 collective-permute-done.17.refs_11_
  40.0 0.7 %collective-permute-start.21 = (bf16[2,720,128]{2,1,0:T(8,128)(2,1)S(1)}, bf16[2,720,128]{2,1,0:T(8,128)(2,1)S(1)}, u32[]{:S(2)}, u32[]{:S(2)}) collective-permute-start(bf16[2,720,128]{2,1,0:T(8,128)(2,1)S(1)} %get-tuple-element.77), channel_id=1, source_target_pairs={{0,4},{1,5},{2,6},{3,7},{4,0},{5,1},{6,2},{7,3},{8,12},{9,13},{10,... | collective-permute-start | bytes 1105928 | tf_op jit(solution)/shard_map/ppermute | solution.py:408
  40.8 0.0 collective-permute-done.14.refs_8_
  40.8 2.2 %collective-permute-start.22 = (bf16[2,720,128]{2,1,0:T(8,128)(2,1)S(1)}, bf16[2,720,128]{2,1,0:T(8,128)(2,1)S(1)}, u32[]{:S(2)}, u32[]{:S(2)}) collective-permute-start(bf16[2,720,128]{2,1,0:T(8,128)(2,1)S(1)} %get-tuple-element.78), channel_id=1, source_target_pairs={{0,6},{1,7},{2,4},{3,5},{4,2},{5,3},{6,0},{7,1},{8,14},{9,15},{10,... | collective-permute-start | bytes 1105928 | tf_op jit(solution)/shard_map/ppermute | solution.py:408
  43.0 0.0 collective-permute-done.16.refs_10_
  43.0 0.0 collective-permute-done.18.refs_12_
  43.0 2.0 %grads_other.1 = (bf16[128,512]{1,0:T(8,128)(2,1)S(1)}, f32[32,2,128]{2,1,0:T(2,128)S(1)}) custom-call(s32[2]{0:T(128)S(1)} %pad_add_fusion.refs_0_, bf16[128,512]{1,0:T(8,128)(2,1)S(1)} %collective-permute-done.11.refs_1_, bf16[512,3584]{1,0:T(8,128)(2,1)S(1)} %bitcast.11, f32[1,128]{1,0:T(1,128)S(1)} %get-tuple-element.65.refs_3_, ...), custom_call_target="tpu_custom_call" | custom-call | flops 107374182400 | bytes 5242880 | tf_op jit(solution)/shard_map/grads_other/pallas_call | solution.py:150
  45.0 1.4 %collective-permute-start.19 = (bf16[128,512]{1,0:T(8,128)(2,1)S(1)}, bf16[128,512]{1,0:T(8,128)(2,1)S(1)}, u32[]{:S(2)}, u32[]{:S(2)}) collective-permute-start(bf16[128,512]{1,0:T(8,128)(2,1)S(1)} %get-tuple-element.69), channel_id=1, source_target_pairs={{0,16},{16,0},{1,17},{17,1},{2,18},{18,2},{3,19},{19,3},{4,20},{20... | collective-permute-start | bytes 393224 | tf_op jit(solution)/shard_map/ppermute | solution.py:403
  46.3 10.3 %all_to_all.5.refs_3_ = f32[32,2,128]{2,1,0:T(2,128)S(1)} all-to-all(f32[32,2,128]{2,1,0:T(2,128)S(1)} %get-tuple-element.68), channel_id=1, replica_groups=mesh['dp'=2,'expert'=16] {'dp','expert'}, dimensions={0} | all-to-all | bytes 65536 | tf_op jit(solution)/shard_map/all_to_all | solution.py:522
  56.6 0.0 collective-permute-done.19.refs_2_
  56.6 0.0 collective-permute-done.22.refs_4_.refs_10_
  56.6 0.4 prepare.1
  57.1 1.9 %panel.1 = (f32[192,128]{1,0:T(8,128)}, f32[96,224]{1,0:T(8,128)S(1)}, bf16[96,224]{1,0:T(8,128)(2,1)S(1)}, bf16[96,224]{1,0:T(8,128)(2,1)S(1)}, bf16[96,224]{1,0:T(8,128)(2,1)S(1)}) custom-call(s32[2]{0:T(128)S(1)} %pad_add_fusion.refs_0_, f32[192,128]{1,0:T(8,128)S(1)} %get-tuple-element.72.refs_1_, f32[192,128]{1,0:T(8,128)S(1)} %get-tuple-element.73.refs_2_, ...), custom_call_target="tpu_custom_call" | custom-call | flops 16777216 | bytes 4194304 | tf_op jit(solution)/shard_map/panel/pallas_call | solution.py:150
  59.0 1.2 %collective-permute-start.25 = (bf16[96,224]{1,0:T(8,128)(2,1)S(1)}, bf16[96,224]{1,0:T(8,128)(2,1)S(1)}, u32[]{:S(2)}, u32[]{:S(2)}) collective-permute-start(bf16[96,224]{1,0:T(8,128)(2,1)S(1)} %get-tuple-element.86), channel_id=1, source_target_pairs={{0,16},{1,17},{2,18},{3,19},{4,20},{5,21},{6,22},{7,23},{8,24},{9,... | collective-permute-start | bytes 129032 | tf_op jit(solution)/shard_map/ppermute | solution.py:413
  60.2 0.6 collective-permute-start.24
  60.8 2.6 %collective-permute-start.23 = (bf16[96,224]{1,0:T(8,128)(2,1)S(1)}, bf16[96,224]{1,0:T(8,128)(2,1)S(1)}, u32[]{:S(2)}, u32[]{:S(2)}) collective-permute-start(bf16[96,224]{1,0:T(8,128)(2,1)S(1)} %get-tuple-element.84), channel_id=1, source_target_pairs={{0,24},{1,25},{2,26},{3,27},{4,28},{5,29},{6,30},{7,31},{8,16},{9,... | collective-permute-start | bytes 129032 | tf_op jit(solution)/shard_map/ppermute | solution.py:413
  63.4 1.6 %hidden.1 = bf16[128,1024]{1,0:T(8,128)(2,1)} custom-call(s32[2]{0:T(128)S(1)} %pad_add_fusion.refs_0_, f32[128,512]{1,0:T(8,128)S(1)} %get-tuple-element.64.refs_1_, bf16[128,512]{1,0:T(8,128)(2,1)S(1)} %collective-permute-done.19.refs_2_, f32[32,2,128]{2,1,0:T(2,128)S(1)} %all_to_all.5.refs_3_), custom_call_target="tpu_custom_call" | custom-call | flops 16777216 | bytes 1048576 | tf_op jit(solution)/shard_map/hidden/pallas_call | solution.py:150
  65.1 1.5 %collective-permute-done.24 = bf16[96,224]{1,0:T(8,128)(2,1)S(1)} collective-permute-done((bf16[96,224]{1,0:T(8,128)(2,1)S(1)}, bf16[96,224]{1,0:T(8,128)(2,1)S(1)}, u32[]{:S(2)}, u32[]{:S(2)}) %collective-permute-start.24) | collective-permute-done | bytes 43040 | tf_op jit(solution)/shard_map/ppermute | solution.py:413
  66.6 0.8 %collective-permute-done.23 = bf16[96,224]{1,0:T(8,128)(2,1)S(1)} collective-permute-done((bf16[96,224]{1,0:T(8,128)(2,1)S(1)}, bf16[96,224]{1,0:T(8,128)(2,1)S(1)}, u32[]{:S(2)}, u32[]{:S(2)}) %collective-permute-start.23) | collective-permute-done | bytes 43040 | tf_op jit(solution)/shard_map/ppermute | solution.py:413
  67.4 0.7 add_bitcast_fusion
  (12 shorter events, 0.0 us)
Async XLA Ops:
  0.6 3.5 %collective-permute-start.1 = (bf16[128,3584]{1,0:T(8,128)(2,1)}, bf16[128,3584]{1,0:T(8,128)(2,1)S(1)}, u32[]{:S(2)}, u32[]{:S(2)}) collective-permute-start(bf16[128,3584]{1,0:T(8,128)(2,1)} %refs_2_.1), channel_id=1, source_target_pairs={{0,1},{1,0},{2,3},{3,2},{4,5},{5,4},{6,7},{7,6},{8,9},{9,8},{10,11... | collective-permute-start | bytes 2752520 | tf_op jit(solution)/shard_map/ppermute | solution.py:408
  1.1 3.0 %collective-permute-start = (s32[8,128]{1,0:T(8,128)}, s32[8,128]{1,0:T(8,128)S(1)}, u32[]{:S(2)}, u32[]{:S(2)}) collective-permute-start(s32[8,128]{1,0:T(8,128)} %bitcast.14), channel_id=1, source_target_pairs={{0,1},{1,0},{2,3},{3,2},{4,5},{5,4},{6,7},{7,6},{8,9},{9,8},{10,11... | collective-permute-start | bytes 12296 | tf_op jit(solution)/shard_map/ppermute | solution.py:408
  1.3 1.2 %copy-start.1 = (bf16[128,3584]{1,0:T(8,128)(2,1)S(1)}, bf16[128,3584]{1,0:T(8,128)(2,1)}, u32[]{:S(2)}) copy-start(bf16[128,3584]{1,0:T(8,128)(2,1)} %refs_2_.1) | copy-start | bytes 2752516
  2.5 0.7 %copy-start.5 = (s32[128,8]{0,1:T(8,128)S(1)}, s32[128,8]{0,1:T(8,128)}, u32[]{:S(2)}) copy-start(s32[128,8]{0,1:T(8,128)} %param.9) | copy-start | bytes 12292
  3.2 1.9 %copy-start.2 = (bf16[128,3584]{1,0:T(8,128)(2,1)S(1)}, bf16[128,3584]{1,0:T(8,128)(2,1)}, u32[]{:S(2)}) copy-start(bf16[128,3584]{1,0:T(8,128)(2,1)} %refs_3_) | copy-start | bytes 2752516
  3.2 1.9 %copy-start.3 = (bf16[1,1,16,8,1024]{4,3,2,1,0:T(8,128)(2,1)S(1)}, bf16[1,1,16,8,1024]{4,3,2,1,0:T(8,128)(2,1)}, u32[]{:S(2)}) copy-start(bf16[1,1,16,8,1024]{4,3,2,1,0:T(8,128)(2,1)} %param.10) | copy-start | bytes 786436
  3.2 1.9 %copy-start.4 = (f32[128,192]{0,1:T(8,128)S(1)}, f32[128,192]{0,1:T(8,128)}, u32[]{:S(2)}) copy-start(f32[128,192]{0,1:T(8,128)} %param.8) | copy-start | bytes 294916
  5.1 32.3 %copy-start = (bf16[1,512,3584]{2,1,0:T(8,128)(2,1)S(1)}, bf16[1,512,3584]{2,1,0:T(8,128)(2,1)}, u32[]{:S(2)}) copy-start(bf16[1,512,3584]{2,1,0:T(8,128)(2,1)} %param.11) | copy-start | bytes 11010052
  6.4 10.6 %collective-permute-start.8 = (bf16[4,720,128]{2,1,0:T(8,128)(2,1)S(1)}, bf16[4,720,128]{2,1,0:T(8,128)(2,1)S(1)}, u32[]{:S(2)}, u32[]{:S(2)}) collective-permute-start(bf16[4,720,128]{2,1,0:T(8,128)(2,1)S(1)} %get-tuple-element.60), channel_id=1, source_target_pairs={{0,1},{1,0},{2,3},{3,2},{4,5},{5,4},{6,7},{7,6},{8,9},{9,8},{10,11... | collective-permute-start | bytes 2211848 | tf_op jit(solution)/shard_map/ppermute | solution.py:408
  6.8 8.2 %collective-permute-start.3 = (bf16[16,3584]{1,0:T(8,128)(2,1)S(1)}, bf16[16,3584]{1,0:T(8,128)(2,1)S(1)}, u32[]{:S(2)}, u32[]{:S(2)}) collective-permute-start(bf16[16,3584]{1,0:T(8,128)(2,1)S(1)} %get-tuple-element.45.refs_3_), channel_id=1, source_target_pairs={{0,16},{16,0},{1,17},{17,1},{2,18},{18,2},{3,19},{19,3},{4,20},{20... | collective-permute-start | bytes 344072 | tf_op jit(solution)/shard_map/ppermute | solution.py:403
  9.4 5.7 %collective-permute-start.2 = (bf16[16,3584]{1,0:T(8,128)(2,1)S(1)}, bf16[16,3584]{1,0:T(8,128)(2,1)S(1)}, u32[]{:S(2)}, u32[]{:S(2)}) collective-permute-start(bf16[16,3584]{1,0:T(8,128)(2,1)S(1)} %get-tuple-element.50), channel_id=1, source_target_pairs={{0,2},{1,3},{2,0},{3,1},{4,6},{5,7},{6,4},{7,5},{8,10},{9,11},{10,... | collective-permute-start | bytes 344072 | tf_op jit(solution)/shard_map/ppermute | solution.py:408
  10.9 12.4 %collective-permute-start.11 = (bf16[128,512]{1,0:T(8,128)(2,1)S(1)}, bf16[128,512]{1,0:T(8,128)(2,1)S(1)}, u32[]{:S(2)}, u32[]{:S(2)}) collective-permute-start(bf16[128,512]{1,0:T(8,128)(2,1)S(1)} %get-tuple-element.62), channel_id=1, source_target_pairs={{0,16},{16,0},{1,17},{17,1},{2,18},{18,2},{3,19},{19,3},{4,20},{20... | collective-permute-start | bytes 393224 | tf_op jit(solution)/shard_map/ppermute | solution.py:403
  11.5 8.9 %collective-permute-start.6 = (bf16[16,3584]{1,0:T(8,128)(2,1)S(1)}, bf16[16,3584]{1,0:T(8,128)(2,1)S(1)}, u32[]{:S(2)}, u32[]{:S(2)}) collective-permute-start(bf16[16,3584]{1,0:T(8,128)(2,1)S(1)} %get-tuple-element.56), channel_id=1, source_target_pairs={{0,12},{1,13},{2,14},{3,15},{4,8},{5,9},{6,10},{7,11},{8,4},{9,5},... | collective-permute-start | bytes 344072 | tf_op jit(solution)/shard_map/ppermute | solution.py:408
  15.1 5.5 %collective-permute-start.4 = (bf16[16,3584]{1,0:T(8,128)(2,1)S(1)}, bf16[16,3584]{1,0:T(8,128)(2,1)S(1)}, u32[]{:S(2)}, u32[]{:S(2)}) collective-permute-start(bf16[16,3584]{1,0:T(8,128)(2,1)S(1)} %get-tuple-element.52), channel_id=1, source_target_pairs={{0,4},{1,5},{2,6},{3,7},{4,0},{5,1},{6,2},{7,3},{8,12},{9,13},{10,... | collective-permute-start | bytes 344072 | tf_op jit(solution)/shard_map/ppermute | solution.py:408
  15.1 9.7 %collective-permute-start.10 = (bf16[16,3584]{1,0:T(8,128)(2,1)S(1)}, bf16[16,3584]{1,0:T(8,128)(2,1)S(1)}, u32[]{:S(2)}, u32[]{:S(2)}) collective-permute-start(bf16[16,3584]{1,0:T(8,128)(2,1)S(1)} %collective-permute-done.2.refs_4_), channel_id=1, source_target_pairs={{0,16},{16,0},{1,17},{17,1},{2,18},{18,2},{3,19},{19,3},{4,20},{20... | collective-permute-start | bytes 344072 | tf_op jit(solution)/shard_map/ppermute | solution.py:403
  17.0 8.6 %collective-permute-start.9 = (bf16[16,3584]{1,0:T(8,128)(2,1)S(1)}, bf16[16,3584]{1,0:T(8,128)(2,1)S(1)}, u32[]{:S(2)}, u32[]{:S(2)}) collective-permute-start(bf16[16,3584]{1,0:T(8,128)(2,1)S(1)} %get-tuple-element.61), channel_id=1, source_target_pairs={{0,14},{1,15},{2,12},{3,13},{4,10},{5,11},{6,8},{7,9},{8,6},{9,7},... | collective-permute-start | bytes 344072 | tf_op jit(solution)/shard_map/ppermute | solution.py:408
  20.4 12.9 %collective-permute-start.7 = (bf16[16,3584]{1,0:T(8,128)(2,1)S(1)}, bf16[16,3584]{1,0:T(8,128)(2,1)S(1)}, u32[]{:S(2)}, u32[]{:S(2)}) collective-permute-start(bf16[16,3584]{1,0:T(8,128)(2,1)S(1)} %get-tuple-element.57), channel_id=1, source_target_pairs={{0,8},{1,9},{2,10},{3,11},{4,12},{5,13},{6,14},{7,15},{8,0},{9,1},... | collective-permute-start | bytes 344072 | tf_op jit(solution)/shard_map/ppermute | solution.py:408
  20.6 13.0 %collective-permute-start.5 = (bf16[16,3584]{1,0:T(8,128)(2,1)S(1)}, bf16[16,3584]{1,0:T(8,128)(2,1)S(1)}, u32[]{:S(2)}, u32[]{:S(2)}) collective-permute-start(bf16[16,3584]{1,0:T(8,128)(2,1)S(1)} %get-tuple-element.54), channel_id=1, source_target_pairs={{0,6},{1,7},{2,4},{3,5},{4,2},{5,3},{6,0},{7,1},{8,14},{9,15},{10,... | collective-permute-start | bytes 344072 | tf_op jit(solution)/shard_map/ppermute | solution.py:408
  23.3 12.0 %collective-permute-start.15 = (bf16[16,3584]{1,0:T(8,128)(2,1)S(1)}, bf16[16,3584]{1,0:T(8,128)(2,1)S(1)}, u32[]{:S(2)}, u32[]{:S(2)}) collective-permute-start(bf16[16,3584]{1,0:T(8,128)(2,1)S(1)} %collective-permute-done.6.refs_9_), channel_id=1, source_target_pairs={{0,16},{16,0},{1,17},{17,1},{2,18},{18,2},{3,19},{19,3},{4,20},{20... | collective-permute-start | bytes 344072 | tf_op jit(solution)/shard_map/ppermute | solution.py:403
  25.6 10.0 %collective-permute-start.12 = (bf16[16,3584]{1,0:T(8,128)(2,1)S(1)}, bf16[16,3584]{1,0:T(8,128)(2,1)S(1)}, u32[]{:S(2)}, u32[]{:S(2)}) collective-permute-start(bf16[16,3584]{1,0:T(8,128)(2,1)S(1)} %get-tuple-element.63), channel_id=1, source_target_pairs={{0,10},{1,11},{2,8},{3,9},{4,14},{5,15},{6,12},{7,13},{8,2},{9,3},... | collective-permute-start | bytes 344072 | tf_op jit(solution)/shard_map/ppermute | solution.py:408
  31.6 7.9 %collective-permute-start.13 = (bf16[16,3584]{1,0:T(8,128)(2,1)S(1)}, bf16[16,3584]{1,0:T(8,128)(2,1)S(1)}, u32[]{:S(2)}, u32[]{:S(2)}) collective-permute-start(bf16[16,3584]{1,0:T(8,128)(2,1)S(1)} %collective-permute-done.4.refs_5_), channel_id=1, source_target_pairs={{0,16},{16,0},{1,17},{17,1},{2,18},{18,2},{3,19},{19,3},{4,20},{20... | collective-permute-start | bytes 344072 | tf_op jit(solution)/shard_map/ppermute | solution.py:403
  33.3 6.7 %collective-permute-start.17 = (bf16[16,3584]{1,0:T(8,128)(2,1)S(1)}, bf16[16,3584]{1,0:T(8,128)(2,1)S(1)}, u32[]{:S(2)}, u32[]{:S(2)}) collective-permute-start(bf16[16,3584]{1,0:T(8,128)(2,1)S(1)} %collective-permute-done.7.refs_7_), channel_id=1, source_target_pairs={{0,16},{16,0},{1,17},{17,1},{2,18},{18,2},{3,19},{19,3},{4,20},{20... | collective-permute-start | bytes 344072 | tf_op jit(solution)/shard_map/ppermute | solution.py:403
  33.6 7.2 %collective-permute-start.14 = (bf16[16,3584]{1,0:T(8,128)(2,1)S(1)}, bf16[16,3584]{1,0:T(8,128)(2,1)S(1)}, u32[]{:S(2)}, u32[]{:S(2)}) collective-permute-start(bf16[16,3584]{1,0:T(8,128)(2,1)S(1)} %collective-permute-done.5.refs_6_), channel_id=1, source_target_pairs={{0,16},{16,0},{1,17},{17,1},{2,18},{18,2},{3,19},{19,3},{4,20},{20... | collective-permute-start | bytes 344072 | tf_op jit(solution)/shard_map/ppermute | solution.py:403
  35.4 7.7 %collective-permute-start.16 = (bf16[16,3584]{1,0:T(8,128)(2,1)S(1)}, bf16[16,3584]{1,0:T(8,128)(2,1)S(1)}, u32[]{:S(2)}, u32[]{:S(2)}) collective-permute-start(bf16[16,3584]{1,0:T(8,128)(2,1)S(1)} %collective-permute-done.9.refs_10_), channel_id=1, source_target_pairs={{0,16},{16,0},{1,17},{17,1},{2,18},{18,2},{3,19},{19,3},{4,20},{20... | collective-permute-start | bytes 344072 | tf_op jit(solution)/shard_map/ppermute | solution.py:403
  35.6 7.4 %collective-permute-start.18 = (bf16[16,3584]{1,0:T(8,128)(2,1)S(1)}, bf16[16,3584]{1,0:T(8,128)(2,1)S(1)}, u32[]{:S(2)}, u32[]{:S(2)}) collective-permute-start(bf16[16,3584]{1,0:T(8,128)(2,1)S(1)} %collective-permute-done.12.refs_8_), channel_id=1, source_target_pairs={{0,16},{16,0},{1,17},{17,1},{2,18},{18,2},{3,19},{19,3},{4,20},{20... | collective-permute-start | bytes 344072 | tf_op jit(solution)/shard_map/ppermute | solution.py:403
  39.4 17.2 %collective-permute-start.20 = (bf16[2,720,128]{2,1,0:T(8,128)(2,1)S(1)}, bf16[2,720,128]{2,1,0:T(8,128)(2,1)S(1)}, u32[]{:S(2)}, u32[]{:S(2)}) collective-permute-start(bf16[2,720,128]{2,1,0:T(8,128)(2,1)S(1)} %get-tuple-element.76), channel_id=1, source_target_pairs={{0,2},{1,3},{2,0},{3,1},{4,6},{5,7},{6,4},{7,5},{8,10},{9,11},{10,... | collective-permute-start | bytes 1105928 | tf_op jit(solution)/shard_map/ppermute | solution.py:408
  40.0 16.6 %collective-permute-start.21 = (bf16[2,720,128]{2,1,0:T(8,128)(2,1)S(1)}, bf16[2,720,128]{2,1,0:T(8,128)(2,1)S(1)}, u32[]{:S(2)}, u32[]{:S(2)}) collective-permute-start(bf16[2,720,128]{2,1,0:T(8,128)(2,1)S(1)} %get-tuple-element.77), channel_id=1, source_target_pairs={{0,4},{1,5},{2,6},{3,7},{4,0},{5,1},{6,2},{7,3},{8,12},{9,13},{10,... | collective-permute-start | bytes 1105928 | tf_op jit(solution)/shard_map/ppermute | solution.py:408
  40.8 15.9 %collective-permute-start.22 = (bf16[2,720,128]{2,1,0:T(8,128)(2,1)S(1)}, bf16[2,720,128]{2,1,0:T(8,128)(2,1)S(1)}, u32[]{:S(2)}, u32[]{:S(2)}) collective-permute-start(bf16[2,720,128]{2,1,0:T(8,128)(2,1)S(1)} %get-tuple-element.78), channel_id=1, source_target_pairs={{0,6},{1,7},{2,4},{3,5},{4,2},{5,3},{6,0},{7,1},{8,14},{9,15},{10,... | collective-permute-start | bytes 1105928 | tf_op jit(solution)/shard_map/ppermute | solution.py:408
  45.0 11.6 %collective-permute-start.19 = (bf16[128,512]{1,0:T(8,128)(2,1)S(1)}, bf16[128,512]{1,0:T(8,128)(2,1)S(1)}, u32[]{:S(2)}, u32[]{:S(2)}) collective-permute-start(bf16[128,512]{1,0:T(8,128)(2,1)S(1)} %get-tuple-element.69), channel_id=1, source_target_pairs={{0,16},{16,0},{1,17},{17,1},{2,18},{18,2},{3,19},{19,3},{4,20},{20... | collective-permute-start | bytes 393224 | tf_op jit(solution)/shard_map/ppermute | solution.py:403
  59.0 6.0 %collective-permute-start.25 = (bf16[96,224]{1,0:T(8,128)(2,1)S(1)}, bf16[96,224]{1,0:T(8,128)(2,1)S(1)}, u32[]{:S(2)}, u32[]{:S(2)}) collective-permute-start(bf16[96,224]{1,0:T(8,128)(2,1)S(1)} %get-tuple-element.86), channel_id=1, source_target_pairs={{0,16},{1,17},{2,18},{3,19},{4,20},{5,21},{6,22},{7,23},{8,24},{9,... | collective-permute-start | bytes 129032 | tf_op jit(solution)/shard_map/ppermute | solution.py:413
  60.2 6.4 %collective-permute-start.24 = (bf16[96,224]{1,0:T(8,128)(2,1)S(1)}, bf16[96,224]{1,0:T(8,128)(2,1)S(1)}, u32[]{:S(2)}, u32[]{:S(2)}) collective-permute-start(bf16[96,224]{1,0:T(8,128)(2,1)S(1)} %get-tuple-element.85), channel_id=1, source_target_pairs={{0,8},{1,9},{2,10},{3,11},{4,12},{5,13},{6,14},{7,15},{8,0},{9,1},... | collective-permute-start | bytes 129032 | tf_op jit(solution)/shard_map/ppermute | solution.py:413
  60.8 6.6 %collective-permute-start.23 = (bf16[96,224]{1,0:T(8,128)(2,1)S(1)}, bf16[96,224]{1,0:T(8,128)(2,1)S(1)}, u32[]{:S(2)}, u32[]{:S(2)}) collective-permute-start(bf16[96,224]{1,0:T(8,128)(2,1)S(1)} %get-tuple-element.84), channel_id=1, source_target_pairs={{0,24},{1,25},{2,26},{3,27},{4,28},{5,29},{6,30},{7,31},{8,16},{9,... | collective-permute-start | bytes 129032 | tf_op jit(solution)/shard_map/ppermute | solution.py:413

commit v5 on v4

--- a/solution.py
+++ b/solution.py
@@ -120,7 +120,7 @@
  'grads_own': 10737418240,
  'grads_other': 107374182400,
  'prepare': 8589934592,
- 'panel': 16777216,
+ 'panel': 1073741824,
  'hidden': 16777216}
 ORDER = (('send', 0), ('first', 0), ('forward', (0,)), ('send', 6), ('send', 1), ('send', 2), ('send', 7),
  ('send', 3), ('forward', (1,)), ('forward', (2,)), ('send', 4), ('send', 5), ('forward', (3,)),
@@ -132,9 +132,8 @@
  2: (('other', 0),)}
 FORWARD = {7: (('first', 0),)}
 FIRST = (('block', 0),)
-SAVED = ()
-PARCEL = ()
 MERGE = (('own', 5),)
+STEPS = 7
 
 
 NT = (((1,), (1,)), ((), ()))
@@ -275,29 +274,43 @@
     return (iota((size, size), 1) == (iota((size, size), 0) ^ (me * cap))).astype(dtype)
 
 
-def finish_grads(me, grads, saved_ref, grads_ref, cap):
-    slots = saved_ref.shape[0]
-    swap = swap_matrix(me, slots, cap, jnp.bfloat16)
-    where_to = swap_matrix(me, slots, cap, jnp.float32)
-    saved = lax.dot_general(swap, saved_ref[...], NN, preferred_element_type=jnp.float32)
+def multiply(pieces, weight_ref, steps):
+    width = weight_ref.shape[1] // steps
+    total = None
+    for k in range(steps):
+        part = slice(k * width, (k + 1) * width)
+        rows = jnp.concatenate([p[:, part] for p in pieces], axis=0)
+        term = lax.dot_general(rows, weight_ref[:, part], NT, preferred_element_type=jnp.float32)
+        total = term if total is None else total + term
+    return total
+
+
+def slot_line(me, saved, grads, cap):
+    sums = jnp.sum(saved * grads, axis=1, keepdims=True)
+    where_to = swap_matrix(me, grads.shape[0], cap, jnp.float32)
+    return jnp.sum(where_to * sums, axis=0, keepdims=True)
+
+
+def grads_own_body(place_ref, saved_ref, saved_other_ref, weight_ref, *refs, cap, steps):
+    pieces, (grads_ref, line_ref, turned_ref) = refs[:-3], refs[-3:]
+    grads = multiply(pieces, weight_ref, steps)
+    swap = swap_matrix(place_ref[1], grads.shape[0], cap, jnp.bfloat16)
+    saved, turned = (
+        lax.dot_general(swap, ref[...], NN, preferred_element_type=jnp.float32)
+        for ref in (saved_ref, saved_other_ref)
+    )
+    turned_ref[...] = turned
+    grads_ref[...] = grads
+    line_ref[...] = slot_line(place_ref[1], saved, grads, cap)
+
+
+def grads_other_body(place_ref, turned_ref, weight_ref, line_own_ref, gate_ref, *refs, cap, spots, steps):
+    groups, (grads_ref, message_ref) = refs[:-2], refs[-2:]
+    size = 2 * cap
+    pieces = [groups[g].at[k * size : (k + 1) * size] for g, k in spots]
+    grads = multiply(pieces, weight_ref, steps)
     grads_ref[...] = grads.astype(grads_ref.dtype)
-    sums = jnp.sum(saved * grads, axis=1, keepdims=True)
-    return jnp.sum(where_to * sums, axis=0, keepdims=True)
-
-
-def grads_own_body(place_ref, saved_ref, weight_ref, *refs, cap):
-    pieces, (grads_ref, line_ref) = refs[:-2], refs[-2:]
-    rows = jnp.concatenate([p[...] for p in pieces], axis=0)
-    grads = lax.dot_general(rows, weight_ref[...], NT, preferred_element_type=jnp.float32)
-    line_ref[...] = finish_grads(place_ref[1], grads, saved_ref, grads_ref, cap)
-
-
-def grads_other_body(place_ref, saved_ref, weight_ref, line_own_ref, gate_ref, *refs, cap, spots):
-    pieces, (grads_ref, message_ref) = refs[:-2], refs[-2:]
-    size = 2 * cap
-    rows = jnp.concatenate([pieces[g][k * size : (k + 1) * size] for g, k in spots], axis=0)
-    grads = lax.dot_general(rows, weight_ref[...], NT, preferred_element_type=jnp.float32)
-    other = finish_grads(place_ref[1], grads, saved_ref, grads_ref, cap)
+    other = slot_line(place_ref[1], turned_ref[...], grads, cap)
     own = line_own_ref[...]
     dp = place_ref[0]
     count = message_ref.shape[0] // 2
@@ -354,11 +367,17 @@
     gate_all = jnp.concatenate(
         [message_ref[e, 0:1] + message_ref[16 + e, 0:1] for e in range(16)], axis=0
     )
-    swap = swap_matrix(me, gate_all.shape[1], cap, jnp.bfloat16)
-    gate_rel = sum(
-        lax.dot_general(part, swap, NN, preferred_element_type=jnp.float32)
-        for part in three_halves(gate_all)
-    )
+    gate_rel = gate_all
+    lanes = iota(gate_all.shape, 1)
+    size = gate_all.shape[1]
+    for bit in range(4):
+        step = cap << bit
+        swapped = jnp.where(
+            (lanes & step) != 0,
+            pltpu.roll(gate_rel, step, 1),
+            pltpu.roll(gate_rel, size - step, 1),
+        )
+        gate_rel = jnp.where(((me >> bit) & 1) == 1, swapped, gate_rel)
     lines, blocks = [], []
     total = None
     for q, (parcel, here) in enumerate(views(parcels)):
@@ -487,8 +506,8 @@
         )
         known["first", 0] = outs[2]
         known["results", 0] = outs
-        known["saved", 0] = over_dp(held(outs[4], SAVED))
-        known["got", 0] = over_expert(held(outs[6], PARCEL), 1)
+        known["saved", 0] = over_dp(outs[4])
+        known["got", 0] = over_expert(outs[6], 1)
 
     for kind, which in ORDER:
         {"send": send, "forward": forward, "first": lambda _: first()}[kind](which)
@@ -504,19 +523,23 @@
         held(parcel_keep, MERGE), parcel_got,
     )
     parcels = (parcel_keep, parcel_got, *(over_expert(m, 2 * q + 2) for q, m in enumerate(merged)))
-    grads_own, line_own = kernel_call(
-        lambda *refs: grads_own_body(*refs, cap=cap),
-        (jax.ShapeDtypeStruct((slots, half), f32), jax.ShapeDtypeStruct((1, slots), f32)),
-        "grads_own", HINT["grads_own"], 5 << 20, place, saved_own, weight, *own,
+    grads_own, line_own, saved_turned = kernel_call(
+        lambda *refs: grads_own_body(*refs, cap=cap, steps=STEPS),
+        (
+            jax.ShapeDtypeStruct((slots, half), f32),
+            jax.ShapeDtypeStruct((1, slots), f32),
+            jax.ShapeDtypeStruct((slots, half), f32),
+        ),
+        "grads_own", HINT["grads_own"], 5 << 20, place, saved_own, saved_other, weight, *own,
     )
     grads_other, message = kernel_call(
-        lambda *refs: grads_other_body(*refs, cap=cap, spots=spots),
+        lambda *refs: grads_other_body(*refs, cap=cap, spots=spots, steps=STEPS),
         (
             jax.ShapeDtypeStruct((slots, half), bf16),
             jax.ShapeDtypeStruct((2 * flight, 2, slots), f32),
         ),
         "grads_other", HINT["grads_other"], 5 << 20,
-        place, saved_other, weight, line_own, slot_gates, *other,
+        place, saved_turned, weight, line_own, slot_gates, *other,
     )
     grads_back = over_dp(grads_other)
     message = lax.all_to_all(message, ("dp", "expert"), 0, 0, tiled=True)
@@ -545,7 +568,8 @@
         "hidden", HINT["hidden"], 1 << 20,
         place, grads_own, grads_back, message,
     )
-    far = [over_both(sums[3], 1, group), over_both(sums[2], 0, group), over_both(sums[1], 1, 0)]
+    moves = {1: (1, 0), 2: (0, group), 3: (1, group)}
+    far = [over_both(sums[k], *moves[k]) for k in (3, 1, 2)]
     router_t = after(sums[0], hidden_grad) + sum(part.astype(f32) for part in far)
     return (
         hidden_grad.reshape(1, 1, flight, cap, hidden),

time: 68.3 us -> 67.8 us (level)
  transfers between devices with their start and end apart: 26 -> 26, of which waited for: 3 -> 2; matrix products, arithmetic and copies ran while one was open for 0% -> 0% of each run, Pallas kernels for 10% -> 10%
where the time goes in v5:
time: 67.8 us; the launch traced here: 67.6 us
  starting transfers between devices  40.2 us (59%)
  Pallas kernels  11.2 us (17%)
  blocking collectives  10.2 us (15%)
  waiting for transfers between devices  2.61 us (4%)
  local copies, waits for them, and re-layouts  1.88 us (3%)
  between operations  0.77 us (1%)
  other arithmetic  0.74 us (1%)
    ppermute x13, starting transfers between devices, over_expert(): return lax.ppermute(value, 'expert', [(k, k ^ bits) for k in range(count)])  22.1 us
    ppermute x10, starting transfers between devices, over_dp(): return lax.ppermute(value, 'dp', [(0, 1), (1, 0)])  13.7 us
    pallas_call x9, Pallas kernels, kernel_call(): pl.pallas_call(body, out_shape=out_shape, in_specs=[pl.BlockSpec(memory_s...  11.2 us
    all_to_all x1, blocking collectives, paired_local(): message = lax.all_to_all(message, ('dp', 'expert'), 0, 0, tiled=True)  10.2 us
    ppermute x3, starting transfers between devices, over_both(): lax.ppermute(value, ('dp', 'expert'), [(k, k ^ dp_bit * count + bits) for...  4.39 us
    unnamed x12, local copies, waits for them, and re-layouts  1.88 us
    ppermute x3, waiting for transfers between devices, over_both(): lax.ppermute(value, ('dp', 'expert'), [(k, k ^ dp_bit * count + bits) for...  1.8 us
  transfers between devices with their start and end apart: 26, of which 2 were waited for; matrix products, arithmetic and copies ran while one was open for 0% of the time, Pallas kernels for 10%

profile of v5, /device:TPU:0, one launch (start us, length us, event | category | flops | bytes accessed | tf_op | source)
XLA Modules:
  0.0 67.6 jit_solution(9917556010462667510)
XLA Ops:
  0.6 0.5 collective-permute-start.1
  1.1 0.1 collective-permute-start
  1.2 0.1 pad_add_fusion.refs_0_
  1.3 1.2 %copy-done.1 = bf16[128,3584]{1,0:T(8,128)(2,1)S(1)} copy-done((bf16[128,3584]{1,0:T(8,128)(2,1)S(1)}, bf16[128,3584]{1,0:T(8,128)(2,1)}, u32[]{:S(2)}) %copy-start.1) | copy-done | bytes 917528
  2.5 0.7 %copy-done.5 = s32[128,8]{0,1:T(8,128)S(1)} copy-done((s32[128,8]{0,1:T(8,128)S(1)}, s32[128,8]{0,1:T(8,128)}, u32[]{:S(2)}) %copy-start.5) | copy-done | bytes 4120
  3.2 0.9 %pack_own.1.refs_1_ = f32[64,3584]{1,0:T(8,128)S(1)} custom-call(s32[2]{0:T(128)S(1)} %pad_add_fusion.refs_0_, s32[8,128]{1,0:T(8,128)S(1)} %bitcast.15, bf16[128,3584]{1,0:T(8,128)(2,1)S(1)} %copy-done.1), custom_call_target="tpu_custom_call" | custom-call | flops 1073741824 | bytes 3145728 | tf_op jit(solution)/shard_map/pack_own/pallas_call | solution.py:149
  4.1 0.0 collective-permute-done.refs_2_
  4.1 0.0 collective-permute-done.1.refs_3_
  4.1 0.9 %pack.1 = (bf16[16,3584]{1,0:T(8,128)(2,1)S(1)}, bf16[16,3584]{1,0:T(8,128)(2,1)S(1)}, bf16[16,3584]{1,0:T(8,128)(2,1)S(1)}, bf16[16,3584]{1,0:T(8,128)(2,1)S(1)...) custom-call(s32[2]{0:T(128)S(1)} %pad_add_fusion.refs_0_, ...), custom_call_target="tpu_custom_call" | custom-call | flops 1073741824 | bytes 3145728 | tf_op jit(solution)/shard_map/pack/pallas_call | solution.py:149
  5.1 0.0 copy-start
  5.1 1.2 %first.1 = (f32[192,128]{1,0:T(8,128)S(1)}, f32[192,128]{1,0:T(8,128)S(1)}, f32[16,128]{1,0:T(8,128)S(1)}, bf16[128,512]{1,0:T(8,128)(2,1)S(1)}, bf16[128,512]{1...) custom-call(s32[2]{0:T(128)S(1)} %pad_add_fusion.refs_0_, ...), custom_call_target="tpu_custom_call" | custom-call | flops 34359738368 | bytes 3145728 | tf_op jit(solution)/shard_map/first/pallas_call | solution.py:149
  6.4 0.5 collective-permute-start.9
  6.8 2.6 %collective-permute-start.4 = (bf16[16,3584]{1,0:T(8,128)(2,1)S(1)}, bf16[16,3584]{1,0:T(8,128)(2,1)S(1)}, u32[]{:S(2)}, u32[]{:S(2)}) collective-permute-start(bf16[16,3584]{1,0:T(8,128)(2,1)S(1)} %get-tuple-element.46.refs_4_), channel_id=1, source_target_pairs={{0,16},{16,0},{1,17},{17,1},{2,18},{18,2},{3,19},{19,3},{4,20},{20... | collective-permute-start | bytes 344072 | tf_op jit(solution)/shard_map/ppermute | solution.py:422
  9.4 1.5 %collective-permute-start.3 = (bf16[16,3584]{1,0:T(8,128)(2,1)S(1)}, bf16[16,3584]{1,0:T(8,128)(2,1)S(1)}, u32[]{:S(2)}, u32[]{:S(2)}) collective-permute-start(bf16[16,3584]{1,0:T(8,128)(2,1)S(1)} %get-tuple-element.52), channel_id=1, source_target_pairs={{0,2},{1,3},{2,0},{3,1},{4,6},{5,7},{6,4},{7,5},{8,10},{9,11},{10,... | collective-permute-start | bytes 344072 | tf_op jit(solution)/shard_map/ppermute | solution.py:427
  10.9 0.5 collective-permute-start.2
  11.5 3.6 %collective-permute-start.7 = (bf16[16,3584]{1,0:T(8,128)(2,1)S(1)}, bf16[16,3584]{1,0:T(8,128)(2,1)S(1)}, u32[]{:S(2)}, u32[]{:S(2)}) collective-permute-start(bf16[16,3584]{1,0:T(8,128)(2,1)S(1)} %get-tuple-element.58), channel_id=1, source_target_pairs={{0,12},{1,13},{2,14},{3,15},{4,8},{5,9},{6,10},{7,11},{8,4},{9,5},... | collective-permute-start | bytes 344072 | tf_op jit(solution)/shard_map/ppermute | solution.py:427
  15.1 0.0 collective-permute-done.4.refs_5_
  15.1 0.0 collective-permute-start.5
  15.1 0.0 collective-permute-done.3.refs_5_
  15.1 1.9 %collective-permute-start.11 = (bf16[16,3584]{1,0:T(8,128)(2,1)S(1)}, bf16[16,3584]{1,0:T(8,128)(2,1)S(1)}, u32[]{:S(2)}, u32[]{:S(2)}) collective-permute-start(bf16[16,3584]{1,0:T(8,128)(2,1)S(1)} %collective-permute-done.3.refs_5_), channel_id=1, source_target_pairs={{0,16},{16,0},{1,17},{17,1},{2,18},{18,2},{3,19},{19,3},{4,20},{20... | collective-permute-start | bytes 344072 | tf_op jit(solution)/shard_map/ppermute | solution.py:422
  17.0 0.0 collective-permute-done.9.got_ref.refs_1_.refs_7_
  17.0 3.4 %collective-permute-start.10 = (bf16[16,3584]{1,0:T(8,128)(2,1)S(1)}, bf16[16,3584]{1,0:T(8,128)(2,1)S(1)}, u32[]{:S(2)}, u32[]{:S(2)}) collective-permute-start(bf16[16,3584]{1,0:T(8,128)(2,1)S(1)} %get-tuple-element.63), channel_id=1, source_target_pairs={{0,14},{1,15},{2,12},{3,13},{4,10},{5,11},{6,8},{7,9},{8,6},{9,7},... | collective-permute-start | bytes 344072 | tf_op jit(solution)/shard_map/ppermute | solution.py:427
  20.4 0.0 collective-permute-done.7.refs_10_
  20.4 0.2 collective-permute-start.8
  20.6 0.0 collective-permute-done.5.refs_6_
  20.6 2.7 %collective-permute-start.6 = (bf16[16,3584]{1,0:T(8,128)(2,1)S(1)}, bf16[16,3584]{1,0:T(8,128)(2,1)S(1)}, u32[]{:S(2)}, u32[]{:S(2)}) collective-permute-start(bf16[16,3584]{1,0:T(8,128)(2,1)S(1)} %get-tuple-element.56), channel_id=1, source_target_pairs={{0,6},{1,7},{2,4},{3,5},{4,2},{5,3},{6,0},{7,1},{8,14},{9,15},{10,... | collective-permute-start | bytes 344072 | tf_op jit(solution)/shard_map/ppermute | solution.py:427
  23.3 0.0 collective-permute-done.2.refs_2_
  23.3 1.5 %collective-permute-start.15 = (bf16[16,3584]{1,0:T(8,128)(2,1)S(1)}, bf16[16,3584]{1,0:T(8,128)(2,1)S(1)}, u32[]{:S(2)}, u32[]{:S(2)}) collective-permute-start(bf16[16,3584]{1,0:T(8,128)(2,1)S(1)} %collective-permute-done.7.refs_10_), channel_id=1, source_target_pairs={{0,16},{16,0},{1,17},{17,1},{2,18},{18,2},{3,19},{19,3},{4,20},{20... | collective-permute-start | bytes 344072 | tf_op jit(solution)/shard_map/ppermute | solution.py:422
  24.8 0.0 collective-permute-done.11.refs_6_
  24.8 0.8 %collective-permute-done.10.refs_11_ = bf16[16,3584]{1,0:T(8,128)(2,1)S(1)} collective-permute-done((bf16[16,3584]{1,0:T(8,128)(2,1)S(1)}, bf16[16,3584]{1,0:T(8,128)(2,1)S(1)}, u32[]{:S(2)}, u32[]{:S(2)}) %collective-permute-start.10) | collective-permute-done | bytes 114720 | tf_op jit(solution)/shard_map/ppermute | solution.py:427
  25.6 6.0 %collective-permute-start.12 = (bf16[16,3584]{1,0:T(8,128)(2,1)S(1)}, bf16[16,3584]{1,0:T(8,128)(2,1)S(1)}, u32[]{:S(2)}, u32[]{:S(2)}) collective-permute-start(bf16[16,3584]{1,0:T(8,128)(2,1)S(1)} %get-tuple-element.64), channel_id=1, source_target_pairs={{0,10},{1,11},{2,8},{3,9},{4,14},{5,15},{6,12},{7,13},{8,2},{9,3},... | collective-permute-start | bytes 344072 | tf_op jit(solution)/shard_map/ppermute | solution.py:427
  31.6 1.8 %collective-permute-start.13 = (bf16[16,3584]{1,0:T(8,128)(2,1)S(1)}, bf16[16,3584]{1,0:T(8,128)(2,1)S(1)}, u32[]{:S(2)}, u32[]{:S(2)}) collective-permute-start(bf16[16,3584]{1,0:T(8,128)(2,1)S(1)} %collective-permute-done.5.refs_6_), channel_id=1, source_target_pairs={{0,16},{16,0},{1,17},{17,1},{2,18},{18,2},{3,19},{19,3},{4,20},{20... | collective-permute-start | bytes 344072 | tf_op jit(solution)/shard_map/ppermute | solution.py:422
  33.3 0.0 collective-permute-done.8.refs_8_
  33.3 0.3 collective-permute-start.17
  33.6 0.0 collective-permute-done.6.refs_7_
  33.6 1.8 %collective-permute-start.14 = (bf16[16,3584]{1,0:T(8,128)(2,1)S(1)}, bf16[16,3584]{1,0:T(8,128)(2,1)S(1)}, u32[]{:S(2)}, u32[]{:S(2)}) collective-permute-start(bf16[16,3584]{1,0:T(8,128)(2,1)S(1)} %collective-permute-done.6.refs_7_), channel_id=1, source_target_pairs={{0,16},{16,0},{1,17},{17,1},{2,18},{18,2},{3,19},{19,3},{4,20},{20... | collective-permute-start | bytes 344072 | tf_op jit(solution)/shard_map/ppermute | solution.py:422
  35.3 0.0 collective-permute-done.15.refs_9_
  35.4 0.3 collective-permute-start.16
  35.6 0.0 collective-permute-done.12.refs_9_
  35.6 1.8 %collective-permute-start.18 = (bf16[16,3584]{1,0:T(8,128)(2,1)S(1)}, bf16[16,3584]{1,0:T(8,128)(2,1)S(1)}, u32[]{:S(2)}, u32[]{:S(2)}) collective-permute-start(bf16[16,3584]{1,0:T(8,128)(2,1)S(1)} %collective-permute-done.12.refs_9_), channel_id=1, source_target_pairs={{0,16},{16,0},{1,17},{17,1},{2,18},{18,2},{3,19},{19,3},{4,20},{20... | collective-permute-start | bytes 344072 | tf_op jit(solution)/shard_map/ppermute | solution.py:422
  37.4 2.0 %grads_own.1 = (f32[128,512]{1,0:T(8,128)S(1)}, f32[1,128]{1,0:T(1,128)S(1)}, f32[128,512]{1,0:T(8,128)S(1)}) custom-call(s32[2]{0:T(128)S(1)} %pad_add_fusion.refs_0_, bf16[128,512]{1,0:T(8,128)(2,1)S(1)} %get-tuple-element.50.refs_1_, bf16[128,512]{1,0:T(8,128)(2,1)S(1)} %collective-permute-done.2.refs_2_, bf16[512,3584]{1,0:T(8,128)(2,1)S(1)} %bitcast.10, ...), custom_call_target="tpu_custom_call" | custom-call | flops 10737418240 | bytes 5242880 | tf_op jit(solution)/shard_map/grads_own/pallas_call | solution.py:149
  39.3 0.1 merge.1
  39.4 0.0 collective-permute-done.13.refs_7_
  39.4 0.6 collective-permute-start.20
  40.0 0.0 collective-permute-done.17.refs_11_
  40.0 0.7 %collective-permute-start.21 = (bf16[2,720,128]{2,1,0:T(8,128)(2,1)S(1)}, bf16[2,720,128]{2,1,0:T(8,128)(2,1)S(1)}, u32[]{:S(2)}, u32[]{:S(2)}) collective-permute-start(bf16[2,720,128]{2,1,0:T(8,128)(2,1)S(1)} %get-tuple-element.79), channel_id=1, source_target_pairs={{0,4},{1,5},{2,6},{3,7},{4,0},{5,1},{6,2},{7,3},{8,12},{9,13},{10,... | collective-permute-start | bytes 1105928 | tf_op jit(solution)/shard_map/ppermute | solution.py:427
  40.8 0.0 collective-permute-done.14.refs_8_
  40.8 2.2 %collective-permute-start.22 = (bf16[2,720,128]{2,1,0:T(8,128)(2,1)S(1)}, bf16[2,720,128]{2,1,0:T(8,128)(2,1)S(1)}, u32[]{:S(2)}, u32[]{:S(2)}) collective-permute-start(bf16[2,720,128]{2,1,0:T(8,128)(2,1)S(1)} %get-tuple-element.80), channel_id=1, source_target_pairs={{0,6},{1,7},{2,4},{3,5},{4,2},{5,3},{6,0},{7,1},{8,14},{9,15},{10,... | collective-permute-start | bytes 1105928 | tf_op jit(solution)/shard_map/ppermute | solution.py:427
  43.0 0.0 collective-permute-done.16.refs_10_
  43.0 0.0 collective-permute-done.18.refs_12_
  43.0 1.9 %grads_other.1 = (bf16[128,512]{1,0:T(8,128)(2,1)S(1)}, f32[32,2,128]{2,1,0:T(2,128)S(1)}) custom-call(s32[2]{0:T(128)S(1)} %pad_add_fusion.refs_0_, f32[128,512]{1,0:T(8,128)S(1)} %get-tuple-element.66.refs_1_, bf16[512,3584]{1,0:T(8,128)(2,1)S(1)} %bitcast.11, f32[1,128]{1,0:T(1,128)S(1)} %get-tuple-element.67.refs_3_, ...), custom_call_target="tpu_custom_call" | custom-call | flops 107374182400 | bytes 5242880 | tf_op jit(solution)/shard_map/grads_other/pallas_call | solution.py:149
  44.9 1.4 %collective-permute-start.19 = (bf16[128,512]{1,0:T(8,128)(2,1)S(1)}, bf16[128,512]{1,0:T(8,128)(2,1)S(1)}, u32[]{:S(2)}, u32[]{:S(2)}) collective-permute-start(bf16[128,512]{1,0:T(8,128)(2,1)S(1)} %get-tuple-element.71), channel_id=1, source_target_pairs={{0,16},{16,0},{1,17},{17,1},{2,18},{18,2},{3,19},{19,3},{4,20},{20... | collective-permute-start | bytes 393224 | tf_op jit(solution)/shard_map/ppermute | solution.py:422
  46.4 10.2 %all_to_all.5.refs_3_ = f32[32,2,128]{2,1,0:T(2,128)S(1)} all-to-all(f32[32,2,128]{2,1,0:T(2,128)S(1)} %get-tuple-element.70), channel_id=1, replica_groups=mesh['dp'=2,'expert'=16] {'dp','expert'}, dimensions={0} | all-to-all | bytes 65536 | tf_op jit(solution)/shard_map/all_to_all | solution.py:545
  56.6 0.0 collective-permute-done.19.refs_2_
  56.6 0.0 collective-permute-done.22.refs_4_.refs_10_
  56.6 0.4 prepare.1
  57.1 2.1 %panel.1 = (f32[192,128]{1,0:T(8,128)}, f32[96,224]{1,0:T(8,128)S(1)}, bf16[96,224]{1,0:T(8,128)(2,1)S(1)}, bf16[96,224]{1,0:T(8,128)(2,1)S(1)}, bf16[96,224]{1,0:T(8,128)(2,1)S(1)}) custom-call(s32[2]{0:T(128)S(1)} %pad_add_fusion.refs_0_, f32[192,128]{1,0:T(8,128)S(1)} %get-tuple-element.74.refs_1_, f32[192,128]{1,0:T(8,128)S(1)} %get-tuple-element.75.refs_2_, ...), custom_call_target="tpu_custom_call" | custom-call | flops 1073741824 | bytes 4194304 | tf_op jit(solution)/shard_map/panel/pallas_call | solution.py:149
  59.1 0.6 collective-permute-start.25
  59.7 1.2 %collective-permute-start.24 = (bf16[96,224]{1,0:T(8,128)(2,1)S(1)}, bf16[96,224]{1,0:T(8,128)(2,1)S(1)}, u32[]{:S(2)}, u32[]{:S(2)}) collective-permute-start(bf16[96,224]{1,0:T(8,128)(2,1)S(1)} %get-tuple-element.87), channel_id=1, source_target_pairs={{0,16},{1,17},{2,18},{3,19},{4,20},{5,21},{6,22},{7,23},{8,24},{9,... | collective-permute-start | bytes 129032 | tf_op jit(solution)/shard_map/ppermute | solution.py:432
  60.9 2.6 %collective-permute-start.23 = (bf16[96,224]{1,0:T(8,128)(2,1)S(1)}, bf16[96,224]{1,0:T(8,128)(2,1)S(1)}, u32[]{:S(2)}, u32[]{:S(2)}) collective-permute-start(bf16[96,224]{1,0:T(8,128)(2,1)S(1)} %get-tuple-element.86), channel_id=1, source_target_pairs={{0,24},{1,25},{2,26},{3,27},{4,28},{5,29},{6,30},{7,31},{8,16},{9,... | collective-permute-start | bytes 129032 | tf_op jit(solution)/shard_map/ppermute | solution.py:432
  63.5 1.6 %hidden.1 = bf16[128,1024]{1,0:T(8,128)(2,1)} custom-call(s32[2]{0:T(128)S(1)} %pad_add_fusion.refs_0_, f32[128,512]{1,0:T(8,128)S(1)} %get-tuple-element.65.refs_1_, bf16[128,512]{1,0:T(8,128)(2,1)S(1)} %collective-permute-done.19.refs_2_, f32[32,2,128]{2,1,0:T(2,128)S(1)} %all_to_all.5.refs_3_), custom_call_target="tpu_custom_call" | custom-call | flops 16777216 | bytes 1048576 | tf_op jit(solution)/shard_map/hidden/pallas_call | solution.py:149
  65.2 0.0 collective-permute-done.25
  65.2 1.8 %collective-permute-done.23 = bf16[96,224]{1,0:T(8,128)(2,1)S(1)} collective-permute-done((bf16[96,224]{1,0:T(8,128)(2,1)S(1)}, bf16[96,224]{1,0:T(8,128)(2,1)S(1)}, u32[]{:S(2)}, u32[]{:S(2)}) %collective-permute-start.23) | collective-permute-done | bytes 43040 | tf_op jit(solution)/shard_map/ppermute | solution.py:432
  67.0 0.7 add_bitcast_fusion
  (12 shorter events, 0.0 us)
Async XLA Ops:
  0.6 3.5 %collective-permute-start.1 = (bf16[128,3584]{1,0:T(8,128)(2,1)}, bf16[128,3584]{1,0:T(8,128)(2,1)S(1)}, u32[]{:S(2)}, u32[]{:S(2)}) collective-permute-start(bf16[128,3584]{1,0:T(8,128)(2,1)} %refs_2_.1), channel_id=1, source_target_pairs={{0,1},{1,0},{2,3},{3,2},{4,5},{5,4},{6,7},{7,6},{8,9},{9,8},{10,11... | collective-permute-start | bytes 2752520 | tf_op jit(solution)/shard_map/ppermute | solution.py:427
  1.1 3.0 %collective-permute-start = (s32[8,128]{1,0:T(8,128)}, s32[8,128]{1,0:T(8,128)S(1)}, u32[]{:S(2)}, u32[]{:S(2)}) collective-permute-start(s32[8,128]{1,0:T(8,128)} %bitcast.14), channel_id=1, source_target_pairs={{0,1},{1,0},{2,3},{3,2},{4,5},{5,4},{6,7},{7,6},{8,9},{9,8},{10,11... | collective-permute-start | bytes 12296 | tf_op jit(solution)/shard_map/ppermute | solution.py:427
  1.3 1.2 %copy-start.1 = (bf16[128,3584]{1,0:T(8,128)(2,1)S(1)}, bf16[128,3584]{1,0:T(8,128)(2,1)}, u32[]{:S(2)}) copy-start(bf16[128,3584]{1,0:T(8,128)(2,1)} %refs_2_.1) | copy-start | bytes 2752516
  2.5 0.7 %copy-start.5 = (s32[128,8]{0,1:T(8,128)S(1)}, s32[128,8]{0,1:T(8,128)}, u32[]{:S(2)}) copy-start(s32[128,8]{0,1:T(8,128)} %param.9) | copy-start | bytes 12292
  3.2 1.9 %copy-start.2 = (bf16[128,3584]{1,0:T(8,128)(2,1)S(1)}, bf16[128,3584]{1,0:T(8,128)(2,1)}, u32[]{:S(2)}) copy-start(bf16[128,3584]{1,0:T(8,128)(2,1)} %refs_3_) | copy-start | bytes 2752516
  3.2 1.9 %copy-start.3 = (bf16[1,1,16,8,1024]{4,3,2,1,0:T(8,128)(2,1)S(1)}, bf16[1,1,16,8,1024]{4,3,2,1,0:T(8,128)(2,1)}, u32[]{:S(2)}) copy-start(bf16[1,1,16,8,1024]{4,3,2,1,0:T(8,128)(2,1)} %param.10) | copy-start | bytes 786436
  3.2 1.9 %copy-start.4 = (f32[128,192]{0,1:T(8,128)S(1)}, f32[128,192]{0,1:T(8,128)}, u32[]{:S(2)}) copy-start(f32[128,192]{0,1:T(8,128)} %param.8) | copy-start | bytes 294916
  5.1 32.3 %copy-start = (bf16[1,512,3584]{2,1,0:T(8,128)(2,1)S(1)}, bf16[1,512,3584]{2,1,0:T(8,128)(2,1)}, u32[]{:S(2)}) copy-start(bf16[1,512,3584]{2,1,0:T(8,128)(2,1)} %param.11) | copy-start | bytes 11010052
  6.4 10.6 %collective-permute-start.9 = (bf16[4,720,128]{2,1,0:T(8,128)(2,1)S(1)}, bf16[4,720,128]{2,1,0:T(8,128)(2,1)S(1)}, u32[]{:S(2)}, u32[]{:S(2)}) collective-permute-start(bf16[4,720,128]{2,1,0:T(8,128)(2,1)S(1)} %get-tuple-element.62), channel_id=1, source_target_pairs={{0,1},{1,0},{2,3},{3,2},{4,5},{5,4},{6,7},{7,6},{8,9},{9,8},{10,11... | collective-permute-start | bytes 2211848 | tf_op jit(solution)/shard_map/ppermute | solution.py:427
  6.8 8.2 %collective-permute-start.4 = (bf16[16,3584]{1,0:T(8,128)(2,1)S(1)}, bf16[16,3584]{1,0:T(8,128)(2,1)S(1)}, u32[]{:S(2)}, u32[]{:S(2)}) collective-permute-start(bf16[16,3584]{1,0:T(8,128)(2,1)S(1)} %get-tuple-element.46.refs_4_), channel_id=1, source_target_pairs={{0,16},{16,0},{1,17},{17,1},{2,18},{18,2},{3,19},{19,3},{4,20},{20... | collective-permute-start | bytes 344072 | tf_op jit(solution)/shard_map/ppermute | solution.py:422
  9.4 5.7 %collective-permute-start.3 = (bf16[16,3584]{1,0:T(8,128)(2,1)S(1)}, bf16[16,3584]{1,0:T(8,128)(2,1)S(1)}, u32[]{:S(2)}, u32[]{:S(2)}) collective-permute-start(bf16[16,3584]{1,0:T(8,128)(2,1)S(1)} %get-tuple-element.52), channel_id=1, source_target_pairs={{0,2},{1,3},{2,0},{3,1},{4,6},{5,7},{6,4},{7,5},{8,10},{9,11},{10,... | collective-permute-start | bytes 344072 | tf_op jit(solution)/shard_map/ppermute | solution.py:427
  10.9 12.4 %collective-permute-start.2 = (bf16[128,512]{1,0:T(8,128)(2,1)S(1)}, bf16[128,512]{1,0:T(8,128)(2,1)S(1)}, u32[]{:S(2)}, u32[]{:S(2)}) collective-permute-start(bf16[128,512]{1,0:T(8,128)(2,1)S(1)} %get-tuple-element.51), channel_id=1, source_target_pairs={{0,16},{16,0},{1,17},{17,1},{2,18},{18,2},{3,19},{19,3},{4,20},{20... | collective-permute-start | bytes 393224 | tf_op jit(solution)/shard_map/ppermute | solution.py:422
  11.5 8.9 %collective-permute-start.7 = (bf16[16,3584]{1,0:T(8,128)(2,1)S(1)}, bf16[16,3584]{1,0:T(8,128)(2,1)S(1)}, u32[]{:S(2)}, u32[]{:S(2)}) collective-permute-start(bf16[16,3584]{1,0:T(8,128)(2,1)S(1)} %get-tuple-element.58), channel_id=1, source_target_pairs={{0,12},{1,13},{2,14},{3,15},{4,8},{5,9},{6,10},{7,11},{8,4},{9,5},... | collective-permute-start | bytes 344072 | tf_op jit(solution)/shard_map/ppermute | solution.py:427
  15.1 5.5 %collective-permute-start.5 = (bf16[16,3584]{1,0:T(8,128)(2,1)S(1)}, bf16[16,3584]{1,0:T(8,128)(2,1)S(1)}, u32[]{:S(2)}, u32[]{:S(2)}) collective-permute-start(bf16[16,3584]{1,0:T(8,128)(2,1)S(1)} %get-tuple-element.54), channel_id=1, source_target_pairs={{0,4},{1,5},{2,6},{3,7},{4,0},{5,1},{6,2},{7,3},{8,12},{9,13},{10,... | collective-permute-start | bytes 344072 | tf_op jit(solution)/shard_map/ppermute | solution.py:427
  15.1 9.7 %collective-permute-start.11 = (bf16[16,3584]{1,0:T(8,128)(2,1)S(1)}, bf16[16,3584]{1,0:T(8,128)(2,1)S(1)}, u32[]{:S(2)}, u32[]{:S(2)}) collective-permute-start(bf16[16,3584]{1,0:T(8,128)(2,1)S(1)} %collective-permute-done.3.refs_5_), channel_id=1, source_target_pairs={{0,16},{16,0},{1,17},{17,1},{2,18},{18,2},{3,19},{19,3},{4,20},{20... | collective-permute-start | bytes 344072 | tf_op jit(solution)/shard_map/ppermute | solution.py:422
  17.0 8.6 %collective-permute-start.10 = (bf16[16,3584]{1,0:T(8,128)(2,1)S(1)}, bf16[16,3584]{1,0:T(8,128)(2,1)S(1)}, u32[]{:S(2)}, u32[]{:S(2)}) collective-permute-start(bf16[16,3584]{1,0:T(8,128)(2,1)S(1)} %get-tuple-element.63), channel_id=1, source_target_pairs={{0,14},{1,15},{2,12},{3,13},{4,10},{5,11},{6,8},{7,9},{8,6},{9,7},... | collective-permute-start | bytes 344072 | tf_op jit(solution)/shard_map/ppermute | solution.py:427
  20.4 12.9 %collective-permute-start.8 = (bf16[16,3584]{1,0:T(8,128)(2,1)S(1)}, bf16[16,3584]{1,0:T(8,128)(2,1)S(1)}, u32[]{:S(2)}, u32[]{:S(2)}) collective-permute-start(bf16[16,3584]{1,0:T(8,128)(2,1)S(1)} %get-tuple-element.59), channel_id=1, source_target_pairs={{0,8},{1,9},{2,10},{3,11},{4,12},{5,13},{6,14},{7,15},{8,0},{9,1},... | collective-permute-start | bytes 344072 | tf_op jit(solution)/shard_map/ppermute | solution.py:427
  20.6 13.0 %collective-permute-start.6 = (bf16[16,3584]{1,0:T(8,128)(2,1)S(1)}, bf16[16,3584]{1,0:T(8,128)(2,1)S(1)}, u32[]{:S(2)}, u32[]{:S(2)}) collective-permute-start(bf16[16,3584]{1,0:T(8,128)(2,1)S(1)} %get-tuple-element.56), channel_id=1, source_target_pairs={{0,6},{1,7},{2,4},{3,5},{4,2},{5,3},{6,0},{7,1},{8,14},{9,15},{10,... | collective-permute-start | bytes 344072 | tf_op jit(solution)/shard_map/ppermute | solution.py:427
  23.3 12.0 %collective-permute-start.15 = (bf16[16,3584]{1,0:T(8,128)(2,1)S(1)}, bf16[16,3584]{1,0:T(8,128)(2,1)S(1)}, u32[]{:S(2)}, u32[]{:S(2)}) collective-permute-start(bf16[16,3584]{1,0:T(8,128)(2,1)S(1)} %collective-permute-done.7.refs_10_), channel_id=1, source_target_pairs={{0,16},{16,0},{1,17},{17,1},{2,18},{18,2},{3,19},{19,3},{4,20},{20... | collective-permute-start | bytes 344072 | tf_op jit(solution)/shard_map/ppermute | solution.py:422
  25.6 10.0 %collective-permute-start.12 = (bf16[16,3584]{1,0:T(8,128)(2,1)S(1)}, bf16[16,3584]{1,0:T(8,128)(2,1)S(1)}, u32[]{:S(2)}, u32[]{:S(2)}) collective-permute-start(bf16[16,3584]{1,0:T(8,128)(2,1)S(1)} %get-tuple-element.64), channel_id=1, source_target_pairs={{0,10},{1,11},{2,8},{3,9},{4,14},{5,15},{6,12},{7,13},{8,2},{9,3},... | collective-permute-start | bytes 344072 | tf_op jit(solution)/shard_map/ppermute | solution.py:427
  31.6 7.9 %collective-permute-start.13 = (bf16[16,3584]{1,0:T(8,128)(2,1)S(1)}, bf16[16,3584]{1,0:T(8,128)(2,1)S(1)}, u32[]{:S(2)}, u32[]{:S(2)}) collective-permute-start(bf16[16,3584]{1,0:T(8,128)(2,1)S(1)} %collective-permute-done.5.refs_6_), channel_id=1, source_target_pairs={{0,16},{16,0},{1,17},{17,1},{2,18},{18,2},{3,19},{19,3},{4,20},{20... | collective-permute-start | bytes 344072 | tf_op jit(solution)/shard_map/ppermute | solution.py:422
  33.3 6.7 %collective-permute-start.17 = (bf16[16,3584]{1,0:T(8,128)(2,1)S(1)}, bf16[16,3584]{1,0:T(8,128)(2,1)S(1)}, u32[]{:S(2)}, u32[]{:S(2)}) collective-permute-start(bf16[16,3584]{1,0:T(8,128)(2,1)S(1)} %collective-permute-done.8.refs_8_), channel_id=1, source_target_pairs={{0,16},{16,0},{1,17},{17,1},{2,18},{18,2},{3,19},{19,3},{4,20},{20... | collective-permute-start | bytes 344072 | tf_op jit(solution)/shard_map/ppermute | solution.py:422
  33.6 7.2 %collective-permute-start.14 = (bf16[16,3584]{1,0:T(8,128)(2,1)S(1)}, bf16[16,3584]{1,0:T(8,128)(2,1)S(1)}, u32[]{:S(2)}, u32[]{:S(2)}) collective-permute-start(bf16[16,3584]{1,0:T(8,128)(2,1)S(1)} %collective-permute-done.6.refs_7_), channel_id=1, source_target_pairs={{0,16},{16,0},{1,17},{17,1},{2,18},{18,2},{3,19},{19,3},{4,20},{20... | collective-permute-start | bytes 344072 | tf_op jit(solution)/shard_map/ppermute | solution.py:422
  35.4 7.7 %collective-permute-start.16 = (bf16[16,3584]{1,0:T(8,128)(2,1)S(1)}, bf16[16,3584]{1,0:T(8,128)(2,1)S(1)}, u32[]{:S(2)}, u32[]{:S(2)}) collective-permute-start(bf16[16,3584]{1,0:T(8,128)(2,1)S(1)} %collective-permute-done.10.refs_11_), channel_id=1, source_target_pairs={{0,16},{16,0},{1,17},{17,1},{2,18},{18,2},{3,19},{19,3},{4,20},{20... | collective-permute-start | bytes 344072 | tf_op jit(solution)/shard_map/ppermute | solution.py:422
  35.6 7.4 %collective-permute-start.18 = (bf16[16,3584]{1,0:T(8,128)(2,1)S(1)}, bf16[16,3584]{1,0:T(8,128)(2,1)S(1)}, u32[]{:S(2)}, u32[]{:S(2)}) collective-permute-start(bf16[16,3584]{1,0:T(8,128)(2,1)S(1)} %collective-permute-done.12.refs_9_), channel_id=1, source_target_pairs={{0,16},{16,0},{1,17},{17,1},{2,18},{18,2},{3,19},{19,3},{4,20},{20... | collective-permute-start | bytes 344072 | tf_op jit(solution)/shard_map/ppermute | solution.py:422
  39.4 17.2 %collective-permute-start.20 = (bf16[2,720,128]{2,1,0:T(8,128)(2,1)S(1)}, bf16[2,720,128]{2,1,0:T(8,128)(2,1)S(1)}, u32[]{:S(2)}, u32[]{:S(2)}) collective-permute-start(bf16[2,720,128]{2,1,0:T(8,128)(2,1)S(1)} %get-tuple-element.78), channel_id=1, source_target_pairs={{0,2},{1,3},{2,0},{3,1},{4,6},{5,7},{6,4},{7,5},{8,10},{9,11},{10,... | collective-permute-start | bytes 1105928 | tf_op jit(solution)/shard_map/ppermute | solution.py:427
  40.0 16.6 %collective-permute-start.21 = (bf16[2,720,128]{2,1,0:T(8,128)(2,1)S(1)}, bf16[2,720,128]{2,1,0:T(8,128)(2,1)S(1)}, u32[]{:S(2)}, u32[]{:S(2)}) collective-permute-start(bf16[2,720,128]{2,1,0:T(8,128)(2,1)S(1)} %get-tuple-element.79), channel_id=1, source_target_pairs={{0,4},{1,5},{2,6},{3,7},{4,0},{5,1},{6,2},{7,3},{8,12},{9,13},{10,... | collective-permute-start | bytes 1105928 | tf_op jit(solution)/shard_map/ppermute | solution.py:427
  40.8 15.8 %collective-permute-start.22 = (bf16[2,720,128]{2,1,0:T(8,128)(2,1)S(1)}, bf16[2,720,128]{2,1,0:T(8,128)(2,1)S(1)}, u32[]{:S(2)}, u32[]{:S(2)}) collective-permute-start(bf16[2,720,128]{2,1,0:T(8,128)(2,1)S(1)} %get-tuple-element.80), channel_id=1, source_target_pairs={{0,6},{1,7},{2,4},{3,5},{4,2},{5,3},{6,0},{7,1},{8,14},{9,15},{10,... | collective-permute-start | bytes 1105928 | tf_op jit(solution)/shard_map/ppermute | solution.py:427
  44.9 11.7 %collective-permute-start.19 = (bf16[128,512]{1,0:T(8,128)(2,1)S(1)}, bf16[128,512]{1,0:T(8,128)(2,1)S(1)}, u32[]{:S(2)}, u32[]{:S(2)}) collective-permute-start(bf16[128,512]{1,0:T(8,128)(2,1)S(1)} %get-tuple-element.71), channel_id=1, source_target_pairs={{0,16},{16,0},{1,17},{17,1},{2,18},{18,2},{3,19},{19,3},{4,20},{20... | collective-permute-start | bytes 393224 | tf_op jit(solution)/shard_map/ppermute | solution.py:422
  59.1 6.0 %collective-permute-start.25 = (bf16[96,224]{1,0:T(8,128)(2,1)S(1)}, bf16[96,224]{1,0:T(8,128)(2,1)S(1)}, u32[]{:S(2)}, u32[]{:S(2)}) collective-permute-start(bf16[96,224]{1,0:T(8,128)(2,1)S(1)} %get-tuple-element.88), channel_id=1, source_target_pairs={{0,8},{1,9},{2,10},{3,11},{4,12},{5,13},{6,14},{7,15},{8,0},{9,1},... | collective-permute-start | bytes 129032 | tf_op jit(solution)/shard_map/ppermute | solution.py:432
  59.7 5.4 %collective-permute-start.24 = (bf16[96,224]{1,0:T(8,128)(2,1)S(1)}, bf16[96,224]{1,0:T(8,128)(2,1)S(1)}, u32[]{:S(2)}, u32[]{:S(2)}) collective-permute-start(bf16[96,224]{1,0:T(8,128)(2,1)S(1)} %get-tuple-element.87), channel_id=1, source_target_pairs={{0,16},{1,17},{2,18},{3,19},{4,20},{5,21},{6,22},{7,23},{8,24},{9,... | collective-permute-start | bytes 129032 | tf_op jit(solution)/shard_map/ppermute | solution.py:432
  60.9 6.0 %collective-permute-start.23 = (bf16[96,224]{1,0:T(8,128)(2,1)S(1)}, bf16[96,224]{1,0:T(8,128)(2,1)S(1)}, u32[]{:S(2)}, u32[]{:S(2)}) collective-permute-start(bf16[96,224]{1,0:T(8,128)(2,1)S(1)} %get-tuple-element.86), channel_id=1, source_target_pairs={{0,24},{1,25},{2,26},{3,27},{4,28},{5,29},{6,30},{7,31},{8,16},{9,... | collective-permute-start | bytes 129032 | tf_op jit(solution)/shard_map/ppermute | solution.py:432
